TPU v7x, 32 devices: a whole 2x2x4 slice. The times are simulated.
32 devices in a mesh: dev: 32 (over z, y, x, core).
Axes of the slice: x: 2, y: 2, z: 4, core: 2. Of those that a mesh axis runs over, the one named last changes fastest.
Arguments:
- tokens: bfloat16 [12288, 1024], P('dev'), may hold values from -6 to 6
- cotangent: bfloat16 [12288, 1024], P('dev'), may hold values from -6 to 6
- image_lengths: int32 [12], replicated, may hold values from 1 to 1370, 12288 in all
- ln1_gain: bfloat16 [1024], P('dev'), may hold values from 0.5 to 1.5
- ln1_bias: bfloat16 [1024], P('dev'), may hold values from -1.75 to 1.75
- qkv_weight: bfloat16 [1024, 3072], P('dev'), may hold values from -0.1875 to 0.1875
- qv_bias: bfloat16 [2048], P('dev'), may hold values from -1.75 to 1.75
- proj_weight: bfloat16 [1024, 1024], P('dev'), may hold values from -1 to 1
- proj_bias: bfloat16 [1024], P('dev'), may hold values from -1.75 to 1.75
- scale_attn: bfloat16 [1024], P('dev'), may hold values from 0.5 to 2
- ln2_gain: bfloat16 [1024], P('dev'), may hold values from 0.5 to 1.5
- ln2_bias: bfloat16 [1024], P('dev'), may hold values from -1.75 to 1.75
- fc1_weight: bfloat16 [1024, 4096], P('dev'), may hold values from -0.1875 to 0.1875
- fc1_bias: bfloat16 [4096], P('dev'), may hold values from -1.75 to 1.75
- fc2_weight: bfloat16 [4096, 1024], P('dev'), may hold values from -0.09375 to 0.09375
- fc2_bias: bfloat16 [1024], P('dev'), may hold values from -1.75 to 1.75
- scale_mlp: bfloat16 [1024], P('dev'), may hold values from 0.5 to 2
Outputs:
- block_out: bfloat16 [12288, 1024], P('dev')
- grad_tokens: bfloat16 [12288, 1024], P('dev')
- grad_ln1_gain: float32 [1024], P('dev')
- grad_ln1_bias: float32 [1024], P('dev')
- grad_qkv_weight: float32 [1024, 3072], P('dev')
- grad_qv_bias: float32 [2048], P('dev')
- grad_proj_weight: float32 [1024, 1024], P('dev')
- grad_proj_bias: float32 [1024], P('dev')
- grad_scale_attn: float32 [1024], P('dev')
- grad_ln2_gain: float32 [1024], P('dev')
- grad_ln2_bias: float32 [1024], P('dev')
- grad_fc1_weight: float32 [1024, 4096], P('dev')
- grad_fc1_bias: float32 [4096], P('dev')
- grad_fc2_weight: float32 [4096, 1024], P('dev')
- grad_fc2_bias: float32 [1024], P('dev')
- grad_scale_mlp: float32 [1024], P('dev')
Inputs may be any that keep to these rules, and one draw needn't show every extreme that they name: `image_lengths`: they sum to 12288; the longest image has exactly 1370 tokens.
All inputs are finite; a program needn't handle non-finite values.
Results may differ from a plain program's by a relative error of at most 0.011.
Values may be sent and summed in bfloat16 or wider, within the bound.
No kernel may reach another device: no remote copies, remote signals or barrier semaphores. Data moves between devices by JAX's collectives and lax.ppermute only.
A program may use at most 192 MiB of HBM per device.

v0:
```python
import functools

import jax
import jax.numpy as jnp
from jax import lax
from jax.experimental import pallas as pl
from jax.experimental.pallas import tpu as pltpu
from jax.sharding import PartitionSpec as P

BQ = 256
BK = 256
SLAB = 2 * BK
HD = 64
LOG2E = 1.4426950408889634
SCALE = 0.125
MASKED = -1e30
NT = (((1,), (1,)), ((), ()))


def head_halves(block):
    first = lax.broadcasted_iota(jnp.int32, block.shape, 1) < HD
    zero = jnp.zeros_like(block)
    return jnp.where(first, block, zero), jnp.where(first, zero, block)


def transpose_into(target, source, column):
    width = target.shape[0]
    for j in range(source.shape[0] // BK):
        part = source[j * BK : (j + 1) * BK, column : column + width].astype(jnp.float32)
        target[:, j * BK : (j + 1) * BK] = part.T.astype(target.dtype)


def slabs(low, high, first, last):
    low = jnp.clip(low, first, last) - first
    count = (jnp.clip(high, first, last) - first - low + 1) // 2
    return jnp.minimum(low, last - first - 2 * count), count


def slab_rows(start, t):
    return pl.ds(pl.multiple_of((start + 2 * t) * BK, BK), SLAB)


def forward_over(span, kv_ref, v_t, offset, q_heads, seg, carry):
    start, count = span
    width = q_heads[0].shape[1]
    begin, end = seg[0:1, :], seg[1:2, :]
    place = lax.broadcasted_iota(jnp.int32, (SLAB, BQ), 0) + offset

    def one_slab(t, carry):
        rows = slab_rows(start, t)
        keys = kv_ref[rows, :width]
        at = place + (start + 2 * t) * BK
        valid = (at >= begin) & (at < end)
        out = []
        for h in range(2):
            top, total, acc = carry[h]
            s = lax.dot_general(keys, q_heads[h], NT, preferred_element_type=jnp.float32)
            s = jnp.where(valid, s * (SCALE * LOG2E), MASKED)
            new_top = jnp.maximum(top, jnp.max(s, axis=0, keepdims=True))
            p = jnp.exp2(s - new_top)
            fade = jnp.exp2(top - new_top)
            total = total * fade + jnp.sum(p, axis=0, keepdims=True)
            v_part = v_t[h * HD : (h + 1) * HD, rows]
            acc = acc * fade + jnp.dot(v_part, p.astype(jnp.bfloat16), preferred_element_type=jnp.float32)
            out.append((new_top, total, acc))
        return tuple(out)

    return lax.fori_loop(0, count, one_slab, carry)


def forward_mid_kernel(low, high, seg, q_ref, kv_ref, acc_ref, stat_ref, v_t, *, edge):
    step = pl.program_id(0)

    @pl.when(step == 0)
    def _():
        transpose_into(v_t, kv_ref, q_ref.shape[1])

    start = (
        jnp.full((1, BQ), MASKED, jnp.float32),
        jnp.zeros((1, BQ), jnp.float32),
        jnp.zeros((HD, BQ), jnp.float32),
    )
    blocks = kv_ref.shape[0] // BK
    span = slabs(low[step], high[step], edge, edge + blocks)
    done = forward_over(span, kv_ref, v_t, edge * BK, head_halves(q_ref[...]), seg, (start, start))
    for h, (top, total, acc) in enumerate(done):
        stat_ref[2 * h : 2 * h + 1, :] = top
        stat_ref[2 * h + 1 : 2 * h + 2, :] = total
        acc_ref[h * HD : (h + 1) * HD, :] = acc


def forward_edge_kernel(
    low, high, seg, q_ref, left_ref, right_ref, acc_ref, stat_ref, o_ref, lse_ref, left_t, right_t, *, last
):
    step = pl.program_id(0)
    width = q_ref.shape[1]
    edge = left_ref.shape[0] // BK

    @pl.when(step == 0)
    def _():
        transpose_into(left_t, left_ref, width)
        transpose_into(right_t, right_ref, width)

    carry = tuple(
        (stat_ref[2 * h : 2 * h + 1, :], stat_ref[2 * h + 1 : 2 * h + 2, :], acc_ref[h * HD : (h + 1) * HD, :])
        for h in range(2)
    )
    q_heads = head_halves(q_ref[...])
    span = slabs(low[step], high[step], 0, edge)
    carry = forward_over(span, left_ref, left_t, 0, q_heads, seg, carry)
    span = slabs(low[step], high[step], last, last + edge)
    carry = forward_over(span, right_ref, right_t, last * BK, q_heads, seg, carry)
    o_ref[...] = jnp.concatenate([acc / total for _, total, acc in carry], axis=0).T.astype(o_ref.dtype)
    for h, (top, total, _) in enumerate(carry):
        lse_ref[h : h + 1, :] = top + jnp.log2(total)


def backward_setup(q_ref, do_ref, o_ref, lse_ref, heads):
    prod = (do_ref[...].astype(jnp.float32) * o_ref[...].astype(jnp.float32)).T
    q_heads, do_heads = head_halves(q_ref[...]), head_halves(do_ref[...])
    return [
        (
            h,
            q_heads[h],
            do_heads[h],
            jnp.sum(prod[h * HD : (h + 1) * HD], axis=0, keepdims=True),
            lse_ref[h : h + 1, :],
        )
        for h in heads
    ]


def backward_over(span, kv_ref, k_t, dkv, dq_t, offset, heads, seg):
    start, count = span
    width = dq_t.shape[0]
    begin, end = seg[0:1, :], seg[1:2, :]
    place = lax.broadcasted_iota(jnp.int32, (SLAB, BQ), 0) + offset
    q_all = jnp.concatenate([q for _, q, _, _, _ in heads], axis=0)
    do_all = jnp.concatenate([d for _, _, d, _, _ in heads], axis=0)

    @pl.loop(0, count)
    def _(t):
        rows = slab_rows(start, t)
        keys, values = kv_ref[rows, :width], kv_ref[rows, width:]
        at = place + (start + 2 * t) * BK
        valid = (at >= begin) & (at < end)
        ps, dss = [], []
        for h, q, do, centre, lse in heads:
            s = lax.dot_general(keys, q, NT, preferred_element_type=jnp.float32)
            p = jnp.where(valid, jnp.exp2(s * (SCALE * LOG2E) - lse), 0.0)
            dp = lax.dot_general(values, do, NT, preferred_element_type=jnp.float32)
            ds = (p * (dp - centre)).astype(jnp.bfloat16)
            ps.append(p.astype(jnp.bfloat16))
            dss.append(ds)
            part = slice(h * HD, (h + 1) * HD)
            dq_t[part, :] += jnp.dot(k_t[part, rows], ds, preferred_element_type=jnp.float32)
        dkv[rows, :width] += jnp.dot(jnp.concatenate(dss, axis=1), q_all, preferred_element_type=jnp.float32)
        dkv[rows, width:] += jnp.dot(jnp.concatenate(ps, axis=1), do_all, preferred_element_type=jnp.float32)


def backward_first_kernel(
    low, high, seg, q_ref, kv_ref, left_ref, right_ref, o_ref, do_ref, lse_ref, dq_t, mid_ref, edge_ref,
    left_t, right_t, k_t, dkv, *, last
):
    step = pl.program_id(0)
    width = q_ref.shape[1]
    edge = left_ref.shape[0] // BK

    @pl.when(step == 0)
    def _():
        transpose_into(left_t, left_ref, 0)
        transpose_into(right_t, right_ref, 0)
        transpose_into(k_t, kv_ref, 0)
        dkv[...] = jnp.zeros_like(dkv)
        mid_ref[...] = jnp.zeros_like(mid_ref)

    heads = backward_setup(q_ref, do_ref, o_ref, lse_ref, range(2))
    dq_t[...] = jnp.zeros_like(dq_t)
    span = slabs(low[step], high[step], 0, edge)
    backward_over(span, left_ref, left_t, dkv.at[0], dq_t, 0, heads, seg)
    span = slabs(low[step], high[step], last, last + edge)
    backward_over(span, right_ref, right_t, dkv.at[1], dq_t, last * BK, heads, seg)
    span = slabs(low[step], high[step], edge, last)
    backward_over(span, kv_ref, k_t, mid_ref, dq_t, edge * BK, heads[:1], seg)

    @pl.when(step == pl.num_programs(0) - 1)
    def _():
        mid_ref[:, :width] = mid_ref[:, :width] * SCALE
        for side in range(2):
            for j in range(edge):
                part = slice(j * BK, (j + 1) * BK)
                edge_ref[side, part, :width] = (dkv[side, part, :width] * SCALE).astype(edge_ref.dtype)
                edge_ref[side, part, width:] = dkv[side, part, width:].astype(edge_ref.dtype)


def backward_mid_kernel(
    low, high, seg, q_ref, kv_ref, o_ref, do_ref, lse_ref, part_ref, dq_ref, mid_ref, k_t, dq_t, *, edge
):
    step = pl.program_id(0)
    width = q_ref.shape[1]

    @pl.when(step == 0)
    def _():
        transpose_into(k_t, kv_ref, 0)
        mid_ref[...] = jnp.zeros_like(mid_ref)

    dq_t[...] = part_ref[...]
    blocks = kv_ref.shape[0] // BK
    span = slabs(low[step], high[step], edge, edge + blocks)
    heads = backward_setup(q_ref, do_ref, o_ref, lse_ref, [1])
    backward_over(span, kv_ref, k_t, mid_ref, dq_t, edge * BK, heads, seg)
    dq_ref[...] = (dq_t[...] * SCALE).T.astype(dq_ref.dtype)

    @pl.when(step == pl.num_programs(0) - 1)
    def _():
        mid_ref[:, :width] = mid_ref[:, :width] * SCALE


def whole_spec(array):
    return pl.BlockSpec(array.shape, lambda i, *_: (0,) * len(array.shape))


def attention_call(kernel, name, prefetch, inputs, in_kinds, outputs, out_kinds, scratch, work):
    span = prefetch[0].shape[0] * BQ

    def spec(array, kind):
        if kind == "r":
            return pl.BlockSpec((BQ, array.shape[1]), lambda i, *_: (i, 0))
        if kind == "c":
            return pl.BlockSpec((array.shape[0], BQ), lambda i, *_: (0, i))
        return whole_spec(array)

    return pl.pallas_call(
        kernel,
        out_shape=tuple(outputs),
        grid_spec=pltpu.PrefetchScalarGridSpec(
            num_scalar_prefetch=2,
            grid=(span // BQ,),
            in_specs=[spec(a, k) for a, k in zip(inputs, in_kinds)],
            out_specs=[spec(a, k) for a, k in zip(outputs, out_kinds)],
            scratch_shapes=scratch,
        ),
        compiler_params=pltpu.CompilerParams(vmem_limit_bytes=48 << 20),
        cost_estimate=pl.CostEstimate(flops=work << 30, bytes_accessed=8 << 20, transcendentals=span * 128),
        name=name,
    )(*prefetch, *inputs)


def shaped(*shape, dtype=jnp.float32):
    return jax.ShapeDtypeStruct(shape, dtype)


def forward_mid(prefetch, seg, q, kv, edge):
    span, width = q.shape
    return attention_call(
        functools.partial(forward_mid_kernel, edge=edge), "forward_mid", prefetch, [seg, q, kv], "crw",
        [shaped(width, span), shaped(8, span)], "cc", [pltpu.VMEM((width, span), jnp.bfloat16)], 3,
    )


def forward_edge(prefetch, seg, q, left, right, acc, stat):
    span, width = q.shape
    halo = pltpu.VMEM((width, left.shape[0]), jnp.bfloat16)
    return attention_call(
        functools.partial(forward_edge_kernel, last=(left.shape[0] + span) // BK), "forward_edge", prefetch,
        [seg, q, left, right, acc, stat], "crwwcc",
        [shaped(span, width, dtype=jnp.bfloat16), shaped(8, span)], "rc", [halo, halo], 3,
    )


def backward_first(prefetch, seg, q, kv, left, right, o, do, lse):
    span, width = q.shape
    halo = pltpu.VMEM((width, left.shape[0]), jnp.bfloat16)
    return attention_call(
        functools.partial(backward_first_kernel, last=(left.shape[0] + span) // BK), "backward_first", prefetch,
        [seg, q, kv, left, right, o, do, lse], "crwwwrrc",
        [shaped(width, span), shaped(*kv.shape), shaped(2, *left.shape, dtype=jnp.bfloat16)], "cww",
        [halo, halo, pltpu.VMEM((width, span), jnp.bfloat16), pltpu.VMEM((2, *left.shape), jnp.float32)], 3,
    )


def backward_second(prefetch, seg, q, kv, o, do, lse, part, edge):
    span, width = q.shape
    return attention_call(
        functools.partial(backward_mid_kernel, edge=edge), "backward_second", prefetch,
        [seg, q, kv, o, do, lse, part], "crwrrcc",
        [shaped(span, width, dtype=jnp.bfloat16), shaped(*kv.shape)], "rw",
        [pltpu.VMEM((width, span), jnp.bfloat16), pltpu.VMEM((width, BQ), jnp.float32)], 3,
    )


HEADS = 16
SEQ = 1370
GROUP = 8
EPS = 1e-06
F32, BF16 = jnp.float32, jnp.bfloat16


def mm(left, right):
    return jnp.dot(left, right, preferred_element_type=F32)


def mm_t(left, right):
    return jnp.einsum("tf,df->td", left, right, preferred_element_type=F32)


def t_mm(left, right):
    return jnp.einsum("td,tf->df", left, right, preferred_element_type=F32)


def normalised(value):
    centre = value - jnp.mean(value, axis=-1, keepdims=True)
    rstd = lax.rsqrt(jnp.mean(centre * centre, axis=-1, keepdims=True) + EPS)
    return centre * rstd, rstd


def norm_back(unit, rstd, grad):
    first = jnp.mean(grad, axis=-1, keepdims=True)
    second = jnp.mean(grad * unit, axis=-1, keepdims=True)
    return rstd * (grad - first - unit * second)


def gelu_parts(z):
    half = 0.5 * (1.0 + lax.erf(z * 0.7071067811865476))
    slope = half + z * (0.3989422804014327 * jnp.exp(-0.5 * z * z))
    return z * half, slope


def groups_of(count):
    return [list(range(first, first + GROUP)) for first in range(0, count, GROUP)]


def gathered(shard):
    return lax.all_gather(shard, "dev", axis=0, tiled=True)


def scattered(whole):
    return lax.psum_scatter(whole, "dev", scatter_dimension=0, tiled=True)


def pack(vectors, count):
    return jnp.concatenate([v.reshape(count, -1) for v in vectors], axis=1)


def unpack(packed, sizes):
    out, at = [], 0
    for size in sizes:
        out.append(packed[:, at : at + size].reshape(-1))
        at += size
    return out


def to_heads(parts, devices):
    rows = parts[0].shape[0]
    sent = jnp.stack([p.reshape(rows, GROUP, -1) for p in parts], axis=2)
    sent = sent.transpose(1, 0, 2, 3)
    back = lax.all_to_all(sent, "dev", 0, 0, axis_index_groups=groups_of(devices), tiled=True)
    return [back[:, :, i].reshape(GROUP * rows, -1) for i in range(len(parts))]


def to_tokens(parts, devices):
    rows = parts[0].shape[0] // GROUP
    sent = jnp.stack([p.reshape(GROUP, rows, -1) for p in parts], axis=2)
    back = lax.all_to_all(sent, "dev", 0, 0, axis_index_groups=groups_of(devices), tiled=True)
    return [back[:, :, i].transpose(1, 0, 2).reshape(rows, -1) for i in range(len(parts))]


def shifted(shard, by, devices):
    pairs = [(i, i + by) for i in range(devices) if 0 <= i + by < devices]
    return lax.ppermute(shard, "dev", pairs)


def take(stack, index, axis):
    return lax.dynamic_index_in_dim(stack, index, axis, keepdims=False)


def swapped(value, bit, devices):
    return lax.ppermute(value, "dev", [(i, i ^ bit) for i in range(devices)])


def in_plane(stack, devices):
    return lax.all_to_all(stack, "dev", 0, 0, axis_index_groups=groups_of(devices), tiled=True)


def position(me):
    return (me // 4) % 2, (me // 2) % 2, me % 2


def qkv_kernel(bits, near_a, far_a, near_b, far_b, slab, n1_ref, q_ref, kv_ref, lines, bias, *, rows):
    step = pl.program_id(0)
    third = q_ref.shape[1]
    width = slab.shape[0]

    @pl.when(step == 0)
    def _():
        lines[...] = slab[:, 3 * third :].astype(F32).T
        group = bits[3]
        unit = lax.broadcasted_iota(jnp.int32, (width, third), 0)
        place = lax.broadcasted_iota(jnp.int32, (width, third), 1)
        some = lines[0:16, :].astype(BF16)
        bias[...] = jnp.zeros_like(bias)
        for part, first in ((0, 0), (2, width // 2)):
            total = jnp.zeros((1, third), F32)
            for column in range(2):
                at = first + group * (third // 2) + (place // (2 * rows)) * rows + place % rows
                chosen = (unit == at) & ((place // rows) % 2 == column)
                total = total + mm(some, jnp.where(chosen, 1.0, 0.0).astype(BF16))[2 + column : 3 + column]
            bias[0:1, part * third : (part + 1) * third] = total

    far = step >= 4
    left = jnp.where(far, far_a[0, 0], near_a[0, 0])
    right = jnp.where(far, far_b[0, 0], near_b[0, 0])
    unit, _ = normalised(jnp.concatenate([left, right], axis=1).astype(F32))
    n1 = (unit * lines[0:1, :] + lines[1:2, :]).astype(BF16)
    n1_ref[...] = n1
    out = (mm(n1, slab[:, : 3 * third]) + bias[0:1, :]).astype(BF16)
    q_ref[...] = out[:, :third]
    kv_ref[...] = out[:, third:]


def plane_qkv(tokens, slab, me, devices):
    rows, width = tokens.shape
    half, third = width // 2, (slab.shape[1] - 128) // 3
    a, b = tokens[:, :half], tokens[:, half:]
    a = jnp.stack([a, swapped(a, 4, devices)])
    b = jnp.stack([b, swapped(b, 2, devices)])
    a = jnp.stack([a, swapped(a, 2, devices)])
    b = jnp.stack([b, swapped(b, 4, devices)])
    far_a, far_b = swapped(a, 1, devices), swapped(b, 1, devices)

    def near_at(s, swap):
        i, j = (s // 2) % 2, s % 2
        i, j = jnp.where(s < 4, i, 1), jnp.where(s < 4, j, 1)
        return (j, i, 0, 0) if swap else (i, j, 0, 0)

    def far_at(s, swap):
        i, j = (s // 2) % 2, s % 2
        i, j = jnp.where(s < 4, 0, i), jnp.where(s < 4, 0, j)
        return (j, i, 0, 0) if swap else (i, j, 0, 0)

    def place(s, bits):
        return ((bits[0] ^ (s % 2)) * 4 + (bits[1] ^ ((s // 2) % 2)) * 2 + (bits[2] ^ (s // 4)), 0)

    piece = (1, 1, rows, half)
    span = GROUP * rows
    return pl.pallas_call(
        functools.partial(qkv_kernel, rows=width // devices),
        out_shape=(
            jax.ShapeDtypeStruct((span, width), BF16),
            jax.ShapeDtypeStruct((span, third), BF16),
            jax.ShapeDtypeStruct((span, 2 * third), BF16),
        ),
        grid_spec=pltpu.PrefetchScalarGridSpec(
            num_scalar_prefetch=1,
            grid=(GROUP,),
            in_specs=[
                pl.BlockSpec(piece, lambda s, bits: near_at(s, False)),
                pl.BlockSpec(piece, lambda s, bits: far_at(s, False)),
                pl.BlockSpec(piece, lambda s, bits: near_at(s, True)),
                pl.BlockSpec(piece, lambda s, bits: far_at(s, True)),
                pl.BlockSpec(slab.shape, lambda s, bits: (0, 0)),
            ],
            out_specs=[pl.BlockSpec((rows, columns), place) for columns in (width, third, 2 * third)],
            scratch_shapes=[pltpu.VMEM((128, width), F32), pltpu.VMEM((8, 3 * third), F32)],
        ),
        compiler_params=pltpu.CompilerParams(vmem_limit_bytes=40 << 20),
        cost_estimate=pl.CostEstimate(flops=5 << 30, bytes_accessed=16 << 20, transcendentals=0),
        name="plane_qkv",
    )(
        jnp.stack([*position(me), me % GROUP]).astype(jnp.int32), a, far_a, b, far_b, slab,
    )


def from_planes(stack, me, devices):
    planes, mine = devices // GROUP, me // GROUP
    got = []
    for k in range(1, planes):
        piece = take(stack, (mine + k) % planes, 0)
        got.append(lax.ppermute(piece, "dev", [(i, (i + k * GROUP) % devices) for i in range(devices)]))
    return take(stack, mine, 0), got


def total_of(own, others):
    total = own.astype(F32)
    for other in others:
        total = total + other.astype(F32)
    return total


def pack_columns(vectors, rows):
    columns = jnp.concatenate([v.reshape(-1, rows).T for v in vectors], axis=1)
    return jnp.pad(columns, ((0, 0), (0, 128 - columns.shape[1])))


def unpack_columns(packed, sizes, rows):
    lines, out, at = packed[:, :16].T, [], 0
    for size in sizes:
        count = size // rows
        part = lines[at : at + count].reshape(count, -1, rows)
        out.append(part.transpose(1, 0, 2).reshape(-1))
        at += count
    return out


def by_parity(transposed, parity, rows):
    blocks = transposed.reshape(-1, 2, rows, transposed.shape[1])
    even, odd = (blocks[:, s].reshape(-1, transposed.shape[1]) for s in range(2))
    return jnp.where(parity == 0, even, odd), jnp.where(parity == 0, odd, even)


def turned(value):
    return value.astype(F32).T.astype(BF16)


def mlp_kernel(
    bits, n2_ref, dml_ref, f1_ref, f2_ref, bias, mlp_ref, dn2_ref, db_ref, keep1, send1, keep2, send2, n2_t
):
    step = pl.program_id(0)
    rows = keep1.shape[1]

    @pl.when(step == 0)
    def _():
        mlp_ref[...] = jnp.zeros_like(mlp_ref)
        dn2_ref[...] = jnp.zeros_like(dn2_ref)
        n2_t[0], n2_t[1] = by_parity(turned(n2_ref[...]), bits[2], rows)

    n2, dml, f1, f2 = n2_ref[...], dml_ref[...], f1_ref[...], f2_ref[...]
    act, slope = gelu_parts(mm(n2, f1) + bias[...])
    act = act.astype(BF16)
    mlp_ref[...] += mm(act, f2)
    dz = lax.dot_general(dml, f2, NT, preferred_element_type=F32) * slope
    db_ref[...] = jnp.sum(dz, axis=0, keepdims=True)
    dz = dz.astype(BF16)
    dn2_ref[...] += lax.dot_general(dz, f1, NT, preferred_element_type=F32)
    for side, out in enumerate((keep1, send1)):
        out[...] = mm(n2_t[side], dz).astype(BF16).reshape(out.shape)
    for part, out in zip(by_parity(turned(act), bits[2], rows), (keep2, send2)):
        out[...] = mm(part, dml).astype(BF16).reshape(out.shape)


def mlp_all(n2, dml, big, bias, me, shard_rows):
    tokens, width = n2.shape
    hidden, owners = bias.shape[0], width // shard_rows
    size = width // 2
    steps = hidden // size
    whole = pl.BlockSpec((tokens, width), lambda s, bits: (0, 0))
    first = pl.BlockSpec((owners // 2, shard_rows, size), lambda s, bits: (0, 0, s))
    second = pl.BlockSpec((owners // 4, shard_rows, width), lambda s, bits: (s % 2, 0, s // 2))
    line = pl.BlockSpec((1, size), lambda s, bits: (0, s))
    grads = jax.ShapeDtypeStruct((owners // 2, shard_rows, hidden), BF16)
    total = jax.ShapeDtypeStruct((tokens, width), F32)
    blocks = hidden // width
    return pl.pallas_call(
        mlp_kernel,
        out_shape=(total, total, jax.ShapeDtypeStruct((1, hidden), F32), grads, grads, grads, grads),
        grid_spec=pltpu.PrefetchScalarGridSpec(
            num_scalar_prefetch=1,
            grid=(steps,),
            in_specs=[
                whole,
                whole,
                pl.BlockSpec((width, size), lambda s, bits: (0, s)),
                pl.BlockSpec((size, width), lambda s, bits: (s % 2, blocks + s // 2)),
                line,
            ],
            out_specs=[whole, whole, line, first, first, second, second],
            scratch_shapes=[pltpu.VMEM((2, width // 2, tokens), BF16)],
        ),
        compiler_params=pltpu.CompilerParams(vmem_limit_bytes=52 << 20),
        cost_estimate=pl.CostEstimate(
            flops=4 * tokens * width * hidden, bytes_accessed=8 * width * hidden, transcendentals=2 * tokens * hidden
        ),
        name="mlp_all",
    )(jnp.stack(position(me)).astype(jnp.int32), n2, dml, big, big, bias[None])


def grad_kernel(bits, a_ref, b_ref, keep_ref, send_ref):
    for part, out in zip(by_parity(turned(a_ref[...]), bits[2], keep_ref.shape[1]), (keep_ref, send_ref)):
        out[...] = mm(part, b_ref[...]).astype(BF16).reshape(out.shape)


def weight_grad(a, b, rows, me):
    out = jax.ShapeDtypeStruct((a.shape[1] // (2 * rows), rows, b.shape[1]), BF16)
    return pl.pallas_call(
        grad_kernel,
        out_shape=(out, out),
        grid_spec=pltpu.PrefetchScalarGridSpec(num_scalar_prefetch=1, grid=(1,)),
        compiler_params=pltpu.CompilerParams(vmem_limit_bytes=40 << 20),
        cost_estimate=pl.CostEstimate(
            flops=2 * a.size * b.shape[1], bytes_accessed=2 * (a.size + b.size + 2 * out.size), transcendentals=0
        ),
        name="weight_grad",
    )(jnp.stack(position(me)).astype(jnp.int32), a, b)


def after_mlp_kernel(
    bits, mlp, dn2, x_ref, branch, g_ref, o_ref, w_proj, vec, block_out, dy1_ref, sums, do_ref, keep, send
):
    layer_attn, gain2, layer_mlp, bias = (vec[i : i + 1, :] for i in range(4))
    g, out = g_ref[...].astype(F32), mlp[...] + bias
    y1 = x_ref[...].astype(F32) + layer_attn * branch[...]
    unit, rstd = normalised(y1)
    block_out[...] = (y1 + layer_mlp * out).astype(BF16)
    dy1 = g + norm_back(unit, rstd, dn2[...] * gain2)
    dy1_ref[...] = dy1
    db = layer_attn * dy1
    totals = (g * out, layer_mlp * g, dn2[...] * unit, dn2[...], dy1 * branch[...], db)
    for i, total in enumerate(totals):
        sums[i : i + 1, :] = jnp.sum(total, axis=0, keepdims=True)
    dbl = db.astype(BF16)
    do = lax.dot_general(dbl, w_proj[...], NT, preferred_element_type=F32).astype(BF16)
    columns = do_ref.shape[2]
    for j in range(do_ref.shape[0]):
        do_ref[j] = do[:, j * columns : (j + 1) * columns]
    for part, to in zip(by_parity(turned(o_ref[...]), bits[2], keep.shape[1]), (keep, send)):
        to[...] = mm(part, dbl).astype(BF16).reshape(to.shape)


def after_mlp(mlp, dn2, x, branch, g, o, big, vec, me, shard_rows):
    tokens, width = mlp.shape
    owners = width // shard_rows
    grads = shaped(owners // 2, shard_rows, width, dtype=BF16)
    outs = (
        shaped(tokens, width, dtype=BF16), shaped(tokens, width), shaped(8, width),
        shaped(GROUP, tokens, width // GROUP, dtype=BF16), grads, grads,
    )
    last = big.shape[1] // width - 1
    return pl.pallas_call(
        after_mlp_kernel,
        out_shape=outs,
        grid_spec=pltpu.PrefetchScalarGridSpec(
            num_scalar_prefetch=1,
            grid=(1,),
            in_specs=[whole_spec(a) for a in (mlp, dn2, x, branch, g, o)]
            + [pl.BlockSpec((width, width), lambda i, *_: (0, last)), whole_spec(vec)],
            out_specs=[whole_spec(a) for a in outs],
        ),
        compiler_params=pltpu.CompilerParams(vmem_limit_bytes=52 << 20),
        cost_estimate=pl.CostEstimate(flops=4 * tokens * width * width, bytes_accessed=20 << 20, transcendentals=0),
        name="after_mlp",
    )(jnp.stack(position(me)).astype(jnp.int32), mlp, dn2, x, branch, g, o, big, vec)


def add_kernel(bits, *refs, terms):
    outs = refs[terms * 2 * (len(refs) // (2 * terms + 1)) :]
    refs = refs[: terms * 2 * len(outs)]
    for n, out in enumerate(outs):
        wide, narrow = (
            [r[...].astype(F32).reshape(r.shape[-2:]) for r in refs[(2 * n + i) * terms : (2 * n + i + 1) * terms]]
            for i in range(2)
        )
        out[...] = jnp.concatenate([sum(wide), sum(narrow)], axis=1).astype(BF16).reshape(out.shape)


def added(operands, indices, grid, out_shape, out_index, me, name):
    flat, specs = [], []
    for sides, places in zip(operands, indices):
        for arrays, at in zip(sides, places):
            for (array, block), index in zip(arrays, at):
                flat.append(array)
                specs.append(pl.BlockSpec(block, index))
    terms = len(operands[0][0])
    outs = [shaped(*out_shape, dtype=BF16)] * len(operands)
    block = (1,) * (len(out_shape) - 2) + out_shape[-2:]
    return pl.pallas_call(
        functools.partial(add_kernel, terms=terms),
        out_shape=tuple(outs),
        grid_spec=pltpu.PrefetchScalarGridSpec(
            num_scalar_prefetch=1,
            grid=grid,
            in_specs=specs,
            out_specs=[pl.BlockSpec(block, out_index)] * len(outs),
        ),
        compiler_params=pltpu.CompilerParams(vmem_limit_bytes=40 << 20),
        cost_estimate=pl.CostEstimate(flops=0, bytes_accessed=16 << 20, transcendentals=0),
        name=name,
    )(jnp.stack(position(me)).astype(jnp.int32), *flat)


def first_sends(pairs, me):
    (one, two, small) = pairs
    planes, _, _, rows, width = one[0].shape
    cut = small[0].shape[-1] // 2
    wide, narrow = (1, 1, 1, rows, width), (1, 1, 1, rows, cut)

    def at_a(column):
        return lambda z, t, bits: (z, t, 1 - bits[1], 0, column)

    def at_b(column):
        return lambda z, t, bits: (z, 1 - bits[0], t, 0, column)

    operands = [
        ([(m, wide) for m in one], [(m, narrow) for m in small]),
        ([(m, wide) for m in two], [(m, narrow) for m in small]),
    ]
    indices = [([at_a(0)] * 2, [at_a(0)] * 2), ([at_b(0)] * 2, [at_b(1)] * 2)]
    shape = (planes, 2, rows, width + cut)
    return added(operands, indices, (planes, 2), shape, lambda z, t, bits: (z, t, 0, 0), me, "first_sends")


def second_sums(pairs, in_a, in_b, me):
    (one, two, small) = pairs
    planes, _, _, rows, width = one[0].shape
    cut = small[0].shape[-1] // 2
    wide, narrow = (1, 1, 1, rows, width), (1, 1, 1, rows, cut)
    wide_in, narrow_in = (1, 1, rows, width), (1, 1, rows, cut)
    operands, indices = [], []
    for sides, got, axis in ((one, in_a, 0), (two, in_b, 1)):
        for keep in (0, 1):
            def other(bits, axis=axis, keep=keep):
                return bits[axis] if keep else 1 - bits[axis]

            def at(column, axis=axis, other=other):
                if axis == 0:
                    return lambda z, bits: (z, other(bits), bits[1], 0, column)
                return lambda z, bits: (z, bits[0], other(bits), 0, column)

            def arrived(column, other=other):
                return lambda z, bits: (z, other(bits), 0, column)

            operands.append(
                ([(m, wide) for m in sides] + [(got, wide_in)], [(m, narrow) for m in small] + [(got, narrow_in)])
            )
            indices.append(
                ([at(0)] * 2 + [arrived(0)], [at(axis)] * 2 + [arrived(width // cut)])
            )
    shape = (planes, rows, width + cut)
    return added(operands, indices, (planes,), shape, lambda z, bits: (z, 0, 0), me, "second_sums")


def body(
    tokens,
    cotangent,
    image_lengths,
    ln1_gain,
    ln1_bias,
    qkv_weight,
    qv_bias,
    proj_weight,
    proj_bias,
    scale_attn,
    ln2_gain,
    ln2_bias,
    fc1_weight,
    fc1_bias,
    fc2_weight,
    fc2_bias,
    scale_mlp,
):
    devices = lax.axis_size("dev")
    me = lax.axis_index("dev")
    rows, width = tokens.shape
    vectors = (
        ln1_gain, ln1_bias, qv_bias, proj_bias, scale_attn, ln2_gain, ln2_bias, fc1_bias, fc2_bias, scale_mlp,
    )
    sizes = [v.shape[0] for v in vectors]
    shard_rows, hidden = qkv_weight.shape[0], fc1_weight.shape[1]
    by_axes = shard_rows % 32 == 0
    blocks = hidden // width
    slab = qkv_weight.reshape(shard_rows, 3, GROUP, -1).transpose(2, 0, 1, 3).reshape(GROUP, shard_rows, -1)
    packed = jnp.broadcast_to(pack_columns(vectors, shard_rows), (GROUP, shard_rows, 128))
    slab = jnp.concatenate([slab, packed], axis=2)
    slab = jnp.broadcast_to(slab[None], (devices // GROUP, *slab.shape)).reshape(devices, shard_rows, -1)
    slab = lax.all_to_all(slab, "dev", 0, 0, tiled=True).reshape(width, -1)
    packed = slab[:, -128:]
    spread = unpack_columns(packed.astype(F32), sizes, shard_rows)
    gain1, shift1, bias_qv, bias_proj, layer_attn, gain2, shift2, bias_fc1, bias_fc2, layer_mlp = spread
    if by_axes:
        first = fc1_weight.reshape(shard_rows, devices, blocks, shard_rows).transpose(0, 2, 1, 3)
        second = fc2_weight.reshape(blocks, shard_rows, width).transpose(1, 0, 2)
        big = jnp.concatenate(
            [first.reshape(shard_rows, hidden), second.reshape(shard_rows, hidden), proj_weight], axis=1
        )
        big = gathered(big)
        w_proj = big[:, 2 * hidden :]
    else:
        w_proj, big = gathered(proj_weight), gathered(fc1_weight)
        w_fc2 = gathered(fc2_weight)
    qkv_late = qkv_weight.reshape(shard_rows, 3, GROUP, -1).transpose(0, 2, 1, 3).reshape(shard_rows, -1)
    qkv_late, packed = lax.optimization_barrier((qkv_late, packed))
    w_qkv = gathered(qkv_late)

    span = GROUP * rows
    halo = -(-(SEQ - 1) // BK) * BK
    base = (me // GROUP) * span - halo
    places = base + halo + jnp.arange(span, dtype=jnp.int32)
    ends = jnp.cumsum(image_lengths)
    before = ends[None, :] <= places[:, None]
    begin = jnp.max(jnp.where(before, ends[None, :], 0), axis=1)
    finish = jnp.min(jnp.where(before, devices * rows, ends[None, :]), axis=1)
    seg = jnp.stack([begin - base, finish - base]).astype(jnp.int32)
    low = seg[0, ::BQ] // BK
    high = -(-seg[1, BQ - 1 :: BQ] // BK)

    x = tokens.astype(F32)
    u1, rstd1 = normalised(x)
    n1, q, kv = plane_qkv(tokens, slab, me, devices)
    prefetch, edge_blocks = (low, high), halo // BK
    left = shifted(kv[span - halo :], GROUP, devices)
    right = shifted(kv[:halo], -GROUP, devices)
    acc, stat = forward_mid(prefetch, seg, q, kv, edge_blocks)
    acc, stat, left, right = lax.optimization_barrier((acc, stat, left, right))
    o_heads, lse = forward_edge(prefetch, seg, q, left, right, acc, stat)
    (o,) = to_tokens([o_heads], devices)

    branch = mm(o, w_proj) + bias_proj
    y1 = x + layer_attn * branch
    u2, rstd2 = normalised(y1)
    n2 = (u2 * gain2 + shift2).astype(BF16)
    g = cotangent.astype(F32)
    dm = layer_mlp * g
    d_fc2_bias = jnp.sum(dm, axis=0)
    dml = dm.astype(BF16)
    if by_axes:
        bias_hidden = bias_fc1.reshape(devices, blocks, shard_rows).transpose(1, 0, 2).reshape(-1)
        mlp, dn2, d_fc1_bias, keep1, send1, keep2, send2 = mlp_all(n2, dml, big, bias_hidden, me, shard_rows)
        d_fc1_bias = d_fc1_bias.reshape(blocks, devices, shard_rows).transpose(1, 0, 2).reshape(-1)
    else:
        act, slope = gelu_parts(mm(n2, big) + bias_fc1)
        act = act.astype(BF16)
        mlp = mm(act, w_fc2)
        dz = mm_t(dml, w_fc2) * slope
        d_fc1_bias = jnp.sum(dz, axis=0)
        dz = dz.astype(BF16)
        dn2 = mm_t(dz, big)
        d_fc1, d_fc2 = scattered(t_mm(n2, dz)), scattered(t_mm(act, dml))
    if by_axes:
        vec = jnp.stack([layer_attn, gain2, layer_mlp, bias_fc2])
        block_out, dy1, totals, do, keep3, send3 = after_mlp(
            mlp, dn2, tokens, branch, cotangent, o, big, vec, me, shard_rows
        )
        d_scale_mlp, d_fc2_bias, d_gain2, d_shift2, d_scale_attn, d_proj_bias = (totals[i] for i in range(6))
        got1, got2, got3 = (swapped(s, 1, devices) for s in (send1, send2, send3))
        do, got1, got2, got3 = lax.optimization_barrier((do, got1, got2, got3))
        view = (devices // GROUP, 2, 2, shard_rows)
        halves = [
            tuple(s.reshape(*view, -1) for s in pair) for pair in ((keep1, got1), (keep2, got2), (keep3, got3))
        ]
        out_a, out_b = first_sends(halves, me)
    else:
        mlp = mlp + bias_fc2
        block_out = (y1 + layer_mlp * mlp).astype(BF16)
        d_scale_mlp = jnp.sum(g * mlp, axis=0)
        d_gain2 = jnp.sum(dn2 * u2, axis=0)
        d_shift2 = jnp.sum(dn2, axis=0)
        dy1 = g + norm_back(u2, rstd2, dn2 * gain2)
        d_scale_attn = jnp.sum(dy1 * branch, axis=0)
        db = layer_attn * dy1
        d_proj_bias = jnp.sum(db, axis=0)
        dbl = db.astype(BF16)
        d_proj = scattered(t_mm(o, dbl))
        do = mm_t(dbl, w_proj).astype(BF16).reshape(rows, GROUP, -1).transpose(1, 0, 2)

    do_heads = in_plane(do, devices).reshape(span, -1)
    if by_axes:
        do_heads, out_a, out_b = lax.optimization_barrier((do_heads, out_a, out_b))
        in_a, in_b = swapped(out_a, 2, devices), swapped(out_b, 4, devices)
    part_dq, mid0, edge = backward_first(prefetch, seg, q, kv, left, right, o_heads, do_heads, lse)
    if by_axes:
        part_dq, in_a, in_b, w_qkv = lax.optimization_barrier((part_dq, in_a, in_b, w_qkv))
        out_a, sum_a, out_b, sum_b = second_sums(halves, in_a, in_b, me)
        part_dq, out_a, out_b = lax.optimization_barrier((part_dq, out_a, out_b))
        in_a, in_b = swapped(out_a, 4, devices), swapped(out_b, 2, devices)
    from_right = shifted(edge[0], -GROUP, devices)
    from_left = shifted(edge[1], GROUP, devices)
    dq, mid1 = backward_second(prefetch, seg, q, kv, o_heads, do_heads, lse, part_dq, edge_blocks)
    dq, mid1, from_left, from_right = lax.optimization_barrier((dq, mid1, from_left, from_right))
    if by_axes:
        dq, in_a, in_b = lax.optimization_barrier((dq, in_a, in_b))
    rest = span - halo
    mid = mid0 + mid1 + jnp.pad(from_left.astype(F32), ((0, rest), (0, 0)))
    mid = mid + jnp.pad(from_right.astype(F32), ((rest, 0), (0, 0)))
    mid = mid.astype(BF16)
    d_heads = jnp.concatenate([dq, mid], axis=1)
    if by_axes:
        third = [(s.astype(F32) + i.astype(F32)).astype(BF16) for s, i in ((sum_a, in_a), (sum_b, in_b))]
        d_heads, third = lax.optimization_barrier((d_heads, jnp.concatenate(third, axis=-1)))
        own_sums, sums = from_planes(third, me, devices)
    dqkv = in_plane(d_heads.reshape(GROUP, rows, -1), devices)
    if by_axes:
        dqkv, n1, sums[:2] = lax.optimization_barrier((dqkv, n1, sums[:2]))
    d_qkv = t_mm(n1, d_heads).astype(BF16).reshape(devices // GROUP, GROUP, shard_rows, -1)
    dqkv, d_qkv = lax.optimization_barrier((dqkv, d_qkv))
    own_qkv, got_qkv = from_planes(d_qkv, me, devices)
    per_head = jnp.sum(dqkv.astype(F32), axis=1)
    half = width // GROUP
    d_qv_bias = jnp.concatenate([per_head[:, :half].reshape(-1), per_head[:, 2 * half :].reshape(-1)])
    dn1 = mm_t(dqkv.transpose(1, 0, 2).reshape(rows, 3 * width), w_qkv)
    if by_axes:
        dn1, sums[2:], got_qkv = lax.optimization_barrier((dn1, sums[2:], got_qkv))
    d_qkv = in_plane(total_of(own_qkv, got_qkv), devices).reshape(GROUP, shard_rows, 3, -1)
    d_qkv = d_qkv.transpose(1, 2, 0, 3).reshape(shard_rows, 3 * width)
    if by_axes:
        sums = total_of(own_sums, sums)
        d_fc1 = sums[:, :hidden].reshape(shard_rows, blocks, devices, shard_rows).transpose(0, 2, 1, 3)
        d_fc1 = d_fc1.reshape(shard_rows, hidden)
        cut = width // 2
        at = hidden + cut
        d_fc2 = sums[:, at : at + hidden].reshape(shard_rows, blocks, width).transpose(1, 0, 2)
        d_fc2 = d_fc2.reshape(blocks * shard_rows, width)
        d_proj = jnp.concatenate([sums[:, hidden:at], sums[:, at + hidden :]], axis=1)
    d_gain1 = jnp.sum(dn1 * u1, axis=0)
    d_shift1 = jnp.sum(dn1, axis=0)
    grad_tokens = (dy1 + norm_back(u1, rstd1, dn1 * gain1)).astype(BF16)

    small = (
        d_gain1, d_shift1, d_qv_bias, d_proj_bias, d_scale_attn, d_gain2, d_shift2, d_fc1_bias, d_fc2_bias, d_scale_mlp,
    )
    small = lax.all_to_all(pack(small, devices), "dev", 0, 0, tiled=True)
    small = jnp.sum(small, axis=0, keepdims=True)
    s_gain1, s_shift1, s_qv, s_proj, s_attn, s_gain2, s_shift2, s_fc1, s_fc2, s_mlp = unpack(small, sizes)
    return (
        block_out,
        grad_tokens,
        s_gain1,
        s_shift1,
        d_qkv,
        s_qv,
        d_proj,
        s_proj,
        s_attn,
        s_gain2,
        s_shift2,
        d_fc1,
        s_fc1,
        d_fc2,
        s_fc2,
        s_mlp,
    )


def solution(mesh):
    matrix, vector = P("dev", None), P("dev")
    return jax.shard_map(
        body,
        mesh=mesh,
        in_specs=(
            matrix, matrix, P(), vector, vector, matrix, vector, matrix, vector, vector, vector, vector, matrix,
            vector, matrix, vector, vector,
        ),
        out_specs=(
            matrix, matrix, vector, vector, matrix, vector, matrix, vector, vector, vector, vector, matrix, vector,
            matrix, vector, vector,
        ),
        check_vma=False,
    )
```

profile of v0, /device:TPU:0, one launch (start us, length us, event | category | flops | bytes accessed | tf_op | source)
XLA Modules:
  0.0 485.5 jit_solution(9043969278316028757)
XLA Ops:
  11.7 3.0 collective-permute-start.3
  16.2 7.6 %collective-permute-done.3 = bf16[384,512]{1,0:T(8,128)(2,1)S(1)} collective-permute-done((bf16[384,512]{1,0:T(8,128)(2,1)S(1)}, bf16[384,512]{1,0:T(8,128)(2,1)S(1)}, u32[]{:S(2)}, u32[]{:S(2)}) %collective-permute-start.3) | collective-permute-done | bytes 393248 | tf_op jit(solution)/shard_map/ppermute | solution.py:378
  31.7 4.6 all-to-all-start
  36.4 18.9 %collective-permute-done.4 = bf16[2,384,512]{2,1,0:T(8,128)(2,1)} collective-permute-done((bf16[2,384,512]{2,1,0:T(8,128)(2,1)}, bf16[2,384,512]{2,1,0:T(8,128)(2,1)}, u32[]{:S(2)}, u32[]{:S(2)}) %collective-permute-start.4) | collective-permute-done | bytes 786464 | tf_op jit(solution)/shard_map/ppermute | solution.py:378
  55.3 2.4 pad_maximum_fusion.3.near_b
  57.7 2.5 pad_maximum_fusion.2.near_a
  62.2 18.7 %all-to-all-done = bf16[32,32,512]{2,1,0:T(8,128)(2,1)S(1)} async-done(((bf16[32,32,512]{2,1,0:T(8,128)(2,1)}), bf16[32,32,512]{2,1,0:T(8,128)(2,1)S(1)}, u32[]{:S(2)}, u32[]{:S(2)}) %all-to-all-start) | async-done | bytes 1048608 | tf_op jit(solution)/shard_map/all_to_all | solution.py:764
  81.0 11.4 %plane_qkv.1 = (bf16[3072,1024]{1,0:T(8,128)(2,1)}, bf16[3072,128]{1,0:T(8,128)(2,1)S(1)}, bf16[3072,256]{1,0:T(8,128)(2,1)S(1)}) custom-call(s32[4]{0:T(128)S(1)} %pad_add_fusion.2.bits, bf16[2,2,384,512]{3,2,1,0:T(8,128)(2,1)} %pad_maximum_fusion.2.near_a, bf16[2,2,384,512]{3,2,1,0:T(8,128)(2,1)} %collective-permute-done.2.far_a, ...), custom_call_target="tpu_custom_call" | custom-call | flops 5368709120 | bytes 16777216 | tf_op jit(solution)/shard_map/plane_qkv/pallas_call | solution.py:446
  94.5 1.9 collective-permute-start.6
  100.7 37.5 %forward_mid.1 = (f32[128,3072]{1,0:T(8,128)S(1)}, f32[8,3072]{1,0:T(8,128)S(1)}) custom-call(s32[12]{0:T(128)S(1)} %get-tuple-element.210.low, s32[12]{0:T(128)S(1)} %get-tuple-element.211.high, s32[2,3072]{1,0:T(2,128)S(1)} %pad_add_fusion.seg, bf16[3072,128]{1,0:T(8,128)(2,1)S(1)} %copy-done.13, bf16[3072,256]{1,0:T(8,128)(2,1)S(1)} %copy-done.4), custom_call_target="tpu_custom_call" | custom-call | flops 3221225472 | bytes 8388608 | tf_op jit(solution)/shard_map/forward_mid/pallas_call | solution.py:233
  138.3 14.5 %collective-permute-done.7.right_ref = bf16[1536,256]{1,0:T(8,128)(2,1)} collective-permute-done((bf16[1536,256]{1,0:T(8,128)(2,1)}, bf16[1536,256]{1,0:T(8,128)(2,1)}, u32[]{:S(2)}, u32[]{:S(2)}) %collective-permute-start.7) | collective-permute-done | bytes 786464 | tf_op jit(solution)/shard_map/ppermute | solution.py:370
  152.8 9.7 %forward_edge.1 = (bf16[3072,128]{1,0:T(8,128)(2,1)}, f32[8,3072]{1,0:T(8,128)S(1)}) custom-call(s32[12]{0:T(128)S(1)} %get-tuple-element.210.low, s32[12]{0:T(128)S(1)} %get-tuple-element.211.high, s32[2,3072]{1,0:T(2,128)S(1)} %pad_add_fusion.seg, bf16[3072,128]{1,0:T(8,128)(2,1)S(1)} %copy-done.14, bf16[1536,256]{1,0:T(8,128)(2,1)S(1)} %collective-permute-done.6.left_ref, ...), custom_call_target="tpu_custom_call" | custom-call | flops 3221225472 | bytes 8388608 | tf_op jit(solution)/shard_map/forward_edge/pallas_call | solution.py:233
  162.5 4.5 all-to-all-start.1
  167.3 12.3 %all-to-all-done.1 = bf16[8,384,1,128]{3,1,2,0:T(8,128)(2,1)} async-done(((bf16[8,384,1,128]{3,1,2,0:T(8,128)(2,1)}), bf16[8,384,1,128]{3,1,2,0:T(8,128)(2,1)}, u32[]{:S(2)}, u32[]{:S(2)}) %all-to-all-start.1) | async-done | bytes 786464 | tf_op jit(solution)/shard_map/all_to_all | solution.py:364
  179.6 3.0 convert_reduce_fusion.1
  184.4 29.7 %mlp_all.1 = (f32[384,1024]{1,0:T(8,128)}, f32[384,1024]{1,0:T(8,128)}, f32[1,4096]{1,0:T(1,128)S(1)}, bf16[16,32,4096]{2,1,0:T(8,128)(2,1)}, bf16[16,32,4096]{2...) custom-call(s32[3]{0:T(128)S(1)} %pad_add_fusion.1.bits, ...), custom_call_target="tpu_custom_call" | custom-call | flops 6442450944 | bytes 33554432 | tf_op jit(solution)/shard_map/mlp_all/pallas_call | solution.py:553
  214.6 2.4 copy_bitcast_fusion.1.o_ref
  217.0 8.8 %after_mlp.1 = (bf16[384,1024]{1,0:T(8,128)(2,1)}, f32[384,1024]{1,0:T(8,128)}, f32[8,1024]{1,0:T(8,128)S(1)}, bf16[8,384,128]{2,1,0:T(8,128)(2,1)S(1)}, bf16[16...) custom-call(s32[3]{0:T(128)S(1)} %pad_add_fusion.1.bits, f32[384,1024]{1,0:T(8,128)} %get-tuple-element.94.mlp, ...), custom_call_target="tpu_custom_call" | custom-call | flops 1610612736 | bytes 20971520 | tf_op jit(solution)/shard_map/after_mlp/pallas_call | solution.py:628
  226.7 4.8 collective-permute-done.10
  231.5 4.4 all-to-all-start.2
  236.0 2.3 copy-done.1
  238.3 6.1 %first_sends.1 = (bf16[4,2,32,4608]{3,2,1,0:T(8,128)(2,1)S(1)}, bf16[4,2,32,4608]{3,2,1,0:T(8,128)(2,1)S(1)}) custom-call(s32[3]{0:T(128)S(1)} %pad_add_fusion.1.bits, bf16[4,2,2,32,4096]{4,3,2,1,0:T(8,128)(2,1)S(1)} %bitcast.186, bf16[4,2,2,32,4096]{4,3,2,1,0:T(8,128)(2,1)} %bitcast.46.refs_1_.refs_7_, bf16[4,2,2,32,1024]{4,3,2,1,0:T(8,128)(2,1)S(1)} %bitcast.172, ...), custom_call_target="tpu_custom_call" | custom-call | bytes 16777216 | tf_op jit(solution)/shard_map/first_sends/pallas_call | solution.py:665
  253.1 33.8 %backward_first.1 = (f32[128,3072]{1,0:T(8,128)S(1)}, f32[3072,256]{1,0:T(8,128)}, bf16[2,1536,256]{2,1,0:T(8,128)(2,1)}) custom-call(s32[12]{0:T(128)S(1)} %get-tuple-element.210.low, s32[12]{0:T(128)S(1)} %get-tuple-element.211.high, s32[2,3072]{1,0:T(2,128)S(1)} %pad_add_fusion.seg, bf16[3072,128]{1,0:T(8,128)(2,1)S(1)} %copy-done.15, ...), custom_call_target="tpu_custom_call" | custom-call | flops 3221225472 | bytes 8388608 | tf_op jit(solution)/shard_map/backward_first/pallas_call | solution.py:233
  286.9 3.2 slice_bitcast_fusion
  290.1 9.8 %collective-permute-start.13 = (bf16[1536,256]{1,0:T(8,128)(2,1)}, bf16[1536,256]{1,0:T(8,128)(2,1)}, u32[]{:S(2)}, u32[]{:S(2)}) collective-permute-start(bf16[1536,256]{1,0:T(8,128)(2,1)} %get-tuple-element.174), channel_id=1, source_target_pairs={{0,8},{1,9},{2,10},{3,11},{4,12},{5,13},{6,14},{7,15},{8,16},{9,17... | collective-permute-start | bytes 2359304 | tf_op jit(solution)/shard_map/ppermute | solution.py:370
  302.6 6.9 %second_sums.1 = (bf16[4,32,4608]{2,1,0:T(8,128)(2,1)S(1)}, bf16[4,32,4608]{2,1,0:T(8,128)(2,1)S(1)}, bf16[4,32,4608]{2,1,0:T(8,128)(2,1)S(1)}, bf16[4,32,4608]{2,1,0:T(8,128)(2,1)S(1)}) custom-call(s32[3]{0:T(128)S(1)} %pad_add_fusion.1.bits, bf16[4,2,2,32,4096]{4,3,2,1,0:T(8,128)(2,1)} %bitcast.184, bf16[4,2,2,32,4096]{4,3,2,1,0:T(8,128)(2,1)} %bitcast.46.refs_1_.refs_7_, ...), custom_call_target="tpu_custom_call" | custom-call | bytes 16777216 | tf_op jit(solution)/shard_map/second_sums/pallas_call | solution.py:665
  311.7 29.7 %backward_second.1 = (bf16[3072,128]{1,0:T(8,128)(2,1)S(1)}, f32[3072,256]{1,0:T(8,128)}) custom-call(s32[12]{0:T(128)S(1)} %get-tuple-element.210.low, s32[12]{0:T(128)S(1)} %get-tuple-element.211.high, s32[2,3072]{1,0:T(2,128)S(1)} %pad_add_fusion.seg, bf16[3072,128]{1,0:T(8,128)(2,1)S(1)} %copy-done.16, bf16[3072,256]{1,0:T(8,128)(2,1)S(1)} %copy-done.5, ...), custom_call_target="tpu_custom_call" | custom-call | flops 3221225472 | bytes 8388608 | tf_op jit(solution)/shard_map/backward_second/pallas_call | solution.py:233
  341.4 2.9 add_convert_fusion
  348.2 4.3 copy.85
  352.5 4.4 all-to-all-start.3
  358.5 2.6 collective-permute-start.17
  361.1 4.7 collective-permute-start.18
  372.5 7.0 %collective-permute-done.17 = bf16[32,9216]{1,0:T(8,128)(2,1)S(1)} collective-permute-done((bf16[32,9216]{1,0:T(8,128)(2,1)S(1)}, bf16[32,9216]{1,0:T(8,128)(2,1)S(1)}, u32[]{:S(2)}, u32[]{:S(2)}) %collective-permute-start.17) | collective-permute-done | bytes 589856 | tf_op jit(solution)/shard_map/ppermute | solution.py:479
  379.5 25.0 %collective-permute-done.18 = bf16[32,9216]{1,0:T(8,128)(2,1)} collective-permute-done((bf16[32,9216]{1,0:T(8,128)(2,1)S(1)}, bf16[32,9216]{1,0:T(8,128)(2,1)}, u32[]{:S(2)}, u32[]{:S(2)}) %collective-permute-start.18) | collective-permute-done | bytes 589856 | tf_op jit(solution)/shard_map/ppermute | solution.py:479
  404.5 6.9 %convolution_convert_fusion = bf16[1024,384]{1,0:T(8,128)(2,1)S(1)} fusion(bf16[3072,1024]{1,0:T(8,128)(2,1)} %get-tuple-element.141, bf16[3072,384]{1,0:T(8,128)(2,1)} %pad_maximum_fusion), kind=kOutput, calls=%fused_computation.29 | convolution fusion | flops 2416312320 | bytes 9437184 | tf_op jit(solution)/shard_map/td,tf->df/dot_general | solution.py:308
  412.4 7.9 %collective-permute-start.20 = (bf16[8,32,384]{2,1,0:T(8,128)(2,1)S(1)}, bf16[8,32,384]{2,1,0:T(8,128)(2,1)S(1)}, u32[]{:S(2)}, u32[]{:S(2)}) collective-permute-start(bf16[8,32,384]{2,1,0:T(8,128)(2,1)S(1)} %get-tuple-element.183), channel_id=1, source_target_pairs={{0,8},{1,9},{2,10},{3,11},{4,12},{5,13},{6,14},{7,15},{8,16},{9,17... | collective-permute-start | bytes 589832 | tf_op jit(solution)/shard_map/ppermute | solution.py:479
  420.3 3.5 collective-permute-start.21
  424.1 7.4 %fusion.33 = f32[384,1024]{1,0:T(8,128)} fusion(bf16[384,3072]{0,1:T(8,128)(2,1)} %bitcast.59, bf16[1024,3072]{1,0:T(8,128)(2,1)} %all-gather.5.cloned.1.call-done), kind=kOutput, calls=%fused_computation.114 | convolution fusion | flops 2415919104 | bytes 10223616 | tf_op jit(solution)/shard_map/tf,df->td/dot_general | solution.py:304
  431.5 2.1 convert_reduce_fusion
  434.4 2.2 collective-permute-done.21
  436.7 1.8 fusion.18
  440.1 3.1 copy.89
  443.2 4.5 reshape.285
  451.0 6.8 %all-to-all-start.4 = ((f32[32,1,448]{2,1,0:T(1,128)}), f32[32,1,448]{2,1,0:T(1,128)S(1)}, u32[]{:S(2)}, u32[]{:S(2)}) async-start(f32[32,1,448]{2,1,0:T(1,128)} %copy.87), calls=%async_computation.4 | async-start | bytes 131072 | tf_op jit(solution)/shard_map/all_to_all | solution.py:909
  459.6 2.9 fusion.11
  463.2 2.1 all-to-all-done.4
  465.2 3.5 all-to-all-start.5
  470.4 6.5 %all-to-all-done.5 = f32[8,32,384]{2,1,0:T(8,128)S(1)} async-done(((f32[8,32,384]{2,1,0:T(8,128)}), f32[8,32,384]{2,1,0:T(8,128)S(1)}, u32[]{:S(2)}, u32[]{:S(2)}) %all-to-all-start.5) | async-done | bytes 393248 | tf_op jit(solution)/shard_map/all_to_all | solution.py:382
  (241 shorter events, 63.1 us)
Async XLA Ops:
  7.2 172.5 %all-gather.3.cloned.1.call-start = ((), (), s32[]{:S(2)}) async-start(), calls=%async_computation.6 | async-start | bytes 19464192 | tf_op jit(solution)/shard_map/all_gather | solution.py:334
  11.7 12.1 %collective-permute-start.3 = (bf16[384,512]{1,0:T(8,128)(2,1)S(1)}, bf16[384,512]{1,0:T(8,128)(2,1)S(1)}, u32[]{:S(2)}, u32[]{:S(2)}) collective-permute-start(bf16[384,512]{1,0:T(8,128)(2,1)S(1)} %get-tuple-element.189), channel_id=1, source_target_pairs={{0,2},{1,3},{2,0},{3,1},{4,6},{5,7},{6,4},{7,5},{8,10},{9,11},{10,... | collective-permute-start | bytes 1179656 | tf_op jit(solution)/shard_map/ppermute | solution.py:378
  14.7 11.9 %collective-permute-start = (bf16[384,512]{1,0:T(8,128)(2,1)S(1)}, bf16[384,512]{1,0:T(8,128)(2,1)S(1)}, u32[]{:S(2)}, u32[]{:S(2)}) collective-permute-start(bf16[384,512]{1,0:T(8,128)(2,1)S(1)} %get-tuple-element.188), channel_id=1, source_target_pairs={{0,4},{1,5},{2,6},{3,7},{4,0},{5,1},{6,2},{7,3},{8,12},{9,13},{10,... | collective-permute-start | bytes 1179656 | tf_op jit(solution)/shard_map/ppermute | solution.py:378
  24.8 4.3 copy-start.26
  24.8 30.4 %collective-permute-start.4 = (bf16[2,384,512]{2,1,0:T(8,128)(2,1)}, bf16[2,384,512]{2,1,0:T(8,128)(2,1)}, u32[]{:S(2)}, u32[]{:S(2)}) collective-permute-start(bf16[2,384,512]{2,1,0:T(8,128)(2,1)} %get-tuple-element.185), channel_id=1, source_target_pairs={{0,4},{1,5},{2,6},{3,7},{4,0},{5,1},{6,2},{7,3},{8,12},{9,13},{10,... | collective-permute-start | bytes 2359304 | tf_op jit(solution)/shard_map/ppermute | solution.py:378
  26.6 3.7 copy-start.44
  26.6 3.7 copy-start.45
  27.7 30.0 %collective-permute-start.1 = (bf16[2,384,512]{2,1,0:T(8,128)(2,1)}, bf16[2,384,512]{2,1,0:T(8,128)(2,1)}, u32[]{:S(2)}, u32[]{:S(2)}) collective-permute-start(bf16[2,384,512]{2,1,0:T(8,128)(2,1)} %get-tuple-element.191), channel_id=1, source_target_pairs={{0,2},{1,3},{2,0},{3,1},{4,6},{5,7},{6,4},{7,5},{8,10},{9,11},{10,... | collective-permute-start | bytes 2359304 | tf_op jit(solution)/shard_map/ppermute | solution.py:378
  31.7 49.3 %all-to-all-start = ((bf16[32,32,512]{2,1,0:T(8,128)(2,1)}), bf16[32,32,512]{2,1,0:T(8,128)(2,1)S(1)}, u32[]{:S(2)}, u32[]{:S(2)}) async-start(bf16[32,32,512]{2,1,0:T(8,128)(2,1)} %bitcast.14), calls=%async_computation | async-start | bytes 2097152 | tf_op jit(solution)/shard_map/all_to_all | solution.py:764
  36.3 264.9 %all-gather.5.cloned.1.call-start = ((), (), s32[]{:S(2)}) async-start(), calls=%async_computation.7 | async-start | bytes 6488064 | tf_op jit(solution)/shard_map/all_gather | solution.py:334
  57.7 23.3 %collective-permute-start.5 = (bf16[2,2,384,512]{3,2,1,0:T(8,128)(2,1)}, bf16[2,2,384,512]{3,2,1,0:T(8,128)(2,1)}, u32[]{:S(2)}, u32[]{:S(2)}) collective-permute-start(bf16[2,2,384,512]{3,2,1,0:T(8,128)(2,1)} %pad_maximum_fusion.3.near_b), channel_id=1, source_target_pairs={{0,1},{1,0},{2,3},{3,2},{4,5},{5,4},{6,7},{7,6},{8,9},{9,8},{10,11... | collective-permute-start | bytes 4718600 | tf_op jit(solution)/shard_map/ppermute | solution.py:378
  57.7 4.0 copy-start.54
  60.2 20.8 %collective-permute-start.2 = (bf16[2,2,384,512]{3,2,1,0:T(8,128)(2,1)}, bf16[2,2,384,512]{3,2,1,0:T(8,128)(2,1)}, u32[]{:S(2)}, u32[]{:S(2)}) collective-permute-start(bf16[2,2,384,512]{3,2,1,0:T(8,128)(2,1)} %pad_maximum_fusion.2.near_a), channel_id=1, source_target_pairs={{0,1},{1,0},{2,3},{3,2},{4,5},{5,4},{6,7},{7,6},{8,9},{9,8},{10,11... | collective-permute-start | bytes 4718600 | tf_op jit(solution)/shard_map/ppermute | solution.py:378
  94.5 43.8 %collective-permute-start.6 = (bf16[1536,256]{1,0:T(8,128)(2,1)}, bf16[1536,256]{1,0:T(8,128)(2,1)S(1)}, u32[]{:S(2)}, u32[]{:S(2)}) collective-permute-start(bf16[1536,256]{1,0:T(8,128)(2,1)} %get-tuple-element.176), channel_id=1, source_target_pairs={{0,8},{1,9},{2,10},{3,11},{4,12},{5,13},{6,14},{7,15},{8,16},{9,17... | collective-permute-start | bytes 2359304 | tf_op jit(solution)/shard_map/ppermute | solution.py:370
  96.4 56.4 %collective-permute-start.7 = (bf16[1536,256]{1,0:T(8,128)(2,1)}, bf16[1536,256]{1,0:T(8,128)(2,1)}, u32[]{:S(2)}, u32[]{:S(2)}) collective-permute-start(bf16[1536,256]{1,0:T(8,128)(2,1)} %get-tuple-element.175), channel_id=1, source_target_pairs={{8,0},{9,1},{10,2},{11,3},{12,4},{13,5},{14,6},{15,7},{16,8},{17,9... | collective-permute-start | bytes 2359304 | tf_op jit(solution)/shard_map/ppermute | solution.py:370
  100.7 52.1 %copy-start.14 = (bf16[3072,128]{1,0:T(8,128)(2,1)S(1)}, bf16[3072,128]{1,0:T(8,128)(2,1)}, u32[]{:S(2)}) copy-start(bf16[3072,128]{1,0:T(8,128)(2,1)} %copy-done.12) | copy-start | bytes 2359300
  138.3 24.2 %copy-start.9 = (bf16[1536,256]{1,0:T(8,128)(2,1)}, bf16[1536,256]{1,0:T(8,128)(2,1)S(1)}, u32[]{:S(2)}) copy-start(bf16[1536,256]{1,0:T(8,128)(2,1)S(1)} %collective-permute-done.6.left_ref) | copy-start | bytes 2359300
  162.5 4.6 copy-start.19
  162.5 17.1 %all-to-all-start.1 = ((bf16[8,384,1,128]{3,1,2,0:T(8,128)(2,1)}), bf16[8,384,1,128]{3,1,2,0:T(8,128)(2,1)}, u32[]{:S(2)}, u32[]{:S(2)}) async-start(bf16[8,384,1,128]{3,1,2,0:T(8,128)(2,1)} %bitcast.34), calls=%async_computation.1 | async-start | bytes 1572864 | tf_op jit(solution)/shard_map/all_to_all | solution.py:364
  214.1 17.4 %collective-permute-start.8 = (bf16[16,32,4096]{2,1,0:T(8,128)(2,1)}, bf16[16,32,4096]{2,1,0:T(8,128)(2,1)}, u32[]{:S(2)}, u32[]{:S(2)}) collective-permute-start(bf16[16,32,4096]{2,1,0:T(8,128)(2,1)} %get-tuple-element.99), channel_id=1, source_target_pairs={{0,1},{1,0},{2,3},{3,2},{4,5},{5,4},{6,7},{7,6},{8,9},{9,8},{10,11... | collective-permute-start | bytes 12582920 | tf_op jit(solution)/shard_map/ppermute | solution.py:378
  214.1 17.4 %collective-permute-start.9 = (bf16[16,32,4096]{2,1,0:T(8,128)(2,1)}, bf16[16,32,4096]{2,1,0:T(8,128)(2,1)}, u32[]{:S(2)}, u32[]{:S(2)}) collective-permute-start(bf16[16,32,4096]{2,1,0:T(8,128)(2,1)} %get-tuple-element.100), channel_id=1, source_target_pairs={{0,1},{1,0},{2,3},{3,2},{4,5},{5,4},{6,7},{7,6},{8,9},{9,8},{10,11... | collective-permute-start | bytes 12582920 | tf_op jit(solution)/shard_map/ppermute | solution.py:378
  226.6 9.3 %copy-start = (bf16[16,32,1024]{2,1,0:T(8,128)(2,1)S(1)}, bf16[16,32,1024]{2,1,0:T(8,128)(2,1)}, u32[]{:S(2)}) copy-start(bf16[16,32,1024]{2,1,0:T(8,128)(2,1)} %get-tuple-element.105) | copy-start | bytes 3145732
  226.6 4.9 %collective-permute-start.10 = (bf16[16,32,1024]{2,1,0:T(8,128)(2,1)}, bf16[16,32,1024]{2,1,0:T(8,128)(2,1)S(1)}, u32[]{:S(2)}, u32[]{:S(2)}) collective-permute-start(bf16[16,32,1024]{2,1,0:T(8,128)(2,1)} %get-tuple-element.101), channel_id=1, source_target_pairs={{0,1},{1,0},{2,3},{3,2},{4,5},{5,4},{6,7},{7,6},{8,9},{9,8},{10,11... | collective-permute-start | bytes 3145736 | tf_op jit(solution)/shard_map/ppermute | solution.py:378
  231.5 17.1 %all-to-all-start.2 = ((bf16[8,384,128]{2,1,0:T(8,128)(2,1)}), bf16[8,384,128]{2,1,0:T(8,128)(2,1)}, u32[]{:S(2)}, u32[]{:S(2)}) async-start(bf16[8,384,128]{2,1,0:T(8,128)(2,1)} %copy-done.6), calls=%async_computation.2 | async-start | bytes 1572864 | tf_op jit(solution)/shard_map/all_to_all | solution.py:382
  248.6 52.7 %collective-permute-start.11 = (bf16[4,2,32,4608]{3,2,1,0:T(8,128)(2,1)}, bf16[4,2,32,4608]{3,2,1,0:T(8,128)(2,1)}, u32[]{:S(2)}, u32[]{:S(2)}) collective-permute-start(bf16[4,2,32,4608]{3,2,1,0:T(8,128)(2,1)} %copy-done.8), channel_id=1, source_target_pairs={{0,2},{1,3},{2,0},{3,1},{4,6},{5,7},{6,4},{7,5},{8,10},{9,11},{10,... | collective-permute-start | bytes 7077896 | tf_op jit(solution)/shard_map/ppermute | solution.py:378
  249.3 53.3 %collective-permute-start.12 = (bf16[4,2,32,4608]{3,2,1,0:T(8,128)(2,1)}, bf16[4,2,32,4608]{3,2,1,0:T(8,128)(2,1)}, u32[]{:S(2)}, u32[]{:S(2)}) collective-permute-start(bf16[4,2,32,4608]{3,2,1,0:T(8,128)(2,1)} %copy-done.7), channel_id=1, source_target_pairs={{0,4},{1,5},{2,6},{3,7},{4,0},{5,1},{6,2},{7,3},{8,12},{9,13},{10,... | collective-permute-start | bytes 7077896 | tf_op jit(solution)/shard_map/ppermute | solution.py:378
  290.1 51.3 %collective-permute-start.13 = (bf16[1536,256]{1,0:T(8,128)(2,1)}, bf16[1536,256]{1,0:T(8,128)(2,1)}, u32[]{:S(2)}, u32[]{:S(2)}) collective-permute-start(bf16[1536,256]{1,0:T(8,128)(2,1)} %get-tuple-element.174), channel_id=1, source_target_pairs={{0,8},{1,9},{2,10},{3,11},{4,12},{5,13},{6,14},{7,15},{8,16},{9,17... | collective-permute-start | bytes 2359304 | tf_op jit(solution)/shard_map/ppermute | solution.py:370
  299.9 41.5 %collective-permute-start.14 = (bf16[1536,256]{1,0:T(8,128)(2,1)}, bf16[1536,256]{1,0:T(8,128)(2,1)}, u32[]{:S(2)}, u32[]{:S(2)}) collective-permute-start(bf16[1536,256]{1,0:T(8,128)(2,1)} %get-tuple-element.173), channel_id=1, source_target_pairs={{8,0},{9,1},{10,2},{11,3},{12,4},{13,5},{14,6},{15,7},{16,8},{17,9... | collective-permute-start | bytes 2359304 | tf_op jit(solution)/shard_map/ppermute | solution.py:370
  302.6 9.0 %copy-start.5 = (bf16[3072,256]{1,0:T(8,128)(2,1)S(1)}, bf16[3072,256]{1,0:T(8,128)(2,1)}, u32[]{:S(2)}) copy-start(bf16[3072,256]{1,0:T(8,128)(2,1)} %copy-done.3) | copy-start | bytes 4718596
  302.6 9.0 %copy-start.16 = (bf16[3072,128]{1,0:T(8,128)(2,1)S(1)}, bf16[3072,128]{1,0:T(8,128)(2,1)}, u32[]{:S(2)}) copy-start(bf16[3072,128]{1,0:T(8,128)(2,1)} %copy-done.12) | copy-start | bytes 2359300
  309.5 34.8 %collective-permute-start.15 = (bf16[4,32,4608]{2,1,0:T(8,128)(2,1)S(1)}, bf16[4,32,4608]{2,1,0:T(8,128)(2,1)S(1)}, u32[]{:S(2)}, u32[]{:S(2)}) collective-permute-start(bf16[4,32,4608]{2,1,0:T(8,128)(2,1)S(1)} %get-tuple-element.126), channel_id=1, source_target_pairs={{0,4},{1,5},{2,6},{3,7},{4,0},{5,1},{6,2},{7,3},{8,12},{9,13},{10,... | collective-permute-start | bytes 3538952 | tf_op jit(solution)/shard_map/ppermute | solution.py:378
  311.0 33.3 %collective-permute-start.16 = (bf16[4,32,4608]{2,1,0:T(8,128)(2,1)S(1)}, bf16[4,32,4608]{2,1,0:T(8,128)(2,1)S(1)}, u32[]{:S(2)}, u32[]{:S(2)}) collective-permute-start(bf16[4,32,4608]{2,1,0:T(8,128)(2,1)S(1)} %get-tuple-element.127), channel_id=1, source_target_pairs={{0,2},{1,3},{2,0},{3,1},{4,6},{5,7},{6,4},{7,5},{8,10},{9,11},{10,... | collective-permute-start | bytes 3538952 | tf_op jit(solution)/shard_map/ppermute | solution.py:378
  311.7 29.8 %copy-start.20 = (f32[3072,256]{1,0:T(8,128)S(1)}, f32[3072,256]{1,0:T(8,128)}, u32[]{:S(2)}) copy-start(f32[3072,256]{1,0:T(8,128)} %get-tuple-element.129) | copy-start | bytes 9437188
  352.5 52.1 %all-to-all-start.3 = ((bf16[8,384,384]{1,2,0:T(8,128)(2,1)}), bf16[8,384,384]{1,2,0:T(8,128)(2,1)}, u32[]{:S(2)}, u32[]{:S(2)}) async-start(bf16[8,384,384]{1,2,0:T(8,128)(2,1)} %copy.85), calls=%async_computation.3 | async-start | bytes 4718592 | tf_op jit(solution)/shard_map/all_to_all | solution.py:382
  356.9 15.0 %copy-start.43 = (f32[384]{0:T(512)S(1)}, f32[384]{0:T(512)}, u32[]{:S(2)}) copy-start(f32[384]{0:T(512)} %get-tuple-element.158) | copy-start | bytes 4612
  358.5 21.0 %collective-permute-start.17 = (bf16[32,9216]{1,0:T(8,128)(2,1)S(1)}, bf16[32,9216]{1,0:T(8,128)(2,1)S(1)}, u32[]{:S(2)}, u32[]{:S(2)}) collective-permute-start(bf16[32,9216]{1,0:T(8,128)(2,1)S(1)} %get-tuple-element.172), channel_id=1, source_target_pairs={{0,8},{1,9},{2,10},{3,11},{4,12},{5,13},{6,14},{7,15},{8,16},{9,17... | collective-permute-start | bytes 1769480 | tf_op jit(solution)/shard_map/ppermute | solution.py:479
  361.1 43.4 %collective-permute-start.18 = (bf16[32,9216]{1,0:T(8,128)(2,1)S(1)}, bf16[32,9216]{1,0:T(8,128)(2,1)}, u32[]{:S(2)}, u32[]{:S(2)}) collective-permute-start(bf16[32,9216]{1,0:T(8,128)(2,1)S(1)} %get-tuple-element.171), channel_id=1, source_target_pairs={{0,16},{1,17},{2,18},{3,19},{4,20},{5,21},{6,22},{7,23},{8,24},{9,... | collective-permute-start | bytes 1769480 | tf_op jit(solution)/shard_map/ppermute | solution.py:479
  372.5 61.9 %collective-permute-start.19 = (bf16[32,9216]{1,0:T(8,128)(2,1)S(1)}, bf16[32,9216]{1,0:T(8,128)(2,1)}, u32[]{:S(2)}, u32[]{:S(2)}) collective-permute-start(bf16[32,9216]{1,0:T(8,128)(2,1)S(1)} %get-tuple-element.170), channel_id=1, source_target_pairs={{0,24},{1,25},{2,26},{3,27},{4,28},{5,29},{6,30},{7,31},{8,0},{9,1... | collective-permute-start | bytes 1769480 | tf_op jit(solution)/shard_map/ppermute | solution.py:479
  412.4 22.0 %collective-permute-start.20 = (bf16[8,32,384]{2,1,0:T(8,128)(2,1)S(1)}, bf16[8,32,384]{2,1,0:T(8,128)(2,1)S(1)}, u32[]{:S(2)}, u32[]{:S(2)}) collective-permute-start(bf16[8,32,384]{2,1,0:T(8,128)(2,1)S(1)} %get-tuple-element.183), channel_id=1, source_target_pairs={{0,8},{1,9},{2,10},{3,11},{4,12},{5,13},{6,14},{7,15},{8,16},{9,17... | collective-permute-start | bytes 589832 | tf_op jit(solution)/shard_map/ppermute | solution.py:479
  420.3 16.3 %collective-permute-start.21 = (bf16[8,32,384]{2,1,0:T(8,128)(2,1)S(1)}, bf16[8,32,384]{2,1,0:T(8,128)(2,1)S(1)}, u32[]{:S(2)}, u32[]{:S(2)}) collective-permute-start(bf16[8,32,384]{2,1,0:T(8,128)(2,1)S(1)} %get-tuple-element.182), channel_id=1, source_target_pairs={{0,16},{1,17},{2,18},{3,19},{4,20},{5,21},{6,22},{7,23},{8,24},{9,... | collective-permute-start | bytes 589832 | tf_op jit(solution)/shard_map/ppermute | solution.py:479
  423.8 12.8 %collective-permute-start.22 = (bf16[8,32,384]{2,1,0:T(8,128)(2,1)S(1)}, bf16[8,32,384]{2,1,0:T(8,128)(2,1)S(1)}, u32[]{:S(2)}, u32[]{:S(2)}) collective-permute-start(bf16[8,32,384]{2,1,0:T(8,128)(2,1)S(1)} %get-tuple-element.181), channel_id=1, source_target_pairs={{0,24},{1,25},{2,26},{3,27},{4,28},{5,29},{6,30},{7,31},{8,0},{9,1... | collective-permute-start | bytes 589832 | tf_op jit(solution)/shard_map/ppermute | solution.py:479
  434.4 4.1 copy-start.27
  443.2 4.5 copy-start.21
  449.2 8.6 %copy-start.28 = (bf16[8,32,384]{2,1,0:T(8,128)(2,1)S(1)}, bf16[8,32,384]{2,1,0:T(8,128)(2,1)}, u32[]{:S(2)}) copy-start(bf16[8,32,384]{2,1,0:T(8,128)(2,1)} %copy-done.27) | copy-start | bytes 589828
  449.2 8.6 %copy-start.30 = (bf16[8,32,384]{2,1,0:T(8,128)(2,1)S(1)}, bf16[8,32,384]{2,1,0:T(8,128)(2,1)}, u32[]{:S(2)}) copy-start(bf16[8,32,384]{2,1,0:T(8,128)(2,1)} %copy-done.29) | copy-start | bytes 589828
  449.2 8.6 %copy-start.32 = (bf16[8,32,384]{2,1,0:T(8,128)(2,1)S(1)}, bf16[8,32,384]{2,1,0:T(8,128)(2,1)}, u32[]{:S(2)}) copy-start(bf16[8,32,384]{2,1,0:T(8,128)(2,1)} %copy-done.31) | copy-start | bytes 589828
  451.0 14.2 %all-to-all-start.4 = ((f32[32,1,448]{2,1,0:T(1,128)}), f32[32,1,448]{2,1,0:T(1,128)S(1)}, u32[]{:S(2)}, u32[]{:S(2)}) async-start(f32[32,1,448]{2,1,0:T(1,128)} %copy.87), calls=%async_computation.4 | async-start | bytes 131072 | tf_op jit(solution)/shard_map/all_to_all | solution.py:909
  465.2 11.7 %all-to-all-start.5 = ((f32[8,32,384]{2,1,0:T(8,128)}), f32[8,32,384]{2,1,0:T(8,128)S(1)}, u32[]{:S(2)}, u32[]{:S(2)}) async-start(f32[8,32,384]{2,1,0:T(8,128)} %fusion.21), calls=%async_computation.5 | async-start | bytes 786432 | tf_op jit(solution)/shard_map/all_to_all | solution.py:382
  (38 other events, 81.3 us)
Sparse Core Ops, SparseCore 0:
  11.7 155.3 all-gather.2
  170.6 68.7 all-gather.4
where the time goes:
time: 494 us; the launch traced here: 485 us
  Pallas kernels  174 us (35%)
  waiting for transfers between devices  122 us (25%)
  starting transfers between devices  74.7 us (15%)
  local copies, waits for them, and re-layouts  52.8 us (11%)
  other arithmetic  29 us (6%)
  matrix products  17.3 us (4%)
  between operations  15.6 us (3%)
    pallas_call x4, Pallas kernels, attention_call(): pl.pallas_call(kernel, out_shape=tuple(outputs), grid_spec=pltpu.Prefetch...  111 us
    ppermute x6, waiting for transfers between devices, from_planes(): lax.ppermute(piece, 'dev', [(i, (i + k * GROUP) % devices) for i in range...  34.2 us
    ppermute x13, waiting for transfers between devices, swapped(): return lax.ppermute(value, 'dev', [(i, i ^ bit) for i in range(devices)])  32.7 us
    pallas_call x1, Pallas kernels, mlp_all(): pl.pallas_call(mlp_kernel, out_shape=(total, total, jax.ShapeDtypeStruct(...  29.7 us
    ppermute x6, starting transfers between devices, from_planes(): lax.ppermute(piece, 'dev', [(i, (i + k * GROUP) % devices) for i in range...  19 us
    all_to_all x1, waiting for transfers between devices, body(): slab = lax.all_to_all(slab, 'dev', 0, 0, tiled=True).reshape(width, -1)  18.7 us
    unnamed x117, local copies, waits for them, and re-layouts  14.6 us
    ppermute x4, waiting for transfers between devices, shifted(): return lax.ppermute(shard, 'dev', pairs)  14.5 us
  transfers between devices with their start and end apart: 31, of which 13 were waited for; matrix products, arithmetic and copies ran while one was open for 12% of the time, Pallas kernels for 36%

commit v1 on v0

--- a/solution.py
+++ b/solution.py
@@ -159,7 +159,7 @@
 
 
 def backward_first_kernel(
-    low, high, seg, q_ref, kv_ref, left_ref, right_ref, o_ref, do_ref, lse_ref, dq_t, mid_ref, edge_ref,
+    low, high, seg, q_ref, kv_ref, left_ref, right_ref, o_ref, do_ref, lse_ref, dq_t, mid_ref, out_left, out_right,
     left_t, right_t, k_t, dkv, *, last
 ):
     step = pl.program_id(0)
@@ -186,11 +186,9 @@
     @pl.when(step == pl.num_programs(0) - 1)
     def _():
         mid_ref[:, :width] = mid_ref[:, :width] * SCALE
-        for side in range(2):
-            for j in range(edge):
-                part = slice(j * BK, (j + 1) * BK)
-                edge_ref[side, part, :width] = (dkv[side, part, :width] * SCALE).astype(edge_ref.dtype)
-                edge_ref[side, part, width:] = dkv[side, part, width:].astype(edge_ref.dtype)
+        for side, out in enumerate((out_left, out_right)):
+            out[:, :width] = (dkv[side, :, :width] * SCALE).astype(out.dtype)
+            out[:, width:] = dkv[side, :, width:].astype(out.dtype)
 
 
 def backward_mid_kernel(
@@ -274,7 +272,7 @@
     return attention_call(
         functools.partial(backward_first_kernel, last=(left.shape[0] + span) // BK), "backward_first", prefetch,
         [seg, q, kv, left, right, o, do, lse], "crwwwrrc",
-        [shaped(width, span), shaped(*kv.shape), shaped(2, *left.shape, dtype=jnp.bfloat16)], "cww",
+        [shaped(width, span), shaped(*kv.shape)] + [shaped(*left.shape, dtype=jnp.bfloat16)] * 2, "cwww",
         [halo, halo, pltpu.VMEM((width, span), jnp.bfloat16), pltpu.VMEM((2, *left.shape), jnp.float32)], 3,
     )
 
@@ -376,6 +374,63 @@
 
 def swapped(value, bit, devices):
     return lax.ppermute(value, "dev", [(i, i ^ bit) for i in range(devices)])
+
+
+def join_kernel(dq, mid0, mid1, left, right, out):
+    width = dq.shape[1]
+    step, edge = pl.program_id(0), pl.num_programs(0) // 2
+    halo = jnp.where(step < edge, left[...], right[...]).astype(F32)
+    out[:, :width] = dq[...]
+    out[:, width:] = (mid0[...] + mid1[...] + halo).astype(out.dtype)
+
+
+def joined_heads(dq, mid0, mid1, left, right):
+    span, width = dq.shape
+    size = BQ
+    half = span // (2 * size)
+    rows = [pl.BlockSpec((size, columns), lambda i: (i, 0)) for columns in (width, 2 * width, 2 * width, 3 * width)]
+    return pl.pallas_call(
+        join_kernel,
+        out_shape=shaped(span, 3 * width, dtype=BF16),
+        grid=(span // size,),
+        in_specs=rows[:3]
+        + [
+            pl.BlockSpec((size, 2 * width), lambda i: (jnp.minimum(i, half - 1), 0)),
+            pl.BlockSpec((size, 2 * width), lambda i: (jnp.maximum(i - half, 0), 0)),
+        ],
+        out_specs=rows[3],
+        cost_estimate=pl.CostEstimate(flops=0, bytes_accessed=10 << 20, transcendentals=0),
+        name="joined_heads",
+    )(dq, mid0, mid1, left, right)
+
+
+def tail_kernel(dqkv, weight, dy1, x_ref, gain, grad, sums, heads):
+    size = dqkv.shape[2]
+    dn1 = jnp.zeros(dy1.shape, F32)
+    for j in range(dqkv.shape[0]):
+        dn1 += lax.dot_general(
+            dqkv[j], weight[:, j * size : (j + 1) * size], NT, preferred_element_type=F32
+        )
+        heads[j : j + 1, :] = jnp.sum(dqkv[j].astype(F32), axis=0, keepdims=True)
+    unit, rstd = normalised(x_ref[...].astype(F32))
+    grad[...] = (dy1[...] + norm_back(unit, rstd, dn1 * gain[...])).astype(grad.dtype)
+    sums[0:1, :] = jnp.sum(dn1 * unit, axis=0, keepdims=True)
+    sums[1:2, :] = jnp.sum(dn1, axis=0, keepdims=True)
+
+
+def input_gradient(dqkv, weight, dy1, tokens, gain):
+    inputs = (dqkv, weight, dy1, tokens, gain[None])
+    outs = (shaped(*tokens.shape, dtype=BF16), shaped(8, tokens.shape[1]), shaped(GROUP, dqkv.shape[2]))
+    return pl.pallas_call(
+        tail_kernel,
+        out_shape=outs,
+        grid=(1,),
+        in_specs=[whole_spec(a) for a in inputs],
+        out_specs=[whole_spec(a) for a in outs],
+        compiler_params=pltpu.CompilerParams(vmem_limit_bytes=44 << 20),
+        cost_estimate=pl.CostEstimate(flops=2 * weight.size * tokens.shape[0], bytes_accessed=12 << 20, transcendentals=0),
+        name="input_gradient",
+    )(*inputs)
 
 
 def in_plane(stack, devices):
@@ -426,6 +481,7 @@
     b = jnp.stack([b, swapped(b, 2, devices)])
     a = jnp.stack([a, swapped(a, 2, devices)])
     b = jnp.stack([b, swapped(b, 4, devices)])
+    a, b, slab = lax.optimization_barrier((a, b, slab))
     far_a, far_b = swapped(a, 1, devices), swapped(b, 1, devices)
 
     def near_at(s, swap):
@@ -534,22 +590,25 @@
     dn2_ref[...] += lax.dot_general(dz, f1, NT, preferred_element_type=F32)
     for side, out in enumerate((keep1, send1)):
         out[...] = mm(n2_t[side], dz).astype(BF16).reshape(out.shape)
-    for part, out in zip(by_parity(turned(act), bits[2], rows), (keep2, send2)):
-        out[...] = mm(part, dml).astype(BF16).reshape(out.shape)
-
-
-def mlp_all(n2, dml, big, bias, me, shard_rows):
+    width = n2.shape[1]
+    parts = keep2.shape[2] // width
+    for part, out in zip(by_parity(turned(act), bits[2], parts * rows), (keep2, send2)):
+        grad = mm(part, dml).astype(BF16).reshape(out.shape[0], parts, rows, width)
+        for i in range(parts):
+            out[:, :, i * width : (i + 1) * width] = grad[:, i]
+
+
+def mlp_all(n2, dml, big, fc2, bias, me, shard_rows):
     tokens, width = n2.shape
     hidden, owners = bias.shape[0], width // shard_rows
     size = width // 2
     steps = hidden // size
     whole = pl.BlockSpec((tokens, width), lambda s, bits: (0, 0))
     first = pl.BlockSpec((owners // 2, shard_rows, size), lambda s, bits: (0, 0, s))
-    second = pl.BlockSpec((owners // 4, shard_rows, width), lambda s, bits: (s % 2, 0, s // 2))
+    second = pl.BlockSpec((owners // (2 * steps), shard_rows, hidden), lambda s, bits: (s, 0, 0))
     line = pl.BlockSpec((1, size), lambda s, bits: (0, s))
     grads = jax.ShapeDtypeStruct((owners // 2, shard_rows, hidden), BF16)
     total = jax.ShapeDtypeStruct((tokens, width), F32)
-    blocks = hidden // width
     return pl.pallas_call(
         mlp_kernel,
         out_shape=(total, total, jax.ShapeDtypeStruct((1, hidden), F32), grads, grads, grads, grads),
@@ -560,7 +619,7 @@
                 whole,
                 whole,
                 pl.BlockSpec((width, size), lambda s, bits: (0, s)),
-                pl.BlockSpec((size, width), lambda s, bits: (s % 2, blocks + s // 2)),
+                pl.BlockSpec((size, width), lambda s, bits: (s, 0)),
                 line,
             ],
             out_specs=[whole, whole, line, first, first, second, second],
@@ -571,7 +630,7 @@
             flops=4 * tokens * width * hidden, bytes_accessed=8 * width * hidden, transcendentals=2 * tokens * hidden
         ),
         name="mlp_all",
-    )(jnp.stack(position(me)).astype(jnp.int32), n2, dml, big, big, bias[None])
+    )(jnp.stack(position(me)).astype(jnp.int32), n2, dml, big, fc2, bias[None])
 
 
 def grad_kernel(bits, a_ref, b_ref, keep_ref, send_ref):
@@ -766,13 +825,9 @@
     spread = unpack_columns(packed.astype(F32), sizes, shard_rows)
     gain1, shift1, bias_qv, bias_proj, layer_attn, gain2, shift2, bias_fc1, bias_fc2, layer_mlp = spread
     if by_axes:
-        first = fc1_weight.reshape(shard_rows, devices, blocks, shard_rows).transpose(0, 2, 1, 3)
-        second = fc2_weight.reshape(blocks, shard_rows, width).transpose(1, 0, 2)
-        big = jnp.concatenate(
-            [first.reshape(shard_rows, hidden), second.reshape(shard_rows, hidden), proj_weight], axis=1
-        )
-        big = gathered(big)
-        w_proj = big[:, 2 * hidden :]
+        big = gathered(jnp.concatenate([fc1_weight, proj_weight], axis=1))
+        w_fc2 = gathered(fc2_weight)
+        w_proj = big[:, hidden:]
     else:
         w_proj, big = gathered(proj_weight), gathered(fc1_weight)
         w_fc2 = gathered(fc2_weight)
@@ -812,9 +867,8 @@
     d_fc2_bias = jnp.sum(dm, axis=0)
     dml = dm.astype(BF16)
     if by_axes:
-        bias_hidden = bias_fc1.reshape(devices, blocks, shard_rows).transpose(1, 0, 2).reshape(-1)
-        mlp, dn2, d_fc1_bias, keep1, send1, keep2, send2 = mlp_all(n2, dml, big, bias_hidden, me, shard_rows)
-        d_fc1_bias = d_fc1_bias.reshape(blocks, devices, shard_rows).transpose(1, 0, 2).reshape(-1)
+        mlp, dn2, d_fc1_bias, keep1, send1, keep2, send2 = mlp_all(n2, dml, big, w_fc2, bias_fc1, me, shard_rows)
+        d_fc1_bias = d_fc1_bias.reshape(-1)
     else:
         act, slope = gelu_parts(mm(n2, big) + bias_fc1)
         act = act.astype(BF16)
@@ -831,7 +885,6 @@
         )
         d_scale_mlp, d_fc2_bias, d_gain2, d_shift2, d_scale_attn, d_proj_bias = (totals[i] for i in range(6))
         got1, got2, got3 = (swapped(s, 1, devices) for s in (send1, send2, send3))
-        do, got1, got2, got3 = lax.optimization_barrier((do, got1, got2, got3))
         view = (devices // GROUP, 2, 2, shard_rows)
         halves = [
             tuple(s.reshape(*view, -1) for s in pair) for pair in ((keep1, got1), (keep2, got2), (keep3, got3))
@@ -855,54 +908,44 @@
     if by_axes:
         do_heads, out_a, out_b = lax.optimization_barrier((do_heads, out_a, out_b))
         in_a, in_b = swapped(out_a, 2, devices), swapped(out_b, 4, devices)
-    part_dq, mid0, edge = backward_first(prefetch, seg, q, kv, left, right, o_heads, do_heads, lse)
+    part_dq, mid0, out_left, out_right = backward_first(prefetch, seg, q, kv, left, right, o_heads, do_heads, lse)
     if by_axes:
         part_dq, in_a, in_b, w_qkv = lax.optimization_barrier((part_dq, in_a, in_b, w_qkv))
         out_a, sum_a, out_b, sum_b = second_sums(halves, in_a, in_b, me)
         part_dq, out_a, out_b = lax.optimization_barrier((part_dq, out_a, out_b))
         in_a, in_b = swapped(out_a, 4, devices), swapped(out_b, 2, devices)
-    from_right = shifted(edge[0], -GROUP, devices)
-    from_left = shifted(edge[1], GROUP, devices)
+    from_right = shifted(out_left, -GROUP, devices)
+    from_left = shifted(out_right, GROUP, devices)
     dq, mid1 = backward_second(prefetch, seg, q, kv, o_heads, do_heads, lse, part_dq, edge_blocks)
     dq, mid1, from_left, from_right = lax.optimization_barrier((dq, mid1, from_left, from_right))
     if by_axes:
         dq, in_a, in_b = lax.optimization_barrier((dq, in_a, in_b))
-    rest = span - halo
-    mid = mid0 + mid1 + jnp.pad(from_left.astype(F32), ((0, rest), (0, 0)))
-    mid = mid + jnp.pad(from_right.astype(F32), ((rest, 0), (0, 0)))
-    mid = mid.astype(BF16)
-    d_heads = jnp.concatenate([dq, mid], axis=1)
+    d_heads = joined_heads(dq, mid0, mid1, from_left, from_right)
     if by_axes:
         third = [(s.astype(F32) + i.astype(F32)).astype(BF16) for s, i in ((sum_a, in_a), (sum_b, in_b))]
         d_heads, third = lax.optimization_barrier((d_heads, jnp.concatenate(third, axis=-1)))
         own_sums, sums = from_planes(third, me, devices)
     dqkv = in_plane(d_heads.reshape(GROUP, rows, -1), devices)
     if by_axes:
-        dqkv, n1, sums[:2] = lax.optimization_barrier((dqkv, n1, sums[:2]))
+        dqkv, n1, sums[0] = lax.optimization_barrier((dqkv, n1, sums[0]))
     d_qkv = t_mm(n1, d_heads).astype(BF16).reshape(devices // GROUP, GROUP, shard_rows, -1)
     dqkv, d_qkv = lax.optimization_barrier((dqkv, d_qkv))
     own_qkv, got_qkv = from_planes(d_qkv, me, devices)
-    per_head = jnp.sum(dqkv.astype(F32), axis=1)
-    half = width // GROUP
+    grad_tokens, totals, per_head = input_gradient(dqkv, w_qkv, dy1, tokens, gain1)
+    d_gain1, d_shift1, half = totals[0], totals[1], width // GROUP
     d_qv_bias = jnp.concatenate([per_head[:, :half].reshape(-1), per_head[:, 2 * half :].reshape(-1)])
-    dn1 = mm_t(dqkv.transpose(1, 0, 2).reshape(rows, 3 * width), w_qkv)
     if by_axes:
-        dn1, sums[2:], got_qkv = lax.optimization_barrier((dn1, sums[2:], got_qkv))
+        d_gain1, sums[1:], got_qkv = lax.optimization_barrier((d_gain1, sums[1:], got_qkv))
     d_qkv = in_plane(total_of(own_qkv, got_qkv), devices).reshape(GROUP, shard_rows, 3, -1)
     d_qkv = d_qkv.transpose(1, 2, 0, 3).reshape(shard_rows, 3 * width)
     if by_axes:
         sums = total_of(own_sums, sums)
-        d_fc1 = sums[:, :hidden].reshape(shard_rows, blocks, devices, shard_rows).transpose(0, 2, 1, 3)
-        d_fc1 = d_fc1.reshape(shard_rows, hidden)
+        d_fc1 = sums[:, :hidden]
         cut = width // 2
         at = hidden + cut
         d_fc2 = sums[:, at : at + hidden].reshape(shard_rows, blocks, width).transpose(1, 0, 2)
         d_fc2 = d_fc2.reshape(blocks * shard_rows, width)
         d_proj = jnp.concatenate([sums[:, hidden:at], sums[:, at + hidden :]], axis=1)
-    d_gain1 = jnp.sum(dn1 * u1, axis=0)
-    d_shift1 = jnp.sum(dn1, axis=0)
-    grad_tokens = (dy1 + norm_back(u1, rstd1, dn1 * gain1)).astype(BF16)
-
     small = (
         d_gain1, d_shift1, d_qv_bias, d_proj_bias, d_scale_attn, d_gain2, d_shift2, d_fc1_bias, d_fc2_bias, d_scale_mlp,
     )

time: 494 us -> 507 us (1.026); the launches traced: 485 us -> 505 us
  waiting for transfers between devices: 122 us -> 176 us
  other arithmetic: 29 us -> 11.9 us
  local copies, waits for them, and re-layouts: 52.8 us -> 38 us
  Pallas kernels: 174 us -> 185 us
  matrix products: 17.3 us -> 9.99 us
  starting transfers between devices: 74.7 us -> 69.3 us
    all_gather x2 -> x3, waiting for transfers between devices: 0.02 us -> 39.5 us  [gathered(): return lax.all_gather(shard, 'dev', axis=0, tiled=True)]
    ppermute x13, waiting for transfers between devices: 32.7 us -> 62.5 us  [swapped(): return lax.ppermute(value, 'dev', [(i, i ^ bit) for i in range(devices)])]
    all_to_all x1, waiting for transfers between devices: 18.7 us -> 0.01 us  [body(): slab = lax.all_to_all(slab, 'dev', 0, 0, tiled=True).reshape(width, -1)]
    pallas_call x0 -> x2, Pallas kernels: none -> 17.4 us  [the longest x1 8.89 us: joined_heads(): pl.pallas_call(join_kernel, out_shape=shaped(span, 3 * width, dtype=BF16)...]
    all_to_all x3, waiting for transfers between devices: 7.67 us -> 22.7 us  [in_plane(): lax.all_to_all(stack, 'dev', 0, 0, axis_index_groups=groups_of(devices),...]
    ppermute x4, waiting for transfers between devices: 14.5 us -> 0.01 us  [shifted(): return lax.ppermute(shard, 'dev', pairs)]
    reshape x9 -> x1, local copies, waits for them, and re-layouts: 12.8 us -> 0.09 us  [unpack_columns(): part = lines[at:at + count].reshape(count, -1, rows)]
    dot_general x1 -> x0, matrix products: 7.44 us -> none  [mm_t(): return jnp.einsum('tf,df->td', left, right, preferred_element_type=F32)]
  transfers between devices with their start and end apart: 31 -> 32, of which waited for: 13 -> 13; matrix products, arithmetic and copies ran while one was open for 12% -> 6% of each run, Pallas kernels for 36% -> 33%
where the time goes in v1:
time: 507 us; the launch traced here: 505 us
  Pallas kernels  185 us (36%)
  waiting for transfers between devices  176 us (35%)
  starting transfers between devices  69.3 us (14%)
  local copies, waits for them, and re-layouts  38 us (7%)
  between operations  14.7 us (3%)
  other arithmetic  11.9 us (2%)
  matrix products  9.99 us (2%)
    pallas_call x4, Pallas kernels, attention_call(): pl.pallas_call(kernel, out_shape=tuple(outputs), grid_spec=pltpu.Prefetch...  105 us
    ppermute x13, waiting for transfers between devices, swapped(): return lax.ppermute(value, 'dev', [(i, i ^ bit) for i in range(devices)])  62.5 us
    all_gather x3, waiting for transfers between devices, gathered(): return lax.all_gather(shard, 'dev', axis=0, tiled=True)  39.5 us
    pallas_call x1, Pallas kernels, mlp_all(): pl.pallas_call(mlp_kernel, out_shape=(total, total, jax.ShapeDtypeStruct(...  29.1 us
    ppermute x6, waiting for transfers between devices, from_planes(): lax.ppermute(piece, 'dev', [(i, (i + k * GROUP) % devices) for i in range...  28.5 us
    all_to_all x3, waiting for transfers between devices, in_plane(): lax.all_to_all(stack, 'dev', 0, 0, axis_index_groups=groups_of(devices),...  22.7 us
    unnamed x90, local copies, waits for them, and re-layouts  19.3 us
    all_to_all x1, waiting for transfers between devices, to_tokens(): lax.all_to_all(sent, 'dev', 0, 0, axis_index_groups=groups_of(devices), t...  17.3 us
  transfers between devices with their start and end apart: 32, of which 13 were waited for; matrix products, arithmetic and copies ran while one was open for 6% of the time, Pallas kernels for 33%

profile of v1, /device:TPU:0, one launch (start us, length us, event | category | flops | bytes accessed | tf_op | source)
XLA Modules:
  0.0 504.9 jit_solution(8183714317355320112)
XLA Ops:
  7.3 1.7 pad_maximum_fusion.5
  12.7 7.3 %all-to-all-start = ((bf16[32,32,512]{2,1,0:T(8,128)(2,1)}), bf16[32,32,512]{2,1,0:T(8,128)(2,1)S(1)}, u32[]{:S(2)}, u32[]{:S(2)}) async-start(bf16[32,32,512]{2,1,0:T(8,128)(2,1)} %bitcast.14), calls=%async_computation | async-start | bytes 2097152 | tf_op jit(solution)/shard_map/all_to_all | solution.py:823
  20.2 1.8 collective-permute-start.2
  23.5 19.3 %collective-permute-done.2 = bf16[384,512]{1,0:T(8,128)(2,1)S(1)} collective-permute-done((bf16[384,512]{1,0:T(8,128)(2,1)S(1)}, bf16[384,512]{1,0:T(8,128)(2,1)S(1)}, u32[]{:S(2)}, u32[]{:S(2)}) %collective-permute-start.2) | collective-permute-done | bytes 393248 | tf_op jit(solution)/shard_map/ppermute | solution.py:376
  45.9 23.0 %collective-permute-done.3 = bf16[2,384,512]{2,1,0:T(8,128)(2,1)S(1)} collective-permute-done((bf16[2,384,512]{2,1,0:T(8,128)(2,1)S(1)}, bf16[2,384,512]{2,1,0:T(8,128)(2,1)S(1)}, u32[]{:S(2)}, u32[]{:S(2)}) %collective-permute-start.3) | collective-permute-done | bytes 786464 | tf_op jit(solution)/shard_map/ppermute | solution.py:376
  69.0 5.2 %collective-permute-done.1 = bf16[2,384,512]{2,1,0:T(8,128)(2,1)S(1)} collective-permute-done((bf16[2,384,512]{2,1,0:T(8,128)(2,1)S(1)}, bf16[2,384,512]{2,1,0:T(8,128)(2,1)S(1)}, u32[]{:S(2)}, u32[]{:S(2)}) %collective-permute-start.1) | collective-permute-done | bytes 786464 | tf_op jit(solution)/shard_map/ppermute | solution.py:376
  76.0 1.7 copy.85
  77.7 1.8 reshape.221
  82.9 11.4 %plane_qkv.1 = (bf16[3072,1024]{1,0:T(8,128)(2,1)}, bf16[3072,128]{1,0:T(8,128)(2,1)S(1)}, bf16[3072,256]{1,0:T(8,128)(2,1)S(1)}) custom-call(s32[4]{0:T(128)S(1)} %pad_add_fusion.2.bits, bf16[2,2,384,512]{3,2,1,0:T(8,128)(2,1)S(1)} %copy-done.7, bf16[2,2,384,512]{3,2,1,0:T(8,128)(2,1)} %collective-permute-done.4.far_a, ...), custom_call_target="tpu_custom_call" | custom-call | flops 5368709120 | bytes 16777216 | tf_op jit(solution)/shard_map/plane_qkv/pallas_call | solution.py:502
  96.2 3.0 collective-permute-start.6
  103.4 32.6 %forward_mid.1 = (f32[128,3072]{1,0:T(8,128)S(1)}, f32[8,3072]{1,0:T(8,128)S(1)}) custom-call(s32[12]{0:T(128)S(1)} %get-tuple-element.209.low, s32[12]{0:T(128)S(1)} %get-tuple-element.210.high, s32[2,3072]{1,0:T(2,128)S(1)} %pad_add_fusion.seg, bf16[3072,128]{1,0:T(8,128)(2,1)S(1)} %copy-done.19, bf16[3072,256]{1,0:T(8,128)(2,1)S(1)} %copy-done.5), custom_call_target="tpu_custom_call" | custom-call | flops 3221225472 | bytes 8388608 | tf_op jit(solution)/shard_map/forward_mid/pallas_call | solution.py:231
  136.0 12.6 %forward_edge.1 = (bf16[3072,128]{1,0:T(8,128)(2,1)}, f32[8,3072]{1,0:T(8,128)S(1)}) custom-call(s32[12]{0:T(128)S(1)} %get-tuple-element.209.low, s32[12]{0:T(128)S(1)} %get-tuple-element.210.high, s32[2,3072]{1,0:T(2,128)S(1)} %pad_add_fusion.seg, bf16[3072,128]{1,0:T(8,128)(2,1)S(1)} %copy-done.20, bf16[1536,256]{1,0:T(8,128)(2,1)S(1)} %collective-permute-done.6.left_ref, ...), custom_call_target="tpu_custom_call" | custom-call | flops 3221225472 | bytes 8388608 | tf_op jit(solution)/shard_map/forward_edge/pallas_call | solution.py:231
  148.7 4.5 all-to-all-start.1
  153.7 17.3 %all-to-all-done.1 = bf16[8,384,1,128]{3,1,2,0:T(8,128)(2,1)} async-done(((bf16[8,384,1,128]{3,1,2,0:T(8,128)(2,1)}), bf16[8,384,1,128]{3,1,2,0:T(8,128)(2,1)}, u32[]{:S(2)}, u32[]{:S(2)}) %all-to-all-start.1) | async-done | bytes 786464 | tf_op jit(solution)/shard_map/all_to_all | solution.py:362
  171.0 3.0 fusion.7
  175.6 39.5 %all-gather.6.cloned.1.call-done.f2_ref = bf16[4096,1024]{1,0:T(8,128)(2,1)} async-done(((bf16[128,1024]{1,0:T(8,128)(2,1)}), bf16[4096,1024]{1,0:T(8,128)(2,1)}) %all-gather.6.cloned.1.call-update) | async-done | bytes 8388624 | tf_op jit(solution)/shard_map/all_gather | solution.py:332
  215.1 29.1 %mlp_all.1 = (f32[384,1024]{1,0:T(8,128)}, f32[384,1024]{1,0:T(8,128)}, f32[1,4096]{1,0:T(1,128)S(1)}, bf16[16,32,4096]{2,1,0:T(8,128)(2,1)}, bf16[16,32,4096]{2...) custom-call(s32[3]{0:T(128)S(1)} %pad_add_fusion.1.bits, ...), custom_call_target="tpu_custom_call" | custom-call | flops 6442450944 | bytes 33554432 | tf_op jit(solution)/shard_map/mlp_all/pallas_call | solution.py:612
  244.8 2.1 copy_bitcast_fusion.o_ref
  246.9 8.8 %after_mlp.1 = (bf16[384,1024]{1,0:T(8,128)(2,1)}, f32[384,1024]{1,0:T(8,128)}, f32[8,1024]{1,0:T(8,128)S(1)}, bf16[8,384,128]{2,1,0:T(8,128)(2,1)S(1)}, bf16[16...) custom-call(s32[3]{0:T(128)S(1)} %pad_add_fusion.1.bits, f32[384,1024]{1,0:T(8,128)} %get-tuple-element.100.mlp, ...), custom_call_target="tpu_custom_call" | custom-call | flops 1610612736 | bytes 20971520 | tf_op jit(solution)/shard_map/after_mlp/pallas_call | solution.py:687
  257.0 4.4 all-to-all-start.2
  261.5 3.0 copy-done.1
  264.5 6.1 %first_sends.1 = (bf16[4,2,32,4608]{3,2,1,0:T(8,128)(2,1)S(1)}, bf16[4,2,32,4608]{3,2,1,0:T(8,128)(2,1)S(1)}) custom-call(s32[3]{0:T(128)S(1)} %pad_add_fusion.1.bits, bf16[4,2,2,32,4096]{4,3,2,1,0:T(8,128)(2,1)S(1)} %bitcast.161, bf16[4,2,2,32,4096]{4,3,2,1,0:T(8,128)(2,1)} %bitcast.44.refs_1_.refs_7_, bf16[4,2,2,32,1024]{4,3,2,1,0:T(8,128)(2,1)S(1)} %bitcast.147, ...), custom_call_target="tpu_custom_call" | custom-call | bytes 16777216 | tf_op jit(solution)/shard_map/first_sends/pallas_call | solution.py:724
  273.5 8.7 %all-to-all-done.2 = bf16[8,384,128]{2,1,0:T(8,128)(2,1)} async-done(((bf16[8,384,128]{2,1,0:T(8,128)(2,1)}), bf16[8,384,128]{2,1,0:T(8,128)(2,1)}, u32[]{:S(2)}, u32[]{:S(2)}) %all-to-all-start.2) | async-done | bytes 786464 | tf_op jit(solution)/shard_map/all_to_all | solution.py:437
  285.6 33.4 %backward_first.1 = (f32[128,3072]{1,0:T(8,128)}, f32[3072,256]{1,0:T(8,128)}, bf16[1536,256]{1,0:T(8,128)(2,1)S(1)}, bf16[1536,256]{1,0:T(8,128)(2,1)S(1)}) custom-call(s32[12]{0:T(128)S(1)} %get-tuple-element.209.low, s32[12]{0:T(128)S(1)} %get-tuple-element.210.high, s32[2,3072]{1,0:T(2,128)S(1)} %pad_add_fusion.seg, bf16[3072,128]{1,0:T(8,128)(2,1)S(1)} %copy-done.21, ...), custom_call_target="tpu_custom_call" | custom-call | flops 3221225472 | bytes 8388608 | tf_op jit(solution)/shard_map/backward_first/pallas_call | solution.py:231
  320.7 13.9 %collective-permute-done.11.refs_2_.refs_5_.refs_8_.refs_11_ = bf16[4,2,32,4608]{3,2,1,0:T(8,128)(2,1)} collective-permute-done((bf16[4,2,32,4608]{3,2,1,0:T(8,128)(2,1)}, bf16[4,2,32,4608]{3,2,1,0:T(8,128)(2,1)}, u32[]{:S(2)}, u32[]{:S(2)}) %collective-permute-start.11) | collective-permute-done | bytes 2359328 | tf_op jit(solution)/shard_map/ppermute | solution.py:376
  334.7 7.3 %second_sums.1 = (bf16[4,32,4608]{2,1,0:T(8,128)(2,1)S(1)}, bf16[4,32,4608]{2,1,0:T(8,128)(2,1)S(1)}, bf16[4,32,4608]{2,1,0:T(8,128)(2,1)S(1)}, bf16[4,32,4608]{2,1,0:T(8,128)(2,1)S(1)}) custom-call(s32[3]{0:T(128)S(1)} %pad_add_fusion.1.bits, bf16[4,2,2,32,4096]{4,3,2,1,0:T(8,128)(2,1)} %bitcast.159, bf16[4,2,2,32,4096]{4,3,2,1,0:T(8,128)(2,1)} %bitcast.44.refs_1_.refs_7_, ...), custom_call_target="tpu_custom_call" | custom-call | bytes 16777216 | tf_op jit(solution)/shard_map/second_sums/pallas_call | solution.py:724
  341.9 1.5 collective-permute-start.15
  344.0 3.6 collective-permute-start.13
  348.9 26.3 %backward_second.1 = (bf16[3072,128]{1,0:T(8,128)(2,1)S(1)}, f32[3072,256]{1,0:T(8,128)}) custom-call(s32[12]{0:T(128)S(1)} %get-tuple-element.209.low, s32[12]{0:T(128)S(1)} %get-tuple-element.210.high, s32[2,3072]{1,0:T(2,128)S(1)} %pad_add_fusion.seg, bf16[3072,128]{1,0:T(8,128)(2,1)S(1)} %copy-done.22, bf16[3072,256]{1,0:T(8,128)(2,1)S(1)} %copy-done.6, ...), custom_call_target="tpu_custom_call" | custom-call | flops 3221225472 | bytes 8388608 | tf_op jit(solution)/shard_map/backward_second/pallas_call | solution.py:231
  377.0 1.7 pad_maximum_fusion
  378.7 8.9 %joined_heads.1 = bf16[3072,384]{1,0:T(8,128)(2,1)} custom-call(bf16[3072,128]{1,0:T(8,128)(2,1)} %copy-done.9, f32[3072,256]{1,0:T(8,128)} %get-tuple-element.131.mid0, f32[3072,256]{1,0:T(8,128)} %get-tuple-element.132.mid1, bf16[1536,256]{1,0:T(8,128)(2,1)} %copy-done.26, bf16[1536,256]{1,0:T(8,128)(2,1)} %copy-done.27), custom_call_target="tpu_custom_call" | custom-call | bytes 10485760 | tf_op jit(solution)/shard_map/joined_heads/pallas_call | solution.py:392
  387.6 4.4 all-to-all-start.3
  392.1 1.5 dynamic-slice_bitcast_fusion
  393.6 5.8 %collective-permute-start.17 = (bf16[32,9216]{1,0:T(8,128)(2,1)S(1)}, bf16[32,9216]{1,0:T(8,128)(2,1)S(1)}, u32[]{:S(2)}, u32[]{:S(2)}) collective-permute-start(bf16[32,9216]{1,0:T(8,128)(2,1)S(1)} %get-tuple-element.170), channel_id=1, source_target_pairs={{0,8},{1,9},{2,10},{3,11},{4,12},{5,13},{6,14},{7,15},{8,16},{9,17... | collective-permute-start | bytes 1769480 | tf_op jit(solution)/shard_map/ppermute | solution.py:535
  402.6 1.5 collective-permute-start.19
  404.2 9.8 %collective-permute-done.17 = bf16[32,9216]{1,0:T(8,128)(2,1)S(1)} collective-permute-done((bf16[32,9216]{1,0:T(8,128)(2,1)S(1)}, bf16[32,9216]{1,0:T(8,128)(2,1)S(1)}, u32[]{:S(2)}, u32[]{:S(2)}) %collective-permute-start.17) | collective-permute-done | bytes 589856 | tf_op jit(solution)/shard_map/ppermute | solution.py:535
  414.0 7.5 %all-to-all-done.3.dqkv = bf16[8,384,384]{2,1,0:T(8,128)(2,1)} async-done(((bf16[8,384,384]{2,1,0:T(8,128)(2,1)}), bf16[8,384,384]{2,1,0:T(8,128)(2,1)}, u32[]{:S(2)}, u32[]{:S(2)}) %all-to-all-start.3) | async-done | bytes 2359328 | tf_op jit(solution)/shard_map/all_to_all | solution.py:437
  421.5 7.0 %convolution_convert_fusion = bf16[1024,384]{1,0:T(8,128)(2,1)S(1)} fusion(bf16[3072,1024]{1,0:T(8,128)(2,1)} %get-tuple-element.143, bf16[3072,384]{1,0:T(8,128)(2,1)} %joined_heads.1), kind=kOutput, calls=%fused_computation.12 | convolution fusion | flops 2416312320 | bytes 9437184 | tf_op jit(solution)/shard_map/td,tf->df/dot_general | solution.py:306
  428.6 5.8 %collective-permute-start.20 = (bf16[8,32,384]{2,1,0:T(8,128)(2,1)S(1)}, bf16[8,32,384]{2,1,0:T(8,128)(2,1)}, u32[]{:S(2)}, u32[]{:S(2)}) collective-permute-start(bf16[8,32,384]{2,1,0:T(8,128)(2,1)S(1)} %get-tuple-element.179), channel_id=1, source_target_pairs={{0,8},{1,9},{2,10},{3,11},{4,12},{5,13},{6,14},{7,15},{8,16},{9,17... | collective-permute-start | bytes 589832 | tf_op jit(solution)/shard_map/ppermute | solution.py:535
  435.3 1.6 collective-permute-start.22
  436.9 8.5 %input_gradient.1 = (bf16[384,1024]{1,0:T(8,128)(2,1)}, f32[8,1024]{1,0:T(8,128)S(1)}, f32[8,384]{1,0:T(8,128)S(1)}) custom-call(bf16[8,384,384]{2,1,0:T(8,128)(2,1)} %all-to-all-done.3.dqkv, bf16[1024,3072]{1,0:T(8,128)(2,1)} %all-gather.8.cloned.1.call-done.weight, f32[384,1024]{1,0:T(8,128)S(1)} %copy-done.3, bf16[384,1024]{1,0:T(8,128)(2,1)S(1)} %copy-done.2, ...), custom_call_target="tpu_custom_call" | custom-call | flops 2415919104 | bytes 12582912 | tf_op jit(solution)/shard_map/input_gradient/pallas_call | solution.py:424
  445.7 18.7 %collective-permute-done.21 = bf16[8,32,384]{2,1,0:T(8,128)(2,1)} collective-permute-done((bf16[8,32,384]{2,1,0:T(8,128)(2,1)S(1)}, bf16[8,32,384]{2,1,0:T(8,128)(2,1)}, u32[]{:S(2)}, u32[]{:S(2)}) %collective-permute-start.21) | collective-permute-done | bytes 196640 | tf_op jit(solution)/shard_map/ppermute | solution.py:535
  464.4 1.9 fusion.6
  469.5 8.6 %all-to-all-start.4 = ((f32[32,1,448]{2,1,0:T(1,128)}), f32[32,1,448]{2,1,0:T(1,128)S(1)}, u32[]{:S(2)}, u32[]{:S(2)}) async-start(f32[32,1,448]{2,1,0:T(1,128)} %all_to_all.25), calls=%async_computation.4 | async-start | bytes 131072 | tf_op jit(solution)/shard_map/all_to_all | solution.py:952
  478.0 2.0 fusion.9
  480.7 4.8 all-to-all-done.4
  485.4 3.5 all-to-all-start.5
  490.7 6.5 %all-to-all-done.5 = f32[8,32,384]{2,1,0:T(8,128)S(1)} async-done(((f32[8,32,384]{2,1,0:T(8,128)}), f32[8,32,384]{2,1,0:T(8,128)S(1)}, u32[]{:S(2)}, u32[]{:S(2)}) %all-to-all-start.5) | async-done | bytes 393248 | tf_op jit(solution)/shard_map/all_to_all | solution.py:437
  (200 shorter events, 46.0 us)
Async XLA Ops:
  7.2 4.1 copy-start.37
  7.2 4.1 copy-start.38
  7.2 4.1 copy-start.39
  7.2 4.1 copy-start.32
  7.3 163.7 %all-gather.4.cloned.1.call-start = ((), (), s32[]{:S(2)}) async-start(), calls=%async_computation.6 | async-start | bytes 10813440 | tf_op jit(solution)/shard_map/all_gather | solution.py:332
  9.1 206.0 %all-gather.6.cloned.1.call-start = ((), (), s32[]{:S(2)}) async-start(), calls=%async_computation.7 | async-start | bytes 8650752 | tf_op jit(solution)/shard_map/all_gather | solution.py:332
  11.6 8.5 %copy-start.2 = (bf16[384,1024]{1,0:T(8,128)(2,1)S(1)}, bf16[384,1024]{1,0:T(8,128)(2,1)}, u32[]{:S(2)}) copy-start(bf16[384,1024]{1,0:T(8,128)(2,1)} %x_ref.3) | copy-start | bytes 2359300
  12.7 62.8 %all-to-all-start = ((bf16[32,32,512]{2,1,0:T(8,128)(2,1)}), bf16[32,32,512]{2,1,0:T(8,128)(2,1)S(1)}, u32[]{:S(2)}, u32[]{:S(2)}) async-start(bf16[32,32,512]{2,1,0:T(8,128)(2,1)} %bitcast.14), calls=%async_computation | async-start | bytes 2097152 | tf_op jit(solution)/shard_map/all_to_all | solution.py:823
  20.0 300.7 %all-gather.8.cloned.1.call-start = ((), (), s32[]{:S(2)}) async-start(), calls=%async_computation.8 | async-start | bytes 6488064 | tf_op jit(solution)/shard_map/all_gather | solution.py:332
  20.2 22.6 %collective-permute-start.2 = (bf16[384,512]{1,0:T(8,128)(2,1)S(1)}, bf16[384,512]{1,0:T(8,128)(2,1)S(1)}, u32[]{:S(2)}, u32[]{:S(2)}) collective-permute-start(bf16[384,512]{1,0:T(8,128)(2,1)S(1)} %get-tuple-element.184), channel_id=1, source_target_pairs={{0,2},{1,3},{2,0},{3,1},{4,6},{5,7},{6,4},{7,5},{8,10},{9,11},{10,... | collective-permute-start | bytes 1179656 | tf_op jit(solution)/shard_map/ppermute | solution.py:376
  22.0 22.4 %collective-permute-start = (bf16[384,512]{1,0:T(8,128)(2,1)S(1)}, bf16[384,512]{1,0:T(8,128)(2,1)S(1)}, u32[]{:S(2)}, u32[]{:S(2)}) collective-permute-start(bf16[384,512]{1,0:T(8,128)(2,1)S(1)} %get-tuple-element.185), channel_id=1, source_target_pairs={{0,4},{1,5},{2,6},{3,7},{4,0},{5,1},{6,2},{7,3},{8,12},{9,13},{10,... | collective-permute-start | bytes 1179656 | tf_op jit(solution)/shard_map/ppermute | solution.py:376
  42.9 26.0 %collective-permute-start.3 = (bf16[2,384,512]{2,1,0:T(8,128)(2,1)S(1)}, bf16[2,384,512]{2,1,0:T(8,128)(2,1)S(1)}, u32[]{:S(2)}, u32[]{:S(2)}) collective-permute-start(bf16[2,384,512]{2,1,0:T(8,128)(2,1)S(1)} %get-tuple-element.181), channel_id=1, source_target_pairs={{0,4},{1,5},{2,6},{3,7},{4,0},{5,1},{6,2},{7,3},{8,12},{9,13},{10,... | collective-permute-start | bytes 2359304 | tf_op jit(solution)/shard_map/ppermute | solution.py:376
  44.5 29.7 %collective-permute-start.1 = (bf16[2,384,512]{2,1,0:T(8,128)(2,1)S(1)}, bf16[2,384,512]{2,1,0:T(8,128)(2,1)S(1)}, u32[]{:S(2)}, u32[]{:S(2)}) collective-permute-start(bf16[2,384,512]{2,1,0:T(8,128)(2,1)S(1)} %get-tuple-element.187), channel_id=1, source_target_pairs={{0,2},{1,3},{2,0},{3,1},{4,6},{5,7},{6,4},{7,5},{8,10},{9,11},{10,... | collective-permute-start | bytes 2359304 | tf_op jit(solution)/shard_map/ppermute | solution.py:376
  74.2 5.4 %copy-start.42 = (s32[12]{0:T(128)S(1)}, s32[12]{0:T(128)}, u32[]{:S(2)}) copy-start(s32[12]{0:T(128)} %param.19) | copy-start | bytes 148
  75.5 6.0 %collective-permute-start.4 = (bf16[2,2,384,512]{3,2,1,0:T(8,128)(2,1)}, bf16[2,2,384,512]{3,2,1,0:T(8,128)(2,1)}, u32[]{:S(2)}, u32[]{:S(2)}) collective-permute-start(bf16[2,2,384,512]{3,2,1,0:T(8,128)(2,1)} %pad_maximum_fusion.1.near_a), channel_id=1, source_target_pairs={{0,1},{1,0},{2,3},{3,2},{4,5},{5,4},{6,7},{7,6},{8,9},{9,8},{10,11... | collective-permute-start | bytes 4718600 | tf_op jit(solution)/shard_map/ppermute | solution.py:376
  75.5 6.0 %collective-permute-start.5 = (bf16[2,2,384,512]{3,2,1,0:T(8,128)(2,1)S(1)}, bf16[2,2,384,512]{3,2,1,0:T(8,128)(2,1)}, u32[]{:S(2)}, u32[]{:S(2)}) collective-permute-start(bf16[2,2,384,512]{3,2,1,0:T(8,128)(2,1)S(1)} %pad_maximum_fusion.2.near_b), channel_id=1, source_target_pairs={{0,1},{1,0},{2,3},{3,2},{4,5},{5,4},{6,7},{7,6},{8,9},{9,8},{10,11... | collective-permute-start | bytes 4718600 | tf_op jit(solution)/shard_map/ppermute | solution.py:376
  96.2 39.8 %collective-permute-start.6 = (bf16[1536,256]{1,0:T(8,128)(2,1)}, bf16[1536,256]{1,0:T(8,128)(2,1)S(1)}, u32[]{:S(2)}, u32[]{:S(2)}) collective-permute-start(bf16[1536,256]{1,0:T(8,128)(2,1)} %get-tuple-element.172), channel_id=1, source_target_pairs={{0,8},{1,9},{2,10},{3,11},{4,12},{5,13},{6,14},{7,15},{8,16},{9,17... | collective-permute-start | bytes 2359304 | tf_op jit(solution)/shard_map/ppermute | solution.py:368
  99.3 36.7 %collective-permute-start.7 = (bf16[1536,256]{1,0:T(8,128)(2,1)}, bf16[1536,256]{1,0:T(8,128)(2,1)}, u32[]{:S(2)}, u32[]{:S(2)}) collective-permute-start(bf16[1536,256]{1,0:T(8,128)(2,1)} %get-tuple-element.171), channel_id=1, source_target_pairs={{8,0},{9,1},{10,2},{11,3},{12,4},{13,5},{14,6},{15,7},{16,8},{17,9... | collective-permute-start | bytes 2359304 | tf_op jit(solution)/shard_map/ppermute | solution.py:368
  103.4 32.6 %copy-start.20 = (bf16[3072,128]{1,0:T(8,128)(2,1)S(1)}, bf16[3072,128]{1,0:T(8,128)(2,1)}, u32[]{:S(2)}) copy-start(bf16[3072,128]{1,0:T(8,128)(2,1)} %copy-done.18) | copy-start | bytes 2359300
  136.0 12.7 %copy-start.12 = (bf16[1536,256]{1,0:T(8,128)(2,1)}, bf16[1536,256]{1,0:T(8,128)(2,1)S(1)}, u32[]{:S(2)}) copy-start(bf16[1536,256]{1,0:T(8,128)(2,1)S(1)} %collective-permute-done.6.left_ref) | copy-start | bytes 2359300
  148.7 4.9 copy-start.24
  148.7 22.4 %all-to-all-start.1 = ((bf16[8,384,1,128]{3,1,2,0:T(8,128)(2,1)}), bf16[8,384,1,128]{3,1,2,0:T(8,128)(2,1)}, u32[]{:S(2)}, u32[]{:S(2)}) async-start(bf16[8,384,1,128]{3,1,2,0:T(8,128)(2,1)} %bitcast.34), calls=%async_computation.1 | async-start | bytes 1572864 | tf_op jit(solution)/shard_map/all_to_all | solution.py:362
  244.2 17.2 %collective-permute-start.8 = (bf16[16,32,4096]{2,1,0:T(8,128)(2,1)}, bf16[16,32,4096]{2,1,0:T(8,128)(2,1)}, u32[]{:S(2)}, u32[]{:S(2)}) collective-permute-start(bf16[16,32,4096]{2,1,0:T(8,128)(2,1)} %get-tuple-element.105), channel_id=1, source_target_pairs={{0,1},{1,0},{2,3},{3,2},{4,5},{5,4},{6,7},{7,6},{8,9},{9,8},{10,11... | collective-permute-start | bytes 12582920 | tf_op jit(solution)/shard_map/ppermute | solution.py:376
  244.6 16.9 %collective-permute-start.10 = (bf16[16,32,4096]{2,1,0:T(8,128)(2,1)}, bf16[16,32,4096]{2,1,0:T(8,128)(2,1)}, u32[]{:S(2)}, u32[]{:S(2)}) collective-permute-start(bf16[16,32,4096]{2,1,0:T(8,128)(2,1)} %get-tuple-element.109), channel_id=1, source_target_pairs={{0,1},{1,0},{2,3},{3,2},{4,5},{5,4},{6,7},{7,6},{8,9},{9,8},{10,11... | collective-permute-start | bytes 12582920 | tf_op jit(solution)/shard_map/ppermute | solution.py:376
  256.6 4.8 copy-start
  256.6 4.8 collective-permute-start.9
  257.0 25.2 %all-to-all-start.2 = ((bf16[8,384,128]{2,1,0:T(8,128)(2,1)}), bf16[8,384,128]{2,1,0:T(8,128)(2,1)}, u32[]{:S(2)}, u32[]{:S(2)}) async-start(bf16[8,384,128]{2,1,0:T(8,128)(2,1)} %copy-done.8), calls=%async_computation.2 | async-start | bytes 1572864 | tf_op jit(solution)/shard_map/all_to_all | solution.py:437
  282.2 52.4 %collective-permute-start.11 = (bf16[4,2,32,4608]{3,2,1,0:T(8,128)(2,1)}, bf16[4,2,32,4608]{3,2,1,0:T(8,128)(2,1)}, u32[]{:S(2)}, u32[]{:S(2)}) collective-permute-start(bf16[4,2,32,4608]{3,2,1,0:T(8,128)(2,1)} %copy-done.11), channel_id=1, source_target_pairs={{0,2},{1,3},{2,0},{3,1},{4,6},{5,7},{6,4},{7,5},{8,10},{9,11},{10,... | collective-permute-start | bytes 7077896 | tf_op jit(solution)/shard_map/ppermute | solution.py:376
  282.2 52.5 %collective-permute-start.12 = (bf16[4,2,32,4608]{3,2,1,0:T(8,128)(2,1)}, bf16[4,2,32,4608]{3,2,1,0:T(8,128)(2,1)}, u32[]{:S(2)}, u32[]{:S(2)}) collective-permute-start(bf16[4,2,32,4608]{3,2,1,0:T(8,128)(2,1)} %copy-done.10), channel_id=1, source_target_pairs={{0,4},{1,5},{2,6},{3,7},{4,0},{5,1},{6,2},{7,3},{8,12},{9,13},{10,... | collective-permute-start | bytes 7077896 | tf_op jit(solution)/shard_map/ppermute | solution.py:376
  334.6 9.4 %copy-start.17 = (bf16[1536,256]{1,0:T(8,128)(2,1)S(1)}, bf16[1536,256]{1,0:T(8,128)(2,1)}, u32[]{:S(2)}) copy-start(bf16[1536,256]{1,0:T(8,128)(2,1)} %copy-done.16) | copy-start | bytes 2359300
  334.6 13.0 %copy-start.15 = (bf16[1536,256]{1,0:T(8,128)(2,1)S(1)}, bf16[1536,256]{1,0:T(8,128)(2,1)}, u32[]{:S(2)}) copy-start(bf16[1536,256]{1,0:T(8,128)(2,1)} %copy-done.14) | copy-start | bytes 2359300
  334.6 14.3 %copy-start.6 = (bf16[3072,256]{1,0:T(8,128)(2,1)S(1)}, bf16[3072,256]{1,0:T(8,128)(2,1)}, u32[]{:S(2)}) copy-start(bf16[3072,256]{1,0:T(8,128)(2,1)} %copy-done.4) | copy-start | bytes 4718596
  334.6 14.3 %copy-start.22 = (bf16[3072,128]{1,0:T(8,128)(2,1)S(1)}, bf16[3072,128]{1,0:T(8,128)(2,1)}, u32[]{:S(2)}) copy-start(bf16[3072,128]{1,0:T(8,128)(2,1)} %copy-done.18) | copy-start | bytes 2359300
  341.9 33.3 %collective-permute-start.15 = (bf16[4,32,4608]{2,1,0:T(8,128)(2,1)S(1)}, bf16[4,32,4608]{2,1,0:T(8,128)(2,1)S(1)}, u32[]{:S(2)}, u32[]{:S(2)}) collective-permute-start(bf16[4,32,4608]{2,1,0:T(8,128)(2,1)S(1)} %get-tuple-element.128), channel_id=1, source_target_pairs={{0,4},{1,5},{2,6},{3,7},{4,0},{5,1},{6,2},{7,3},{8,12},{9,13},{10,... | collective-permute-start | bytes 3538952 | tf_op jit(solution)/shard_map/ppermute | solution.py:376
  343.5 31.8 %collective-permute-start.16 = (bf16[4,32,4608]{2,1,0:T(8,128)(2,1)S(1)}, bf16[4,32,4608]{2,1,0:T(8,128)(2,1)S(1)}, u32[]{:S(2)}, u32[]{:S(2)}) collective-permute-start(bf16[4,32,4608]{2,1,0:T(8,128)(2,1)S(1)} %get-tuple-element.129), channel_id=1, source_target_pairs={{0,2},{1,3},{2,0},{3,1},{4,6},{5,7},{6,4},{7,5},{8,10},{9,11},{10,... | collective-permute-start | bytes 3538952 | tf_op jit(solution)/shard_map/ppermute | solution.py:376
  344.0 31.2 %collective-permute-start.13 = (bf16[1536,256]{1,0:T(8,128)(2,1)S(1)}, bf16[1536,256]{1,0:T(8,128)(2,1)S(1)}, u32[]{:S(2)}, u32[]{:S(2)}) collective-permute-start(bf16[1536,256]{1,0:T(8,128)(2,1)S(1)} %copy-done.17), channel_id=1, source_target_pairs={{0,8},{1,9},{2,10},{3,11},{4,12},{5,13},{6,14},{7,15},{8,16},{9,17... | collective-permute-start | bytes 2359304 | tf_op jit(solution)/shard_map/ppermute | solution.py:368
  347.6 27.6 %collective-permute-start.14 = (bf16[1536,256]{1,0:T(8,128)(2,1)S(1)}, bf16[1536,256]{1,0:T(8,128)(2,1)S(1)}, u32[]{:S(2)}, u32[]{:S(2)}) collective-permute-start(bf16[1536,256]{1,0:T(8,128)(2,1)S(1)} %copy-done.15), channel_id=1, source_target_pairs={{8,0},{9,1},{10,2},{11,3},{12,4},{13,5},{14,6},{15,7},{16,8},{17,9... | collective-permute-start | bytes 2359304 | tf_op jit(solution)/shard_map/ppermute | solution.py:368
  387.6 33.9 %all-to-all-start.3 = ((bf16[8,384,384]{2,1,0:T(8,128)(2,1)}), bf16[8,384,384]{2,1,0:T(8,128)(2,1)}, u32[]{:S(2)}, u32[]{:S(2)}) async-start(bf16[8,384,384]{2,1,0:T(8,128)(2,1)} %bitcast.168), calls=%async_computation.3 | async-start | bytes 4718592 | tf_op jit(solution)/shard_map/all_to_all | solution.py:437
  393.6 20.4 %collective-permute-start.17 = (bf16[32,9216]{1,0:T(8,128)(2,1)S(1)}, bf16[32,9216]{1,0:T(8,128)(2,1)S(1)}, u32[]{:S(2)}, u32[]{:S(2)}) collective-permute-start(bf16[32,9216]{1,0:T(8,128)(2,1)S(1)} %get-tuple-element.170), channel_id=1, source_target_pairs={{0,8},{1,9},{2,10},{3,11},{4,12},{5,13},{6,14},{7,15},{8,16},{9,17... | collective-permute-start | bytes 1769480 | tf_op jit(solution)/shard_map/ppermute | solution.py:535
  401.8 43.9 %collective-permute-start.18 = (bf16[32,9216]{1,0:T(8,128)(2,1)S(1)}, bf16[32,9216]{1,0:T(8,128)(2,1)}, u32[]{:S(2)}, u32[]{:S(2)}) collective-permute-start(bf16[32,9216]{1,0:T(8,128)(2,1)S(1)} %get-tuple-element.169), channel_id=1, source_target_pairs={{0,16},{1,17},{2,18},{3,19},{4,20},{5,21},{6,22},{7,23},{8,24},{9,... | collective-permute-start | bytes 1769480 | tf_op jit(solution)/shard_map/ppermute | solution.py:535
  402.6 43.1 %collective-permute-start.19 = (bf16[32,9216]{1,0:T(8,128)(2,1)S(1)}, bf16[32,9216]{1,0:T(8,128)(2,1)}, u32[]{:S(2)}, u32[]{:S(2)}) collective-permute-start(bf16[32,9216]{1,0:T(8,128)(2,1)S(1)} %get-tuple-element.168), channel_id=1, source_target_pairs={{0,24},{1,25},{2,26},{3,27},{4,28},{5,29},{6,30},{7,31},{8,0},{9,1... | collective-permute-start | bytes 1769480 | tf_op jit(solution)/shard_map/ppermute | solution.py:535
  414.0 7.5 %copy-start.28 = (bf16[32,9216]{1,0:T(8,128)(2,1)}, bf16[32,9216]{1,0:T(8,128)(2,1)S(1)}, u32[]{:S(2)}) copy-start(bf16[32,9216]{1,0:T(8,128)(2,1)S(1)} %collective-permute-done.17) | copy-start | bytes 1769476
  421.5 15.4 %copy-start.3 = (f32[384,1024]{1,0:T(8,128)S(1)}, f32[384,1024]{1,0:T(8,128)}, u32[]{:S(2)}) copy-start(f32[384,1024]{1,0:T(8,128)} %get-tuple-element.146.dy1) | copy-start | bytes 4718596
  428.6 17.1 %collective-permute-start.20 = (bf16[8,32,384]{2,1,0:T(8,128)(2,1)S(1)}, bf16[8,32,384]{2,1,0:T(8,128)(2,1)}, u32[]{:S(2)}, u32[]{:S(2)}) collective-permute-start(bf16[8,32,384]{2,1,0:T(8,128)(2,1)S(1)} %get-tuple-element.179), channel_id=1, source_target_pairs={{0,8},{1,9},{2,10},{3,11},{4,12},{5,13},{6,14},{7,15},{8,16},{9,17... | collective-permute-start | bytes 589832 | tf_op jit(solution)/shard_map/ppermute | solution.py:535
  434.4 29.9 %collective-permute-start.21 = (bf16[8,32,384]{2,1,0:T(8,128)(2,1)S(1)}, bf16[8,32,384]{2,1,0:T(8,128)(2,1)}, u32[]{:S(2)}, u32[]{:S(2)}) collective-permute-start(bf16[8,32,384]{2,1,0:T(8,128)(2,1)S(1)} %get-tuple-element.178), channel_id=1, source_target_pairs={{0,16},{1,17},{2,18},{3,19},{4,20},{5,21},{6,22},{7,23},{8,24},{9,... | collective-permute-start | bytes 589832 | tf_op jit(solution)/shard_map/ppermute | solution.py:535
  435.3 29.1 %collective-permute-start.22 = (bf16[8,32,384]{2,1,0:T(8,128)(2,1)S(1)}, bf16[8,32,384]{2,1,0:T(8,128)(2,1)}, u32[]{:S(2)}, u32[]{:S(2)}) collective-permute-start(bf16[8,32,384]{2,1,0:T(8,128)(2,1)S(1)} %get-tuple-element.177), channel_id=1, source_target_pairs={{0,24},{1,25},{2,26},{3,27},{4,28},{5,29},{6,30},{7,31},{8,0},{9,1... | collective-permute-start | bytes 589832 | tf_op jit(solution)/shard_map/ppermute | solution.py:535
  469.5 16.0 %all-to-all-start.4 = ((f32[32,1,448]{2,1,0:T(1,128)}), f32[32,1,448]{2,1,0:T(1,128)S(1)}, u32[]{:S(2)}, u32[]{:S(2)}) async-start(f32[32,1,448]{2,1,0:T(1,128)} %all_to_all.25), calls=%async_computation.4 | async-start | bytes 131072 | tf_op jit(solution)/shard_map/all_to_all | solution.py:952
  485.4 11.7 %all-to-all-start.5 = ((f32[8,32,384]{2,1,0:T(8,128)}), f32[8,32,384]{2,1,0:T(8,128)S(1)}, u32[]{:S(2)}, u32[]{:S(2)}) async-start(f32[8,32,384]{2,1,0:T(8,128)} %fusion.9), calls=%async_computation.5 | async-start | bytes 786432 | tf_op jit(solution)/shard_map/all_to_all | solution.py:437
  (27 other events, 52.6 us)
Sparse Core Ops, SparseCore 0:
  11.5 112.7 all-gather.3
  127.2 87.9 all-gather.5
  218.6 77.4 all-gather.7

commit v2 on v1

--- a/solution.py
+++ b/solution.py
@@ -185,14 +185,13 @@
 
     @pl.when(step == pl.num_programs(0) - 1)
     def _():
-        mid_ref[:, :width] = mid_ref[:, :width] * SCALE
         for side, out in enumerate((out_left, out_right)):
             out[:, :width] = (dkv[side, :, :width] * SCALE).astype(out.dtype)
             out[:, width:] = dkv[side, :, width:].astype(out.dtype)
 
 
 def backward_mid_kernel(
-    low, high, seg, q_ref, kv_ref, o_ref, do_ref, lse_ref, part_ref, dq_ref, mid_ref, k_t, dq_t, *, edge
+    low, high, seg, q_ref, kv_ref, o_ref, do_ref, lse_ref, part_ref, first_ref, dq_ref, mid_ref, k_t, dq_t, *, edge
 ):
     step = pl.program_id(0)
     width = q_ref.shape[1]
@@ -200,7 +199,7 @@
     @pl.when(step == 0)
     def _():
         transpose_into(k_t, kv_ref, 0)
-        mid_ref[...] = jnp.zeros_like(mid_ref)
+        mid_ref[...] = first_ref[...]
 
     dq_t[...] = part_ref[...]
     blocks = kv_ref.shape[0] // BK
@@ -277,11 +276,11 @@
     )
 
 
-def backward_second(prefetch, seg, q, kv, o, do, lse, part, edge):
+def backward_second(prefetch, seg, q, kv, o, do, lse, part, first, edge):
     span, width = q.shape
     return attention_call(
         functools.partial(backward_mid_kernel, edge=edge), "backward_second", prefetch,
-        [seg, q, kv, o, do, lse, part], "crwrrcc",
+        [seg, q, kv, o, do, lse, part, first], "crwrrccw",
         [shaped(span, width, dtype=jnp.bfloat16), shaped(*kv.shape)], "rw",
         [pltpu.VMEM((width, span), jnp.bfloat16), pltpu.VMEM((width, BQ), jnp.float32)], 3,
     )
@@ -376,32 +375,32 @@
     return lax.ppermute(value, "dev", [(i, i ^ bit) for i in range(devices)])
 
 
-def join_kernel(dq, mid0, mid1, left, right, out):
+def join_kernel(dq, mid, left, right, out):
     width = dq.shape[1]
     step, edge = pl.program_id(0), pl.num_programs(0) // 2
     halo = jnp.where(step < edge, left[...], right[...]).astype(F32)
     out[:, :width] = dq[...]
-    out[:, width:] = (mid0[...] + mid1[...] + halo).astype(out.dtype)
-
-
-def joined_heads(dq, mid0, mid1, left, right):
+    out[:, width:] = (mid[...] + halo).astype(out.dtype)
+
+
+def joined_heads(dq, mid, left, right):
     span, width = dq.shape
-    size = BQ
+    size = 3 * BQ
     half = span // (2 * size)
-    rows = [pl.BlockSpec((size, columns), lambda i: (i, 0)) for columns in (width, 2 * width, 2 * width, 3 * width)]
+    rows = [pl.BlockSpec((size, columns), lambda i: (i, 0)) for columns in (width, 2 * width, 3 * width)]
     return pl.pallas_call(
         join_kernel,
         out_shape=shaped(span, 3 * width, dtype=BF16),
         grid=(span // size,),
-        in_specs=rows[:3]
+        in_specs=rows[:2]
         + [
             pl.BlockSpec((size, 2 * width), lambda i: (jnp.minimum(i, half - 1), 0)),
             pl.BlockSpec((size, 2 * width), lambda i: (jnp.maximum(i - half, 0), 0)),
         ],
-        out_specs=rows[3],
+        out_specs=rows[2],
         cost_estimate=pl.CostEstimate(flops=0, bytes_accessed=10 << 20, transcendentals=0),
         name="joined_heads",
-    )(dq, mid0, mid1, left, right)
+    )(dq, mid, left, right)
 
 
 def tail_kernel(dqkv, weight, dy1, x_ref, gain, grad, sums, heads):
@@ -475,10 +474,12 @@
 
 def plane_qkv(tokens, slab, me, devices):
     rows, width = tokens.shape
-    half, third = width // 2, (slab.shape[1] - 128) // 3
+    half, third = width // 2, (slab.shape[2] - 128) // 3
     a, b = tokens[:, :half], tokens[:, half:]
-    a = jnp.stack([a, swapped(a, 4, devices)])
-    b = jnp.stack([b, swapped(b, 2, devices)])
+    got_a, got_b, slab = lax.optimization_barrier((swapped(a, 4, devices), swapped(b, 2, devices), slab))
+    slab = lax.all_to_all(slab, "dev", 0, 0, tiled=True).reshape(width, -1)
+    packed = slab[:, -128:]
+    a, b = jnp.stack([a, got_a]), jnp.stack([b, got_b])
     a = jnp.stack([a, swapped(a, 2, devices)])
     b = jnp.stack([b, swapped(b, 4, devices)])
     a, b, slab = lax.optimization_barrier((a, b, slab))
@@ -499,7 +500,7 @@
 
     piece = (1, 1, rows, half)
     span = GROUP * rows
-    return pl.pallas_call(
+    out = pl.pallas_call(
         functools.partial(qkv_kernel, rows=width // devices),
         out_shape=(
             jax.ShapeDtypeStruct((span, width), BF16),
@@ -525,15 +526,19 @@
     )(
         jnp.stack([*position(me), me % GROUP]).astype(jnp.int32), a, far_a, b, far_b, slab,
     )
-
-
-def from_planes(stack, me, devices):
+    return (*out, packed)
+
+
+def plane_pieces(stack, me, devices):
     planes, mine = devices // GROUP, me // GROUP
-    got = []
-    for k in range(1, planes):
-        piece = take(stack, (mine + k) % planes, 0)
-        got.append(lax.ppermute(piece, "dev", [(i, (i + k * GROUP) % devices) for i in range(devices)]))
-    return take(stack, mine, 0), got
+    return take(stack, mine, 0), [take(stack, (mine + k) % planes, 0) for k in range(1, planes)]
+
+
+def send_planes(pieces, devices):
+    return [
+        lax.ppermute(piece, "dev", [(i, (i + (k + 1) * GROUP) % devices) for i in range(devices)])
+        for k, piece in enumerate(pieces)
+    ]
 
 
 def total_of(own, others):
@@ -580,7 +585,9 @@
         dn2_ref[...] = jnp.zeros_like(dn2_ref)
         n2_t[0], n2_t[1] = by_parity(turned(n2_ref[...]), bits[2], rows)
 
-    n2, dml, f1, f2 = n2_ref[...], dml_ref[...], f1_ref[...], f2_ref[...]
+    n2, dml = n2_ref[...], dml_ref[...]
+    f1 = f1_ref[...].reshape(n2.shape[1], -1)
+    f2 = f2_ref[...].reshape(-1, n2.shape[1])
     act, slope = gelu_parts(mm(n2, f1) + bias[...])
     act = act.astype(BF16)
     mlp_ref[...] += mm(act, f2)
@@ -598,7 +605,7 @@
             out[:, :, i * width : (i + 1) * width] = grad[:, i]
 
 
-def mlp_all(n2, dml, big, fc2, bias, me, shard_rows):
+def mlp_all(n2, dml, big, bias, me, shard_rows):
     tokens, width = n2.shape
     hidden, owners = bias.shape[0], width // shard_rows
     size = width // 2
@@ -618,8 +625,8 @@
             in_specs=[
                 whole,
                 whole,
-                pl.BlockSpec((width, size), lambda s, bits: (0, s)),
-                pl.BlockSpec((size, width), lambda s, bits: (s, 0)),
+                pl.BlockSpec((owners, shard_rows, size), lambda s, bits: (0, s // 2, s % 2)),
+                pl.BlockSpec((owners // steps, hidden // owners, width), lambda s, bits: (s, 1, 0)),
                 line,
             ],
             out_specs=[whole, whole, line, first, first, second, second],
@@ -630,7 +637,7 @@
             flops=4 * tokens * width * hidden, bytes_accessed=8 * width * hidden, transcendentals=2 * tokens * hidden
         ),
         name="mlp_all",
-    )(jnp.stack(position(me)).astype(jnp.int32), n2, dml, big, fc2, bias[None])
+    )(jnp.stack(position(me)).astype(jnp.int32), n2, dml, big, big, bias[None])
 
 
 def grad_kernel(bits, a_ref, b_ref, keep_ref, send_ref):
@@ -667,7 +674,8 @@
     for i, total in enumerate(totals):
         sums[i : i + 1, :] = jnp.sum(total, axis=0, keepdims=True)
     dbl = db.astype(BF16)
-    do = lax.dot_general(dbl, w_proj[...], NT, preferred_element_type=F32).astype(BF16)
+    weight = w_proj[...].reshape(dbl.shape[1], -1)
+    do = lax.dot_general(dbl, weight, NT, preferred_element_type=F32).astype(BF16)
     columns = do_ref.shape[2]
     for j in range(do_ref.shape[0]):
         do_ref[j] = do[:, j * columns : (j + 1) * columns]
@@ -683,7 +691,7 @@
         shaped(tokens, width, dtype=BF16), shaped(tokens, width), shaped(8, width),
         shaped(GROUP, tokens, width // GROUP, dtype=BF16), grads, grads,
     )
-    last = big.shape[1] // width - 1
+    last = big.shape[1] // shard_rows - 1
     return pl.pallas_call(
         after_mlp_kernel,
         out_shape=outs,
@@ -691,7 +699,7 @@
             num_scalar_prefetch=1,
             grid=(1,),
             in_specs=[whole_spec(a) for a in (mlp, dn2, x, branch, g, o)]
-            + [pl.BlockSpec((width, width), lambda i, *_: (0, last)), whole_spec(vec)],
+            + [pl.BlockSpec((owners, shard_rows, width), lambda i, *_: (0, last, 0)), whole_spec(vec)],
             out_specs=[whole_spec(a) for a in outs],
         ),
         compiler_params=pltpu.CompilerParams(vmem_limit_bytes=52 << 20),
@@ -820,14 +828,13 @@
     packed = jnp.broadcast_to(pack_columns(vectors, shard_rows), (GROUP, shard_rows, 128))
     slab = jnp.concatenate([slab, packed], axis=2)
     slab = jnp.broadcast_to(slab[None], (devices // GROUP, *slab.shape)).reshape(devices, shard_rows, -1)
-    slab = lax.all_to_all(slab, "dev", 0, 0, tiled=True).reshape(width, -1)
-    packed = slab[:, -128:]
+    n1, q, kv, packed = plane_qkv(tokens, slab, me, devices)
     spread = unpack_columns(packed.astype(F32), sizes, shard_rows)
     gain1, shift1, bias_qv, bias_proj, layer_attn, gain2, shift2, bias_fc1, bias_fc2, layer_mlp = spread
     if by_axes:
-        big = gathered(jnp.concatenate([fc1_weight, proj_weight], axis=1))
-        w_fc2 = gathered(fc2_weight)
-        w_proj = big[:, hidden:]
+        first = fc1_weight.reshape(shard_rows, blocks, width).transpose(1, 0, 2).reshape(-1, width)
+        big = gathered(jnp.concatenate([first, fc2_weight, proj_weight])).reshape(devices, -1, width)
+        w_proj = big[:, 2 * blocks * shard_rows :].reshape(width, width)
     else:
         w_proj, big = gathered(proj_weight), gathered(fc1_weight)
         w_fc2 = gathered(fc2_weight)
@@ -849,7 +856,6 @@
 
     x = tokens.astype(F32)
     u1, rstd1 = normalised(x)
-    n1, q, kv = plane_qkv(tokens, slab, me, devices)
     prefetch, edge_blocks = (low, high), halo // BK
     left = shifted(kv[span - halo :], GROUP, devices)
     right = shifted(kv[:halo], -GROUP, devices)
@@ -867,7 +873,7 @@
     d_fc2_bias = jnp.sum(dm, axis=0)
     dml = dm.astype(BF16)
     if by_axes:
-        mlp, dn2, d_fc1_bias, keep1, send1, keep2, send2 = mlp_all(n2, dml, big, w_fc2, bias_fc1, me, shard_rows)
+        mlp, dn2, d_fc1_bias, keep1, send1, keep2, send2 = mlp_all(n2, dml, big, bias_fc1, me, shard_rows)
         d_fc1_bias = d_fc1_bias.reshape(-1)
     else:
         act, slope = gelu_parts(mm(n2, big) + bias_fc1)
@@ -906,7 +912,6 @@
 
     do_heads = in_plane(do, devices).reshape(span, -1)
     if by_axes:
-        do_heads, out_a, out_b = lax.optimization_barrier((do_heads, out_a, out_b))
         in_a, in_b = swapped(out_a, 2, devices), swapped(out_b, 4, devices)
     part_dq, mid0, out_left, out_right = backward_first(prefetch, seg, q, kv, left, right, o_heads, do_heads, lse)
     if by_axes:
@@ -916,26 +921,29 @@
         in_a, in_b = swapped(out_a, 4, devices), swapped(out_b, 2, devices)
     from_right = shifted(out_left, -GROUP, devices)
     from_left = shifted(out_right, GROUP, devices)
-    dq, mid1 = backward_second(prefetch, seg, q, kv, o_heads, do_heads, lse, part_dq, edge_blocks)
-    dq, mid1, from_left, from_right = lax.optimization_barrier((dq, mid1, from_left, from_right))
+    dq, mid = backward_second(prefetch, seg, q, kv, o_heads, do_heads, lse, part_dq, mid0, edge_blocks)
+    dq, mid, from_left, from_right = lax.optimization_barrier((dq, mid, from_left, from_right))
     if by_axes:
         dq, in_a, in_b = lax.optimization_barrier((dq, in_a, in_b))
-    d_heads = joined_heads(dq, mid0, mid1, from_left, from_right)
     if by_axes:
         third = [(s.astype(F32) + i.astype(F32)).astype(BF16) for s, i in ((sum_a, in_a), (sum_b, in_b))]
-        d_heads, third = lax.optimization_barrier((d_heads, jnp.concatenate(third, axis=-1)))
-        own_sums, sums = from_planes(third, me, devices)
+        own_sums, pieces = plane_pieces(jnp.concatenate(third, axis=-1), me, devices)
+        dq, pieces = lax.optimization_barrier((dq, pieces))
+        sums = send_planes(pieces, devices)
+    d_heads = joined_heads(dq, mid, from_left, from_right)
     dqkv = in_plane(d_heads.reshape(GROUP, rows, -1), devices)
     if by_axes:
-        dqkv, n1, sums[0] = lax.optimization_barrier((dqkv, n1, sums[0]))
+        dqkv, n1 = lax.optimization_barrier((dqkv, n1))
     d_qkv = t_mm(n1, d_heads).astype(BF16).reshape(devices // GROUP, GROUP, shard_rows, -1)
-    dqkv, d_qkv = lax.optimization_barrier((dqkv, d_qkv))
-    own_qkv, got_qkv = from_planes(d_qkv, me, devices)
+    if by_axes:
+        dqkv, d_qkv, sums = lax.optimization_barrier((dqkv, d_qkv, sums))
+    own_qkv, pieces = plane_pieces(d_qkv, me, devices)
+    got_qkv = send_planes(pieces, devices)
     grad_tokens, totals, per_head = input_gradient(dqkv, w_qkv, dy1, tokens, gain1)
     d_gain1, d_shift1, half = totals[0], totals[1], width // GROUP
     d_qv_bias = jnp.concatenate([per_head[:, :half].reshape(-1), per_head[:, 2 * half :].reshape(-1)])
     if by_axes:
-        d_gain1, sums[1:], got_qkv = lax.optimization_barrier((d_gain1, sums[1:], got_qkv))
+        d_gain1, got_qkv = lax.optimization_barrier((d_gain1, got_qkv))
     d_qkv = in_plane(total_of(own_qkv, got_qkv), devices).reshape(GROUP, shard_rows, 3, -1)
     d_qkv = d_qkv.transpose(1, 2, 0, 3).reshape(shard_rows, 3 * width)
     if by_axes:

time: 507 us -> 525 us (1.036)
  blocking collectives: 0 us -> 61 us
  waiting for transfers between devices: 176 us -> 119 us
  Pallas kernels: 185 us -> 193 us
    all_to_all x0 -> x1, blocking collectives: none -> 61 us  [in_plane(): lax.all_to_all(stack, 'dev', 0, 0, axis_index_groups=groups_of(devices),...]
    all_gather x3 -> x2, waiting for transfers between devices: 39.5 us -> 0.02 us  [gathered(): return lax.all_gather(shard, 'dev', axis=0, tiled=True)]
    ppermute x6, waiting for transfers between devices: 28.5 us -> 11.2 us  [send_planes(): lax.ppermute(piece, 'dev', [(i, (i + (k + 1) * GROUP) % devices) for i in...]
    ppermute x4, waiting for transfers between devices: 0.01 us -> 15.1 us  [shifted(): return lax.ppermute(shard, 'dev', pairs)]
    ppermute x13, waiting for transfers between devices: 62.5 us -> 51.7 us  [swapped(): return lax.ppermute(value, 'dev', [(i, i ^ bit) for i in range(devices)])]
    pallas_call x4, Pallas kernels: 105 us -> 115 us  [attention_call(): pl.pallas_call(kernel, out_shape=tuple(outputs), grid_spec=pltpu.Prefetch...]
    all_to_all x1, waiting for transfers between devices: 17.3 us -> 8.7 us  [to_tokens(): lax.all_to_all(sent, 'dev', 0, 0, axis_index_groups=groups_of(devices), t...]
    ppermute x6, starting transfers between devices: 16.5 us -> 23.1 us  [send_planes(): lax.ppermute(piece, 'dev', [(i, (i + (k + 1) * GROUP) % devices) for i in...]
  transfers between devices with their start and end apart: 32 -> 30, of which waited for: 13 -> 13; matrix products, arithmetic and copies ran while one was open for 6% -> 7% of each run, Pallas kernels for 33% -> 35%
where the time goes in v2:
time: 525 us; the launch traced here: 522 us
  Pallas kernels  193 us (37%)
  waiting for transfers between devices  119 us (23%)
  starting transfers between devices  70.8 us (13%)
  blocking collectives  61 us (12%)
  local copies, waits for them, and re-layouts  39.9 us (8%)
  between operations  14.9 us (3%)
  other arithmetic  12.9 us (2%)
  matrix products  10.9 us (2%)
    pallas_call x4, Pallas kernels, attention_call(): pl.pallas_call(kernel, out_shape=tuple(outputs), grid_spec=pltpu.Prefetch...  115 us
    all_to_all x1, blocking collectives, in_plane(): lax.all_to_all(stack, 'dev', 0, 0, axis_index_groups=groups_of(devices),...  61 us
    ppermute x13, waiting for transfers between devices, swapped(): return lax.ppermute(value, 'dev', [(i, i ^ bit) for i in range(devices)])  51.7 us
    pallas_call x1, Pallas kernels, mlp_all(): pl.pallas_call(mlp_kernel, out_shape=(total, total, jax.ShapeDtypeStruct(...  29.6 us
    all_to_all x2, waiting for transfers between devices, in_plane(): lax.all_to_all(stack, 'dev', 0, 0, axis_index_groups=groups_of(devices),...  26.7 us
    ppermute x6, starting transfers between devices, send_planes(): lax.ppermute(piece, 'dev', [(i, (i + (k + 1) * GROUP) % devices) for i in...  23.1 us
    unnamed x100, local copies, waits for them, and re-layouts  16 us
    pallas_call x2, Pallas kernels, added(): pl.pallas_call(functools.partial(add_kernel, terms=terms), out_shape=tupl...  15.4 us
  transfers between devices with their start and end apart: 30, of which 13 were waited for; matrix products, arithmetic and copies ran while one was open for 7% of the time, Pallas kernels for 35%

profile of v2, /device:TPU:0, one launch (start us, length us, event | category | flops | bytes accessed | tf_op | source)
XLA Modules:
  0.0 522.5 jit_solution(8931355694200335558)
XLA Ops:
  8.3 1.9 pad_maximum_fusion.4
  11.2 3.0 collective-permute-start
  14.2 1.5 collective-permute-start.1
  17.1 6.3 %collective-permute-done = bf16[384,512]{1,0:T(8,128)(2,1)S(1)} collective-permute-done((bf16[384,512]{1,0:T(8,128)(2,1)}, bf16[384,512]{1,0:T(8,128)(2,1)S(1)}, u32[]{:S(2)}, u32[]{:S(2)}) %collective-permute-start) | collective-permute-done | bytes 393248 | tf_op jit(solution)/shard_map/ppermute | solution.py:375
  23.5 1.9 collective-permute-done.1
  26.5 6.0 %all-to-all-start = ((bf16[32,32,512]{2,1,0:T(8,128)(2,1)}), bf16[32,32,512]{2,1,0:T(8,128)(2,1)S(1)}, u32[]{:S(2)}, u32[]{:S(2)}) async-start(bf16[32,32,512]{2,1,0:T(8,128)(2,1)} %bitcast.14), calls=%async_computation | async-start | bytes 2097152 | tf_op jit(solution)/shard_map/all_to_all | solution.py:480
  32.6 1.8 collective-permute-start.3
  34.6 1.5 collective-permute-start.2
  36.1 35.7 %collective-permute-done.3 = bf16[2,384,512]{2,1,0:T(8,128)(2,1)S(1)} collective-permute-done((bf16[2,384,512]{2,1,0:T(8,128)(2,1)S(1)}, bf16[2,384,512]{2,1,0:T(8,128)(2,1)S(1)}, u32[]{:S(2)}, u32[]{:S(2)}) %collective-permute-start.3) | collective-permute-done | bytes 786464 | tf_op jit(solution)/shard_map/ppermute | solution.py:375
  75.1 1.7 copy.93
  76.8 1.8 reshape.237
  82.0 11.2 %plane_qkv.1 = (bf16[3072,1024]{1,0:T(8,128)(2,1)}, bf16[3072,128]{1,0:T(8,128)(2,1)S(1)}, bf16[3072,256]{1,0:T(8,128)(2,1)S(1)}) custom-call(s32[4]{0:T(128)S(1)} %pad_add_fusion.2.bits, bf16[2,2,384,512]{3,2,1,0:T(8,128)(2,1)S(1)} %copy-done.8, bf16[2,2,384,512]{3,2,1,0:T(8,128)(2,1)} %collective-permute-done.4.far_a, ...), custom_call_target="tpu_custom_call" | custom-call | flops 5368709120 | bytes 16777216 | tf_op jit(solution)/shard_map/plane_qkv/pallas_call | solution.py:503
  95.1 3.1 collective-permute-start.6
  102.3 37.5 %forward_mid.1 = (f32[128,3072]{1,0:T(8,128)S(1)}, f32[8,3072]{1,0:T(8,128)S(1)}) custom-call(s32[12]{0:T(128)S(1)} %get-tuple-element.213.low, s32[12]{0:T(128)S(1)} %get-tuple-element.214.high, s32[2,3072]{1,0:T(2,128)S(1)} %pad_add_fusion.seg, bf16[3072,128]{1,0:T(8,128)(2,1)S(1)} %copy-done.19, bf16[3072,256]{1,0:T(8,128)(2,1)S(1)} %copy-done.6), custom_call_target="tpu_custom_call" | custom-call | flops 3221225472 | bytes 8388608 | tf_op jit(solution)/shard_map/forward_mid/pallas_call | solution.py:230
  139.8 15.1 %collective-permute-done.7.right_ref = bf16[1536,256]{1,0:T(8,128)(2,1)} collective-permute-done((bf16[1536,256]{1,0:T(8,128)(2,1)}, bf16[1536,256]{1,0:T(8,128)(2,1)}, u32[]{:S(2)}, u32[]{:S(2)}) %collective-permute-start.7) | collective-permute-done | bytes 786464 | tf_op jit(solution)/shard_map/ppermute | solution.py:367
  154.9 10.9 %forward_edge.1 = (bf16[3072,128]{1,0:T(8,128)(2,1)}, f32[8,3072]{1,0:T(8,128)S(1)}) custom-call(s32[12]{0:T(128)S(1)} %get-tuple-element.213.low, s32[12]{0:T(128)S(1)} %get-tuple-element.214.high, s32[2,3072]{1,0:T(2,128)S(1)} %pad_add_fusion.seg, bf16[3072,128]{1,0:T(8,128)(2,1)S(1)} %copy-done.20, bf16[1536,256]{1,0:T(8,128)(2,1)S(1)} %collective-permute-done.6.left_ref, ...), custom_call_target="tpu_custom_call" | custom-call | flops 3221225472 | bytes 8388608 | tf_op jit(solution)/shard_map/forward_edge/pallas_call | solution.py:230
  165.8 4.6 all-to-all-start.1
  170.9 3.2 slice.169
  174.1 8.7 %all-to-all-done.1 = bf16[8,384,1,128]{3,1,2,0:T(8,128)(2,1)} async-done(((bf16[8,384,1,128]{3,1,2,0:T(8,128)(2,1)}), bf16[8,384,1,128]{3,1,2,0:T(8,128)(2,1)}, u32[]{:S(2)}, u32[]{:S(2)}) %all-to-all-start.1) | async-done | bytes 786464 | tf_op jit(solution)/shard_map/all_to_all | solution.py:361
  182.8 3.0 fusion.10
  187.0 29.6 %mlp_all.1 = (f32[384,1024]{1,0:T(8,128)}, f32[384,1024]{1,0:T(8,128)}, f32[1,4096]{1,0:T(1,128)S(1)}, bf16[16,32,4096]{2,1,0:T(8,128)(2,1)}, bf16[16,32,4096]{2...) custom-call(s32[3]{0:T(128)S(1)} %pad_add_fusion.1.bits, ...), custom_call_target="tpu_custom_call" | custom-call | flops 6442450944 | bytes 33554432 | tf_op jit(solution)/shard_map/mlp_all/pallas_call | solution.py:619
  217.1 2.2 copy_bitcast_fusion.o_ref
  219.3 9.0 %after_mlp.1 = (bf16[384,1024]{1,0:T(8,128)(2,1)}, f32[384,1024]{1,0:T(8,128)}, f32[8,1024]{1,0:T(8,128)S(1)}, bf16[8,384,128]{2,1,0:T(8,128)(2,1)S(1)}, bf16[16...) custom-call(s32[3]{0:T(128)S(1)} %pad_add_fusion.1.bits, f32[384,1024]{1,0:T(8,128)} %get-tuple-element.105.mlp, ...), custom_call_target="tpu_custom_call" | custom-call | flops 1610612736 | bytes 20971520 | tf_op jit(solution)/shard_map/after_mlp/pallas_call | solution.py:695
  228.4 5.3 %collective-permute-done.9 = bf16[16,32,1024]{2,1,0:T(8,128)(2,1)S(1)} collective-permute-done((bf16[16,32,1024]{2,1,0:T(8,128)(2,1)}, bf16[16,32,1024]{2,1,0:T(8,128)(2,1)S(1)}, u32[]{:S(2)}, u32[]{:S(2)}) %collective-permute-start.9) | collective-permute-done | bytes 1048608 | tf_op jit(solution)/shard_map/ppermute | solution.py:375
  235.0 7.8 %first_sends.1 = (bf16[4,2,32,4608]{3,2,1,0:T(8,128)(2,1)}, bf16[4,2,32,4608]{3,2,1,0:T(8,128)(2,1)}) custom-call(s32[3]{0:T(128)S(1)} %pad_add_fusion.1.bits, bf16[4,2,2,32,4096]{4,3,2,1,0:T(8,128)(2,1)S(1)} %bitcast.173, bf16[4,2,2,32,4096]{4,3,2,1,0:T(8,128)(2,1)} %bitcast.48.refs_1_.refs_7_, bf16[4,2,2,32,1024]{4,3,2,1,0:T(8,128)(2,1)S(1)} %bitcast.159, ...), custom_call_target="tpu_custom_call" | custom-call | bytes 16777216 | tf_op jit(solution)/shard_map/first_sends/pallas_call | solution.py:732
  244.0 61.0 %all_to_all.34 = bf16[8,384,128]{2,1,0:T(8,128)(2,1)S(1)} all-to-all(bf16[8,384,128]{2,1,0:T(8,128)(2,1)S(1)} %get-tuple-element.108), channel_id=1, replica_groups={{0,1,2,3,4,5,6,7},{8,9,10,11,12,13,14,15},{16,17,18,19,20,21,22,23},{24..., dimensions={0} | all-to-all | bytes 1572864 | tf_op jit(solution)/shard_map/all_to_all | solution.py:436
  305.0 35.9 %backward_first.1 = (f32[128,3072]{1,0:T(8,128)}, f32[3072,256]{1,0:T(8,128)}, bf16[1536,256]{1,0:T(8,128)(2,1)}, bf16[1536,256]{1,0:T(8,128)(2,1)}) custom-call(s32[12]{0:T(128)S(1)} %get-tuple-element.213.low, s32[12]{0:T(128)S(1)} %get-tuple-element.214.high, s32[2,3072]{1,0:T(2,128)S(1)} %pad_add_fusion.seg, bf16[3072,128]{1,0:T(8,128)(2,1)S(1)} %copy-done.21, ...), custom_call_target="tpu_custom_call" | custom-call | flops 3221225472 | bytes 8388608 | tf_op jit(solution)/shard_map/backward_first/pallas_call | solution.py:230
  341.8 7.6 %second_sums.1 = (bf16[4,32,4608]{2,1,0:T(8,128)(2,1)}, bf16[4,32,4608]{2,1,0:T(8,128)(2,1)S(1)}, bf16[4,32,4608]{2,1,0:T(8,128)(2,1)}, bf16[4,32,4608]{2,1,0:T(8,128)(2,1)S(1)}) custom-call(s32[3]{0:T(128)S(1)} %pad_add_fusion.1.bits, bf16[4,2,2,32,4096]{4,3,2,1,0:T(8,128)(2,1)} %bitcast.171, bf16[4,2,2,32,4096]{4,3,2,1,0:T(8,128)(2,1)} %bitcast.48.refs_1_.refs_7_, ...), custom_call_target="tpu_custom_call" | custom-call | bytes 16777216 | tf_op jit(solution)/shard_map/second_sums/pallas_call | solution.py:732
  353.7 4.2 collective-permute-start.13
  363.0 30.4 %backward_second.1 = (bf16[3072,128]{1,0:T(8,128)(2,1)S(1)}, f32[3072,256]{1,0:T(8,128)}) custom-call(s32[12]{0:T(128)S(1)} %get-tuple-element.213.low, s32[12]{0:T(128)S(1)} %get-tuple-element.214.high, s32[2,3072]{1,0:T(2,128)S(1)} %pad_add_fusion.seg, bf16[3072,128]{1,0:T(8,128)(2,1)S(1)} %copy-done.22, bf16[3072,256]{1,0:T(8,128)(2,1)S(1)} %copy-done.7, ...), custom_call_target="tpu_custom_call" | custom-call | flops 3221225472 | bytes 8388608 | tf_op jit(solution)/shard_map/backward_second/pallas_call | solution.py:230
  394.6 1.7 add_convert_fusion
  398.2 4.6 joined_heads.1
  402.8 4.5 all-to-all-start.3
  409.7 4.0 collective-permute-start.17
  413.7 2.9 collective-permute-start.19
  416.6 20.2 %all-to-all-done.3.dqkv = bf16[8,384,384]{2,1,0:T(8,128)(2,1)} async-done(((bf16[8,384,384]{2,1,0:T(8,128)(2,1)}), bf16[8,384,384]{2,1,0:T(8,128)(2,1)}, u32[]{:S(2)}, u32[]{:S(2)}) %all-to-all-start.3) | async-done | bytes 2359328 | tf_op jit(solution)/shard_map/all_to_all | solution.py:436
  436.8 7.9 %convolution_convert_fusion = bf16[1024,384]{1,0:T(8,128)(2,1)} fusion(bf16[3072,1024]{1,0:T(8,128)(2,1)} %get-tuple-element.144, bf16[3072,384]{1,0:T(8,128)(2,1)} %joined_heads.1), kind=kOutput, calls=%fused_computation.17 | convolution fusion | flops 2416312320 | bytes 9437184 | tf_op jit(solution)/shard_map/td,tf->df/dot_general | solution.py:305
  444.7 8.1 %collective-permute-done.18 = bf16[32,9216]{1,0:T(8,128)(2,1)} collective-permute-done((bf16[32,9216]{1,0:T(8,128)(2,1)S(1)}, bf16[32,9216]{1,0:T(8,128)(2,1)}, u32[]{:S(2)}, u32[]{:S(2)}) %collective-permute-start.18) | collective-permute-done | bytes 589856 | tf_op jit(solution)/shard_map/ppermute | solution.py:539
  452.8 1.7 fusion.1
  458.6 13.2 %collective-permute-start.20 = (bf16[8,32,384]{2,1,0:T(8,128)(2,1)S(1)}, bf16[8,32,384]{2,1,0:T(8,128)(2,1)S(1)}, u32[]{:S(2)}, u32[]{:S(2)}) collective-permute-start(bf16[8,32,384]{2,1,0:T(8,128)(2,1)S(1)} %get-tuple-element.183), channel_id=1, source_target_pairs={{0,8},{1,9},{2,10},{3,11},{4,12},{5,13},{6,14},{7,15},{8,16},{9,17... | collective-permute-start | bytes 589832 | tf_op jit(solution)/shard_map/ppermute | solution.py:539
  471.8 3.0 collective-permute-start.21
  474.9 8.5 %input_gradient.1 = (bf16[384,1024]{1,0:T(8,128)(2,1)}, f32[8,1024]{1,0:T(8,128)S(1)}, f32[8,384]{1,0:T(8,128)S(1)}) custom-call(bf16[8,384,384]{2,1,0:T(8,128)(2,1)} %all-to-all-done.3.dqkv, bf16[1024,3072]{1,0:T(8,128)(2,1)} %all-gather.5.cloned.1.call-done.weight, f32[384,1024]{1,0:T(8,128)S(1)} %copy-done.4, bf16[384,1024]{1,0:T(8,128)(2,1)S(1)} %copy-done.3, ...), custom_call_target="tpu_custom_call" | custom-call | flops 2415919104 | bytes 12582912 | tf_op jit(solution)/shard_map/input_gradient/pallas_call | solution.py:423
  484.4 3.2 collective-permute-done.21
  488.4 6.9 %all-to-all-start.4 = ((f32[32,1,448]{2,1,0:T(1,128)}), f32[32,1,448]{2,1,0:T(1,128)S(1)}, u32[]{:S(2)}, u32[]{:S(2)}) async-start(f32[32,1,448]{2,1,0:T(1,128)} %all_to_all.25), calls=%async_computation.4 | async-start | bytes 131072 | tf_op jit(solution)/shard_map/all_to_all | solution.py:960
  495.3 2.0 fusion.12
  497.2 5.4 %all-to-all-done.4 = f32[32,1,448]{2,1,0:T(1,128)S(1)} async-done(((f32[32,1,448]{2,1,0:T(1,128)}), f32[32,1,448]{2,1,0:T(1,128)S(1)}, u32[]{:S(2)}, u32[]{:S(2)}) %all-to-all-start.4) | async-done | bytes 57376 | tf_op jit(solution)/shard_map/all_to_all | solution.py:960
  502.7 3.5 all-to-all-start.5
  507.9 6.5 %all-to-all-done.5 = f32[8,32,384]{2,1,0:T(8,128)S(1)} async-done(((f32[8,32,384]{2,1,0:T(8,128)}), f32[8,32,384]{2,1,0:T(8,128)S(1)}, u32[]{:S(2)}, u32[]{:S(2)}) %all-to-all-start.5) | async-done | bytes 393248 | tf_op jit(solution)/shard_map/all_to_all | solution.py:436
  (207 shorter events, 46.2 us)
Async XLA Ops:
  7.2 163.7 %all-gather.3.cloned.1.call-start = ((), (), s32[]{:S(2)}) async-start(), calls=%async_computation.6 | async-start | bytes 19464192 | tf_op jit(solution)/shard_map/all_gather | solution.py:331
  10.2 6.6 %copy-start.37 = (bf16[32]{0:T(256)(128)(2,1)S(1)}, bf16[32]{0:T(256)(128)(2,1)}, u32[]{:S(2)}) copy-start(bf16[32]{0:T(256)(128)(2,1)} %param.20) | copy-start | bytes 196
  10.2 6.6 %copy-start.38 = (bf16[32]{0:T(256)(128)(2,1)S(1)}, bf16[32]{0:T(256)(128)(2,1)}, u32[]{:S(2)}) copy-start(bf16[32]{0:T(256)(128)(2,1)} %param.21) | copy-start | bytes 196
  10.2 6.6 %copy-start.39 = (bf16[32]{0:T(256)(128)(2,1)S(1)}, bf16[32]{0:T(256)(128)(2,1)}, u32[]{:S(2)}) copy-start(bf16[32]{0:T(256)(128)(2,1)} %param.25) | copy-start | bytes 196
  10.3 6.6 %copy-start.40 = (bf16[32]{0:T(256)(128)(2,1)S(1)}, bf16[32]{0:T(256)(128)(2,1)}, u32[]{:S(2)}) copy-start(bf16[32]{0:T(256)(128)(2,1)} %param.26) | copy-start | bytes 196
  11.2 12.3 %collective-permute-start = (bf16[384,512]{1,0:T(8,128)(2,1)}, bf16[384,512]{1,0:T(8,128)(2,1)S(1)}, u32[]{:S(2)}, u32[]{:S(2)}) collective-permute-start(bf16[384,512]{1,0:T(8,128)(2,1)} %get-tuple-element.189), channel_id=1, source_target_pairs={{0,4},{1,5},{2,6},{3,7},{4,0},{5,1},{6,2},{7,3},{8,12},{9,13},{10,... | collective-permute-start | bytes 1179656 | tf_op jit(solution)/shard_map/ppermute | solution.py:375
  14.2 11.3 %collective-permute-start.1 = (bf16[384,512]{1,0:T(8,128)(2,1)S(1)}, bf16[384,512]{1,0:T(8,128)(2,1)S(1)}, u32[]{:S(2)}, u32[]{:S(2)}) collective-permute-start(bf16[384,512]{1,0:T(8,128)(2,1)S(1)} %get-tuple-element.188), channel_id=1, source_target_pairs={{0,2},{1,3},{2,0},{3,1},{4,6},{5,7},{6,4},{7,5},{8,10},{9,11},{10,... | collective-permute-start | bytes 1179656 | tf_op jit(solution)/shard_map/ppermute | solution.py:375
  26.5 48.0 %all-to-all-start = ((bf16[32,32,512]{2,1,0:T(8,128)(2,1)}), bf16[32,32,512]{2,1,0:T(8,128)(2,1)S(1)}, u32[]{:S(2)}, u32[]{:S(2)}) async-start(bf16[32,32,512]{2,1,0:T(8,128)(2,1)} %bitcast.14), calls=%async_computation | async-start | bytes 2097152 | tf_op jit(solution)/shard_map/all_to_all | solution.py:480
  32.5 309.3 %all-gather.5.cloned.1.call-start = ((), (), s32[]{:S(2)}) async-start(), calls=%async_computation.7 | async-start | bytes 6488064 | tf_op jit(solution)/shard_map/all_gather | solution.py:331
  32.6 39.2 %collective-permute-start.3 = (bf16[2,384,512]{2,1,0:T(8,128)(2,1)S(1)}, bf16[2,384,512]{2,1,0:T(8,128)(2,1)S(1)}, u32[]{:S(2)}, u32[]{:S(2)}) collective-permute-start(bf16[2,384,512]{2,1,0:T(8,128)(2,1)S(1)} %get-tuple-element.185), channel_id=1, source_target_pairs={{0,4},{1,5},{2,6},{3,7},{4,0},{5,1},{6,2},{7,3},{8,12},{9,13},{10,... | collective-permute-start | bytes 2359304 | tf_op jit(solution)/shard_map/ppermute | solution.py:375
  34.6 38.7 %collective-permute-start.2 = (bf16[2,384,512]{2,1,0:T(8,128)(2,1)S(1)}, bf16[2,384,512]{2,1,0:T(8,128)(2,1)S(1)}, u32[]{:S(2)}, u32[]{:S(2)}) collective-permute-start(bf16[2,384,512]{2,1,0:T(8,128)(2,1)S(1)} %get-tuple-element.191), channel_id=1, source_target_pairs={{0,2},{1,3},{2,0},{3,1},{4,6},{5,7},{6,4},{7,5},{8,10},{9,11},{10,... | collective-permute-start | bytes 2359304 | tf_op jit(solution)/shard_map/ppermute | solution.py:375
  74.6 6.0 %collective-permute-start.4 = (bf16[2,2,384,512]{3,2,1,0:T(8,128)(2,1)}, bf16[2,2,384,512]{3,2,1,0:T(8,128)(2,1)}, u32[]{:S(2)}, u32[]{:S(2)}) collective-permute-start(bf16[2,2,384,512]{3,2,1,0:T(8,128)(2,1)} %pad_maximum_fusion.near_a), channel_id=1, source_target_pairs={{0,1},{1,0},{2,3},{3,2},{4,5},{5,4},{6,7},{7,6},{8,9},{9,8},{10,11... | collective-permute-start | bytes 4718600 | tf_op jit(solution)/shard_map/ppermute | solution.py:375
  74.6 6.0 %collective-permute-start.5 = (bf16[2,2,384,512]{3,2,1,0:T(8,128)(2,1)S(1)}, bf16[2,2,384,512]{3,2,1,0:T(8,128)(2,1)}, u32[]{:S(2)}, u32[]{:S(2)}) collective-permute-start(bf16[2,2,384,512]{3,2,1,0:T(8,128)(2,1)S(1)} %pad_maximum_fusion.1.near_b), channel_id=1, source_target_pairs={{0,1},{1,0},{2,3},{3,2},{4,5},{5,4},{6,7},{7,6},{8,9},{9,8},{10,11... | collective-permute-start | bytes 4718600 | tf_op jit(solution)/shard_map/ppermute | solution.py:375
  95.1 44.7 %collective-permute-start.6 = (bf16[1536,256]{1,0:T(8,128)(2,1)}, bf16[1536,256]{1,0:T(8,128)(2,1)S(1)}, u32[]{:S(2)}, u32[]{:S(2)}) collective-permute-start(bf16[1536,256]{1,0:T(8,128)(2,1)} %get-tuple-element.176), channel_id=1, source_target_pairs={{0,8},{1,9},{2,10},{3,11},{4,12},{5,13},{6,14},{7,15},{8,16},{9,17... | collective-permute-start | bytes 2359304 | tf_op jit(solution)/shard_map/ppermute | solution.py:367
  98.2 56.7 %collective-permute-start.7 = (bf16[1536,256]{1,0:T(8,128)(2,1)}, bf16[1536,256]{1,0:T(8,128)(2,1)}, u32[]{:S(2)}, u32[]{:S(2)}) collective-permute-start(bf16[1536,256]{1,0:T(8,128)(2,1)} %get-tuple-element.175), channel_id=1, source_target_pairs={{8,0},{9,1},{10,2},{11,3},{12,4},{13,5},{14,6},{15,7},{16,8},{17,9... | collective-permute-start | bytes 2359304 | tf_op jit(solution)/shard_map/ppermute | solution.py:367
  102.3 52.6 %copy-start.20 = (bf16[3072,128]{1,0:T(8,128)(2,1)S(1)}, bf16[3072,128]{1,0:T(8,128)(2,1)}, u32[]{:S(2)}) copy-start(bf16[3072,128]{1,0:T(8,128)(2,1)} %copy-done.18) | copy-start | bytes 2359300
  139.8 26.0 %copy-start.16 = (bf16[1536,256]{1,0:T(8,128)(2,1)}, bf16[1536,256]{1,0:T(8,128)(2,1)S(1)}, u32[]{:S(2)}) copy-start(bf16[1536,256]{1,0:T(8,128)(2,1)S(1)} %collective-permute-done.6.left_ref) | copy-start | bytes 2359300
  165.8 17.0 %all-to-all-start.1 = ((bf16[8,384,1,128]{3,1,2,0:T(8,128)(2,1)}), bf16[8,384,1,128]{3,1,2,0:T(8,128)(2,1)}, u32[]{:S(2)}, u32[]{:S(2)}) async-start(bf16[8,384,1,128]{3,1,2,0:T(8,128)(2,1)} %bitcast.34), calls=%async_computation.1 | async-start | bytes 1572864 | tf_op jit(solution)/shard_map/all_to_all | solution.py:361
  216.6 17.1 %collective-permute-start.8 = (bf16[16,32,4096]{2,1,0:T(8,128)(2,1)}, bf16[16,32,4096]{2,1,0:T(8,128)(2,1)}, u32[]{:S(2)}, u32[]{:S(2)}) collective-permute-start(bf16[16,32,4096]{2,1,0:T(8,128)(2,1)} %get-tuple-element.112), channel_id=1, source_target_pairs={{0,1},{1,0},{2,3},{3,2},{4,5},{5,4},{6,7},{7,6},{8,9},{9,8},{10,11... | collective-permute-start | bytes 12582920 | tf_op jit(solution)/shard_map/ppermute | solution.py:375
  216.6 17.1 %collective-permute-start.10 = (bf16[16,32,4096]{2,1,0:T(8,128)(2,1)}, bf16[16,32,4096]{2,1,0:T(8,128)(2,1)}, u32[]{:S(2)}, u32[]{:S(2)}) collective-permute-start(bf16[16,32,4096]{2,1,0:T(8,128)(2,1)} %get-tuple-element.116), channel_id=1, source_target_pairs={{0,1},{1,0},{2,3},{3,2},{4,5},{5,4},{6,7},{7,6},{8,9},{9,8},{10,11... | collective-permute-start | bytes 12582920 | tf_op jit(solution)/shard_map/ppermute | solution.py:375
  219.3 14.4 %copy-start.2 = (bf16[16,32,4096]{2,1,0:T(8,128)(2,1)S(1)}, bf16[16,32,4096]{2,1,0:T(8,128)(2,1)}, u32[]{:S(2)}) copy-start(bf16[16,32,4096]{2,1,0:T(8,128)(2,1)} %get-tuple-element.111) | copy-start | bytes 12582916
  228.4 5.3 %collective-permute-start.9 = (bf16[16,32,1024]{2,1,0:T(8,128)(2,1)}, bf16[16,32,1024]{2,1,0:T(8,128)(2,1)S(1)}, u32[]{:S(2)}, u32[]{:S(2)}) collective-permute-start(bf16[16,32,1024]{2,1,0:T(8,128)(2,1)} %get-tuple-element.114), channel_id=1, source_target_pairs={{0,1},{1,0},{2,3},{3,2},{4,5},{5,4},{6,7},{7,6},{8,9},{9,8},{10,11... | collective-permute-start | bytes 3145736 | tf_op jit(solution)/shard_map/ppermute | solution.py:375
  242.7 62.3 %copy-start.17 = (bf16[1536,256]{1,0:T(8,128)(2,1)S(1)}, bf16[1536,256]{1,0:T(8,128)(2,1)}, u32[]{:S(2)}) copy-start(bf16[1536,256]{1,0:T(8,128)(2,1)} %copy-done.16) | copy-start | bytes 2359300
  242.7 62.3 %copy-start.21 = (bf16[3072,128]{1,0:T(8,128)(2,1)S(1)}, bf16[3072,128]{1,0:T(8,128)(2,1)}, u32[]{:S(2)}) copy-start(bf16[3072,128]{1,0:T(8,128)(2,1)} %copy-done.18) | copy-start | bytes 2359300
  242.7 99.1 %collective-permute-start.11 = (bf16[4,2,32,4608]{3,2,1,0:T(8,128)(2,1)}, bf16[4,2,32,4608]{3,2,1,0:T(8,128)(2,1)}, u32[]{:S(2)}, u32[]{:S(2)}) collective-permute-start(bf16[4,2,32,4608]{3,2,1,0:T(8,128)(2,1)} %get-tuple-element.117), channel_id=1, source_target_pairs={{0,2},{1,3},{2,0},{3,1},{4,6},{5,7},{6,4},{7,5},{8,10},{9,11},{10,... | collective-permute-start | bytes 7077896 | tf_op jit(solution)/shard_map/ppermute | solution.py:375
  243.3 98.5 %collective-permute-start.12 = (bf16[4,2,32,4608]{3,2,1,0:T(8,128)(2,1)}, bf16[4,2,32,4608]{3,2,1,0:T(8,128)(2,1)}, u32[]{:S(2)}, u32[]{:S(2)}) collective-permute-start(bf16[4,2,32,4608]{3,2,1,0:T(8,128)(2,1)} %get-tuple-element.118), channel_id=1, source_target_pairs={{0,4},{1,5},{2,6},{3,7},{4,0},{5,1},{6,2},{7,3},{8,12},{9,13},{10,... | collective-permute-start | bytes 7077896 | tf_op jit(solution)/shard_map/ppermute | solution.py:375
  305.0 36.8 %copy-start.1 = (bf16[16,32,1024]{2,1,0:T(8,128)(2,1)S(1)}, bf16[16,32,1024]{2,1,0:T(8,128)(2,1)}, u32[]{:S(2)}) copy-start(bf16[16,32,1024]{2,1,0:T(8,128)(2,1)} %get-tuple-element.113) | copy-start | bytes 3145732
  351.6 41.9 %collective-permute-start.15 = (bf16[4,32,4608]{2,1,0:T(8,128)(2,1)}, bf16[4,32,4608]{2,1,0:T(8,128)(2,1)S(1)}, u32[]{:S(2)}, u32[]{:S(2)}) collective-permute-start(bf16[4,32,4608]{2,1,0:T(8,128)(2,1)} %get-tuple-element.131), channel_id=1, source_target_pairs={{0,4},{1,5},{2,6},{3,7},{4,0},{5,1},{6,2},{7,3},{8,12},{9,13},{10,... | collective-permute-start | bytes 3538952 | tf_op jit(solution)/shard_map/ppermute | solution.py:375
  352.9 40.6 %collective-permute-start.16 = (bf16[4,32,4608]{2,1,0:T(8,128)(2,1)}, bf16[4,32,4608]{2,1,0:T(8,128)(2,1)}, u32[]{:S(2)}, u32[]{:S(2)}) collective-permute-start(bf16[4,32,4608]{2,1,0:T(8,128)(2,1)} %get-tuple-element.132), channel_id=1, source_target_pairs={{0,2},{1,3},{2,0},{3,1},{4,6},{5,7},{6,4},{7,5},{8,10},{9,11},{10,... | collective-permute-start | bytes 3538952 | tf_op jit(solution)/shard_map/ppermute | solution.py:375
  353.7 39.7 %collective-permute-start.13 = (bf16[1536,256]{1,0:T(8,128)(2,1)}, bf16[1536,256]{1,0:T(8,128)(2,1)S(1)}, u32[]{:S(2)}, u32[]{:S(2)}) collective-permute-start(bf16[1536,256]{1,0:T(8,128)(2,1)} %get-tuple-element.128), channel_id=1, source_target_pairs={{0,8},{1,9},{2,10},{3,11},{4,12},{5,13},{6,14},{7,15},{8,16},{9,17... | collective-permute-start | bytes 2359304 | tf_op jit(solution)/shard_map/ppermute | solution.py:367
  358.0 35.5 %collective-permute-start.14 = (bf16[1536,256]{1,0:T(8,128)(2,1)}, bf16[1536,256]{1,0:T(8,128)(2,1)}, u32[]{:S(2)}, u32[]{:S(2)}) collective-permute-start(bf16[1536,256]{1,0:T(8,128)(2,1)} %get-tuple-element.129), channel_id=1, source_target_pairs={{8,0},{9,1},{10,2},{11,3},{12,4},{13,5},{14,6},{15,7},{16,8},{17,9... | collective-permute-start | bytes 2359304 | tf_op jit(solution)/shard_map/ppermute | solution.py:367
  363.0 31.5 %copy-start.12 = (bf16[4,32,4608]{2,1,0:T(8,128)(2,1)S(1)}, bf16[4,32,4608]{2,1,0:T(8,128)(2,1)}, u32[]{:S(2)}) copy-start(bf16[4,32,4608]{2,1,0:T(8,128)(2,1)} %copy-done.11) | copy-start | bytes 3538948
  402.8 10.8 %copy-start.31 = (bf16[32,9216]{1,0:T(8,128)(2,1)S(1)}, bf16[32,9216]{1,0:T(8,128)(2,1)}, u32[]{:S(2)}) copy-start(bf16[32,9216]{1,0:T(8,128)(2,1)} %get-tuple-element.146) | copy-start | bytes 1769476
  402.8 34.0 %all-to-all-start.3 = ((bf16[8,384,384]{2,1,0:T(8,128)(2,1)}), bf16[8,384,384]{2,1,0:T(8,128)(2,1)}, u32[]{:S(2)}, u32[]{:S(2)}) async-start(bf16[8,384,384]{2,1,0:T(8,128)(2,1)} %bitcast.186), calls=%async_computation.3 | async-start | bytes 4718592 | tf_op jit(solution)/shard_map/all_to_all | solution.py:436
  409.7 35.1 %collective-permute-start.17 = (bf16[32,9216]{1,0:T(8,128)(2,1)}, bf16[32,9216]{1,0:T(8,128)(2,1)}, u32[]{:S(2)}, u32[]{:S(2)}) collective-permute-start(bf16[32,9216]{1,0:T(8,128)(2,1)} %get-tuple-element.145), channel_id=1, source_target_pairs={{0,8},{1,9},{2,10},{3,11},{4,12},{5,13},{6,14},{7,15},{8,16},{9,17... | collective-permute-start | bytes 1769480 | tf_op jit(solution)/shard_map/ppermute | solution.py:539
  413.7 39.1 %collective-permute-start.18 = (bf16[32,9216]{1,0:T(8,128)(2,1)S(1)}, bf16[32,9216]{1,0:T(8,128)(2,1)}, u32[]{:S(2)}, u32[]{:S(2)}) collective-permute-start(bf16[32,9216]{1,0:T(8,128)(2,1)S(1)} %copy-done.31), channel_id=1, source_target_pairs={{0,16},{1,17},{2,18},{3,19},{4,20},{5,21},{6,22},{7,23},{8,24},{9,... | collective-permute-start | bytes 1769480 | tf_op jit(solution)/shard_map/ppermute | solution.py:539
  413.7 39.1 %collective-permute-start.19 = (bf16[32,9216]{1,0:T(8,128)(2,1)S(1)}, bf16[32,9216]{1,0:T(8,128)(2,1)}, u32[]{:S(2)}, u32[]{:S(2)}) collective-permute-start(bf16[32,9216]{1,0:T(8,128)(2,1)S(1)} %get-tuple-element.147), channel_id=1, source_target_pairs={{0,24},{1,25},{2,26},{3,27},{4,28},{5,29},{6,30},{7,31},{8,0},{9,1... | collective-permute-start | bytes 1769480 | tf_op jit(solution)/shard_map/ppermute | solution.py:539
  436.8 16.0 %copy-start.25 = (bf16[4,32,4608]{2,1,0:T(8,128)(2,1)S(1)}, bf16[4,32,4608]{2,1,0:T(8,128)(2,1)}, u32[]{:S(2)}) copy-start(bf16[4,32,4608]{2,1,0:T(8,128)(2,1)} %copy-done.24) | copy-start | bytes 3538948
  456.0 18.9 %copy-start.4 = (f32[384,1024]{1,0:T(8,128)S(1)}, f32[384,1024]{1,0:T(8,128)}, u32[]{:S(2)}) copy-start(f32[384,1024]{1,0:T(8,128)} %get-tuple-element.150.dy1) | copy-start | bytes 4718596
  458.6 25.7 %collective-permute-start.20 = (bf16[8,32,384]{2,1,0:T(8,128)(2,1)S(1)}, bf16[8,32,384]{2,1,0:T(8,128)(2,1)S(1)}, u32[]{:S(2)}, u32[]{:S(2)}) collective-permute-start(bf16[8,32,384]{2,1,0:T(8,128)(2,1)S(1)} %get-tuple-element.183), channel_id=1, source_target_pairs={{0,8},{1,9},{2,10},{3,11},{4,12},{5,13},{6,14},{7,15},{8,16},{9,17... | collective-permute-start | bytes 589832 | tf_op jit(solution)/shard_map/ppermute | solution.py:539
  471.8 15.7 %collective-permute-start.21 = (bf16[8,32,384]{2,1,0:T(8,128)(2,1)S(1)}, bf16[8,32,384]{2,1,0:T(8,128)(2,1)}, u32[]{:S(2)}, u32[]{:S(2)}) collective-permute-start(bf16[8,32,384]{2,1,0:T(8,128)(2,1)S(1)} %get-tuple-element.182), channel_id=1, source_target_pairs={{0,16},{1,17},{2,18},{3,19},{4,20},{5,21},{6,22},{7,23},{8,24},{9,... | collective-permute-start | bytes 589832 | tf_op jit(solution)/shard_map/ppermute | solution.py:539
  474.8 12.7 %collective-permute-start.22 = (bf16[8,32,384]{2,1,0:T(8,128)(2,1)S(1)}, bf16[8,32,384]{2,1,0:T(8,128)(2,1)}, u32[]{:S(2)}, u32[]{:S(2)}) collective-permute-start(bf16[8,32,384]{2,1,0:T(8,128)(2,1)S(1)} %get-tuple-element.181), channel_id=1, source_target_pairs={{0,24},{1,25},{2,26},{3,27},{4,28},{5,29},{6,30},{7,31},{8,0},{9,1... | collective-permute-start | bytes 589832 | tf_op jit(solution)/shard_map/ppermute | solution.py:539
  474.9 8.8 %copy-start.32 = (f32[32,512]{1,0:T(8,128)S(1)}, f32[32,512]{1,0:T(8,128)}, u32[]{:S(2)}) copy-start(f32[32,512]{1,0:T(8,128)} %get-tuple-element.180) | copy-start | bytes 196612
  474.9 12.7 %copy-start.34 = (f32[32,32]{1,0:T(8,128)S(1)}, f32[32,32]{1,0:T(8,128)}, u32[]{:S(2)}) copy-start(f32[32,32]{1,0:T(8,128)} %reshape_squeeze.25) | copy-start | bytes 12292
  474.9 12.7 %copy-start.35 = (f32[32,32]{1,0:T(8,128)S(1)}, f32[32,32]{1,0:T(8,128)}, u32[]{:S(2)}) copy-start(f32[32,32]{1,0:T(8,128)} %reshape_squeeze.26) | copy-start | bytes 12292
  474.9 12.7 %copy-start.36 = (f32[32,32]{1,0:T(8,128)S(1)}, f32[32,32]{1,0:T(8,128)}, u32[]{:S(2)}) copy-start(f32[32,32]{1,0:T(8,128)} %reshape_squeeze.27) | copy-start | bytes 12292
  488.4 14.3 %all-to-all-start.4 = ((f32[32,1,448]{2,1,0:T(1,128)}), f32[32,1,448]{2,1,0:T(1,128)S(1)}, u32[]{:S(2)}, u32[]{:S(2)}) async-start(f32[32,1,448]{2,1,0:T(1,128)} %all_to_all.25), calls=%async_computation.4 | async-start | bytes 131072 | tf_op jit(solution)/shard_map/all_to_all | solution.py:960
  502.7 11.7 %all-to-all-start.5 = ((f32[8,32,384]{2,1,0:T(8,128)}), f32[8,32,384]{2,1,0:T(8,128)S(1)}, u32[]{:S(2)}, u32[]{:S(2)}) async-start(f32[8,32,384]{2,1,0:T(8,128)} %fusion.12), calls=%async_computation.5 | async-start | bytes 786432 | tf_op jit(solution)/shard_map/all_to_all | solution.py:436
  (30 other events, 89.3 us)
Sparse Core Ops, SparseCore 0:
  10.9 158.8 all-gather.2
  173.3 68.9 all-gather.4

commit v3 on v2

--- a/solution.py
+++ b/solution.py
@@ -912,6 +912,7 @@
 
     do_heads = in_plane(do, devices).reshape(span, -1)
     if by_axes:
+        do_heads, out_a, out_b = lax.optimization_barrier((do_heads, out_a, out_b))
         in_a, in_b = swapped(out_a, 2, devices), swapped(out_b, 4, devices)
     part_dq, mid0, out_left, out_right = backward_first(prefetch, seg, q, kv, left, right, o_heads, do_heads, lse)
     if by_axes:

time: 525 us -> 484 us (0.922)
  blocking collectives: 61 us -> 0 us
  waiting for transfers between devices: 119 us -> 131 us
  starting transfers between devices: 70.8 us -> 78.8 us
    all_to_all x1 -> x0, blocking collectives: 61 us -> none  [in_plane(): lax.all_to_all(stack, 'dev', 0, 0, axis_index_groups=groups_of(devices),...]
    ppermute x13, waiting for transfers between devices: 51.7 us -> 61.2 us  [swapped(): return lax.ppermute(value, 'dev', [(i, i ^ bit) for i in range(devices)])]
    all_to_all x2 -> x3, starting transfers between devices: 7.99 us -> 12.5 us  [in_plane(): lax.all_to_all(stack, 'dev', 0, 0, axis_index_groups=groups_of(devices),...]
    all_to_all x2 -> x3, waiting for transfers between devices: 26.7 us -> 30.7 us  [in_plane(): lax.all_to_all(stack, 'dev', 0, 0, axis_index_groups=groups_of(devices),...]
  transfers between devices with their start and end apart: 30 -> 31, of which waited for: 13 -> 16; matrix products, arithmetic and copies ran while one was open for 7% -> 7% of each run, Pallas kernels for 35% -> 37%
where the time goes in v3:
time: 484 us; the launch traced here: 483 us
  Pallas kernels  190 us (39%)
  waiting for transfers between devices  131 us (27%)
  starting transfers between devices  78.8 us (16%)
  local copies, waits for them, and re-layouts  45 us (9%)
  between operations  14.9 us (3%)
  other arithmetic  12.8 us (3%)
  matrix products  10.9 us (2%)
    pallas_call x4, Pallas kernels, attention_call(): pl.pallas_call(kernel, out_shape=tuple(outputs), grid_spec=pltpu.Prefetch...  113 us
    ppermute x13, waiting for transfers between devices, swapped(): return lax.ppermute(value, 'dev', [(i, i ^ bit) for i in range(devices)])  61.2 us
    all_to_all x3, waiting for transfers between devices, in_plane(): lax.all_to_all(stack, 'dev', 0, 0, axis_index_groups=groups_of(devices),...  30.7 us
    pallas_call x1, Pallas kernels, mlp_all(): pl.pallas_call(mlp_kernel, out_shape=(total, total, jax.ShapeDtypeStruct(...  29.7 us
    unnamed x100, local copies, waits for them, and re-layouts  21.1 us
    ppermute x6, starting transfers between devices, send_planes(): lax.ppermute(piece, 'dev', [(i, (i + (k + 1) * GROUP) % devices) for i in...  18.8 us
    ppermute x4, waiting for transfers between devices, shifted(): return lax.ppermute(shard, 'dev', pairs)  15.2 us
    ppermute x4, starting transfers between devices, shifted(): return lax.ppermute(shard, 'dev', pairs)  14.9 us
  transfers between devices with their start and end apart: 31, of which 16 were waited for; matrix products, arithmetic and copies ran while one was open for 7% of the time, Pallas kernels for 37%

profile of v3, /device:TPU:0, one launch (start us, length us, event | category | flops | bytes accessed | tf_op | source)
XLA Modules:
  0.0 482.7 jit_solution(5661288158204200072)
XLA Ops:
  8.3 1.9 pad_maximum_fusion.4
  11.2 3.0 collective-permute-start
  17.1 6.4 %collective-permute-done = bf16[384,512]{1,0:T(8,128)(2,1)S(1)} collective-permute-done((bf16[384,512]{1,0:T(8,128)(2,1)}, bf16[384,512]{1,0:T(8,128)(2,1)S(1)}, u32[]{:S(2)}, u32[]{:S(2)}) %collective-permute-start) | collective-permute-done | bytes 393248 | tf_op jit(solution)/shard_map/ppermute | solution.py:375
  23.5 1.9 collective-permute-done.1
  26.5 6.0 %all-to-all-start = ((bf16[32,32,512]{2,1,0:T(8,128)(2,1)}), bf16[32,32,512]{2,1,0:T(8,128)(2,1)S(1)}, u32[]{:S(2)}, u32[]{:S(2)}) async-start(bf16[32,32,512]{2,1,0:T(8,128)(2,1)} %bitcast.14), calls=%async_computation | async-start | bytes 2097152 | tf_op jit(solution)/shard_map/all_to_all | solution.py:480
  32.6 1.8 collective-permute-start.3
  34.6 1.5 collective-permute-start.2
  36.1 35.7 %collective-permute-done.3 = bf16[2,384,512]{2,1,0:T(8,128)(2,1)S(1)} collective-permute-done((bf16[2,384,512]{2,1,0:T(8,128)(2,1)S(1)}, bf16[2,384,512]{2,1,0:T(8,128)(2,1)S(1)}, u32[]{:S(2)}, u32[]{:S(2)}) %collective-permute-start.3) | collective-permute-done | bytes 786464 | tf_op jit(solution)/shard_map/ppermute | solution.py:375
  75.1 1.7 copy.93
  76.8 1.8 reshape.237
  82.0 11.2 %plane_qkv.1 = (bf16[3072,1024]{1,0:T(8,128)(2,1)}, bf16[3072,128]{1,0:T(8,128)(2,1)S(1)}, bf16[3072,256]{1,0:T(8,128)(2,1)S(1)}) custom-call(s32[4]{0:T(128)S(1)} %pad_add_fusion.2.bits, bf16[2,2,384,512]{3,2,1,0:T(8,128)(2,1)S(1)} %copy-done.7, bf16[2,2,384,512]{3,2,1,0:T(8,128)(2,1)} %collective-permute-done.4.far_a, ...), custom_call_target="tpu_custom_call" | custom-call | flops 5368709120 | bytes 16777216 | tf_op jit(solution)/shard_map/plane_qkv/pallas_call | solution.py:503
  95.1 3.1 collective-permute-start.6
  102.3 37.5 %forward_mid.1 = (f32[128,3072]{1,0:T(8,128)S(1)}, f32[8,3072]{1,0:T(8,128)S(1)}) custom-call(s32[12]{0:T(128)S(1)} %get-tuple-element.219.low, s32[12]{0:T(128)S(1)} %get-tuple-element.220.high, s32[2,3072]{1,0:T(2,128)S(1)} %pad_add_fusion.seg, bf16[3072,128]{1,0:T(8,128)(2,1)S(1)} %copy-done.19, bf16[3072,256]{1,0:T(8,128)(2,1)S(1)} %copy-done.5), custom_call_target="tpu_custom_call" | custom-call | flops 3221225472 | bytes 8388608 | tf_op jit(solution)/shard_map/forward_mid/pallas_call | solution.py:230
  139.9 15.2 %collective-permute-done.7.right_ref = bf16[1536,256]{1,0:T(8,128)(2,1)} collective-permute-done((bf16[1536,256]{1,0:T(8,128)(2,1)}, bf16[1536,256]{1,0:T(8,128)(2,1)}, u32[]{:S(2)}, u32[]{:S(2)}) %collective-permute-start.7) | collective-permute-done | bytes 786464 | tf_op jit(solution)/shard_map/ppermute | solution.py:367
  155.0 10.3 %forward_edge.1 = (bf16[3072,128]{1,0:T(8,128)(2,1)}, f32[8,3072]{1,0:T(8,128)S(1)}) custom-call(s32[12]{0:T(128)S(1)} %get-tuple-element.219.low, s32[12]{0:T(128)S(1)} %get-tuple-element.220.high, s32[2,3072]{1,0:T(2,128)S(1)} %pad_add_fusion.seg, bf16[3072,128]{1,0:T(8,128)(2,1)S(1)} %copy-done.20, bf16[1536,256]{1,0:T(8,128)(2,1)S(1)} %collective-permute-done.6.left_ref, ...), custom_call_target="tpu_custom_call" | custom-call | flops 3221225472 | bytes 8388608 | tf_op jit(solution)/shard_map/forward_edge/pallas_call | solution.py:230
  165.3 4.5 all-to-all-start.1
  170.4 3.2 slice.169
  173.6 8.7 %all-to-all-done.1 = bf16[8,384,1,128]{3,1,2,0:T(8,128)(2,1)} async-done(((bf16[8,384,1,128]{3,1,2,0:T(8,128)(2,1)}), bf16[8,384,1,128]{3,1,2,0:T(8,128)(2,1)}, u32[]{:S(2)}, u32[]{:S(2)}) %all-to-all-start.1) | async-done | bytes 786464 | tf_op jit(solution)/shard_map/all_to_all | solution.py:361
  182.3 3.0 fusion.10
  186.4 29.7 %mlp_all.1 = (f32[384,1024]{1,0:T(8,128)}, f32[384,1024]{1,0:T(8,128)}, f32[1,4096]{1,0:T(1,128)S(1)}, bf16[16,32,4096]{2,1,0:T(8,128)(2,1)}, bf16[16,32,4096]{2...) custom-call(s32[3]{0:T(128)S(1)} %pad_add_fusion.1.bits, ...), custom_call_target="tpu_custom_call" | custom-call | flops 6442450944 | bytes 33554432 | tf_op jit(solution)/shard_map/mlp_all/pallas_call | solution.py:619
  216.6 2.1 copy_bitcast_fusion.o_ref
  218.8 8.8 %after_mlp.1 = (bf16[384,1024]{1,0:T(8,128)(2,1)}, f32[384,1024]{1,0:T(8,128)}, f32[8,1024]{1,0:T(8,128)S(1)}, bf16[8,384,128]{2,1,0:T(8,128)(2,1)S(1)}, bf16[16...) custom-call(s32[3]{0:T(128)S(1)} %pad_add_fusion.1.bits, f32[384,1024]{1,0:T(8,128)} %get-tuple-element.108.mlp, ...), custom_call_target="tpu_custom_call" | custom-call | flops 1610612736 | bytes 20971520 | tf_op jit(solution)/shard_map/after_mlp/pallas_call | solution.py:695
  228.5 4.6 all-to-all-start.2
  233.2 2.2 copy-done.1
  235.4 6.2 %first_sends.1 = (bf16[4,2,32,4608]{3,2,1,0:T(8,128)(2,1)S(1)}, bf16[4,2,32,4608]{3,2,1,0:T(8,128)(2,1)S(1)}) custom-call(s32[3]{0:T(128)S(1)} %pad_add_fusion.1.bits, bf16[4,2,2,32,4096]{4,3,2,1,0:T(8,128)(2,1)S(1)} %bitcast.173, bf16[4,2,2,32,4096]{4,3,2,1,0:T(8,128)(2,1)} %bitcast.48.refs_1_.refs_7_, bf16[4,2,2,32,1024]{4,3,2,1,0:T(8,128)(2,1)S(1)} %bitcast.159, ...), custom_call_target="tpu_custom_call" | custom-call | bytes 16777216 | tf_op jit(solution)/shard_map/first_sends/pallas_call | solution.py:732
  243.1 1.5 copy-done.15
  249.9 34.8 %backward_first.1 = (f32[128,3072]{1,0:T(8,128)}, f32[3072,256]{1,0:T(8,128)}, bf16[1536,256]{1,0:T(8,128)(2,1)}, bf16[1536,256]{1,0:T(8,128)(2,1)}) custom-call(s32[12]{0:T(128)S(1)} %get-tuple-element.219.low, s32[12]{0:T(128)S(1)} %get-tuple-element.220.high, s32[2,3072]{1,0:T(2,128)S(1)} %pad_add_fusion.seg, bf16[3072,128]{1,0:T(8,128)(2,1)S(1)} %copy-done.21, ...), custom_call_target="tpu_custom_call" | custom-call | flops 3221225472 | bytes 8388608 | tf_op jit(solution)/shard_map/backward_first/pallas_call | solution.py:230
  284.8 13.4 %collective-permute-done.11.refs_2_.refs_5_.refs_8_.refs_11_ = bf16[4,2,32,4608]{3,2,1,0:T(8,128)(2,1)} collective-permute-done((bf16[4,2,32,4608]{3,2,1,0:T(8,128)(2,1)}, bf16[4,2,32,4608]{3,2,1,0:T(8,128)(2,1)}, u32[]{:S(2)}, u32[]{:S(2)}) %collective-permute-start.11) | collective-permute-done | bytes 2359328 | tf_op jit(solution)/shard_map/ppermute | solution.py:375
  299.4 7.6 %second_sums.1 = (bf16[4,32,4608]{2,1,0:T(8,128)(2,1)}, bf16[4,32,4608]{2,1,0:T(8,128)(2,1)S(1)}, bf16[4,32,4608]{2,1,0:T(8,128)(2,1)}, bf16[4,32,4608]{2,1,0:T(8,128)(2,1)S(1)}) custom-call(s32[3]{0:T(128)S(1)} %pad_add_fusion.1.bits, bf16[4,2,2,32,4096]{4,3,2,1,0:T(8,128)(2,1)} %bitcast.171, bf16[4,2,2,32,4096]{4,3,2,1,0:T(8,128)(2,1)} %bitcast.48.refs_1_.refs_7_, ...), custom_call_target="tpu_custom_call" | custom-call | bytes 16777216 | tf_op jit(solution)/shard_map/second_sums/pallas_call | solution.py:732
  309.2 1.5 collective-permute-start.15
  311.3 9.2 %collective-permute-start.13 = (bf16[1536,256]{1,0:T(8,128)(2,1)}, bf16[1536,256]{1,0:T(8,128)(2,1)S(1)}, u32[]{:S(2)}, u32[]{:S(2)}) collective-permute-start(bf16[1536,256]{1,0:T(8,128)(2,1)} %get-tuple-element.134), channel_id=1, source_target_pairs={{0,8},{1,9},{2,10},{3,11},{4,12},{5,13},{6,14},{7,15},{8,16},{9,17... | collective-permute-start | bytes 2359304 | tf_op jit(solution)/shard_map/ppermute | solution.py:367
  324.4 30.6 %backward_second.1 = (bf16[3072,128]{1,0:T(8,128)(2,1)S(1)}, f32[3072,256]{1,0:T(8,128)}) custom-call(s32[12]{0:T(128)S(1)} %get-tuple-element.219.low, s32[12]{0:T(128)S(1)} %get-tuple-element.220.high, s32[2,3072]{1,0:T(2,128)S(1)} %pad_add_fusion.seg, bf16[3072,128]{1,0:T(8,128)(2,1)S(1)} %copy-done.22, bf16[3072,256]{1,0:T(8,128)(2,1)S(1)} %copy-done.6, ...), custom_call_target="tpu_custom_call" | custom-call | flops 3221225472 | bytes 8388608 | tf_op jit(solution)/shard_map/backward_second/pallas_call | solution.py:230
  356.1 1.7 add_convert_fusion
  359.7 4.6 joined_heads.1
  364.4 4.5 all-to-all-start.3
  372.0 3.1 collective-permute-start.19
  375.1 23.3 %all-to-all-done.3.dqkv = bf16[8,384,384]{2,1,0:T(8,128)(2,1)} async-done(((bf16[8,384,384]{2,1,0:T(8,128)(2,1)}), bf16[8,384,384]{2,1,0:T(8,128)(2,1)}, u32[]{:S(2)}, u32[]{:S(2)}) %all-to-all-start.3) | async-done | bytes 2359328 | tf_op jit(solution)/shard_map/all_to_all | solution.py:436
  398.4 7.9 %convolution_convert_fusion = bf16[1024,384]{1,0:T(8,128)(2,1)} fusion(bf16[3072,1024]{1,0:T(8,128)(2,1)} %get-tuple-element.150, bf16[3072,384]{1,0:T(8,128)(2,1)} %joined_heads.1), kind=kOutput, calls=%fused_computation.17 | convolution fusion | flops 2416312320 | bytes 9437184 | tf_op jit(solution)/shard_map/td,tf->df/dot_general | solution.py:305
  406.3 8.1 %collective-permute-done.18 = bf16[32,9216]{1,0:T(8,128)(2,1)} collective-permute-done((bf16[32,9216]{1,0:T(8,128)(2,1)S(1)}, bf16[32,9216]{1,0:T(8,128)(2,1)}, u32[]{:S(2)}, u32[]{:S(2)}) %collective-permute-start.18) | collective-permute-done | bytes 589856 | tf_op jit(solution)/shard_map/ppermute | solution.py:539
  414.3 1.7 fusion.1
  420.2 12.5 %collective-permute-start.20 = (bf16[8,32,384]{2,1,0:T(8,128)(2,1)S(1)}, bf16[8,32,384]{2,1,0:T(8,128)(2,1)S(1)}, u32[]{:S(2)}, u32[]{:S(2)}) collective-permute-start(bf16[8,32,384]{2,1,0:T(8,128)(2,1)S(1)} %get-tuple-element.189), channel_id=1, source_target_pairs={{0,8},{1,9},{2,10},{3,11},{4,12},{5,13},{6,14},{7,15},{8,16},{9,17... | collective-permute-start | bytes 589832 | tf_op jit(solution)/shard_map/ppermute | solution.py:539
  432.8 2.3 collective-permute-start.22
  435.1 8.6 %input_gradient.1 = (bf16[384,1024]{1,0:T(8,128)(2,1)}, f32[8,1024]{1,0:T(8,128)S(1)}, f32[8,384]{1,0:T(8,128)S(1)}) custom-call(bf16[8,384,384]{2,1,0:T(8,128)(2,1)} %all-to-all-done.3.dqkv, bf16[1024,3072]{1,0:T(8,128)(2,1)} %all-gather.5.cloned.1.call-done.weight, f32[384,1024]{1,0:T(8,128)S(1)} %copy-done.3, bf16[384,1024]{1,0:T(8,128)(2,1)S(1)} %copy-done.2, ...), custom_call_target="tpu_custom_call" | custom-call | flops 2415919104 | bytes 12582912 | tf_op jit(solution)/shard_map/input_gradient/pallas_call | solution.py:423
  446.6 8.8 %all-to-all-start.4 = ((f32[32,1,448]{2,1,0:T(1,128)}), f32[32,1,448]{2,1,0:T(1,128)S(1)}, u32[]{:S(2)}, u32[]{:S(2)}) async-start(f32[32,1,448]{2,1,0:T(1,128)} %all_to_all.25), calls=%async_computation.4 | async-start | bytes 131072 | tf_op jit(solution)/shard_map/all_to_all | solution.py:961
  455.5 2.0 fusion.12
  457.4 5.4 %all-to-all-done.4 = f32[32,1,448]{2,1,0:T(1,128)S(1)} async-done(((f32[32,1,448]{2,1,0:T(1,128)}), f32[32,1,448]{2,1,0:T(1,128)S(1)}, u32[]{:S(2)}, u32[]{:S(2)}) %all-to-all-start.4) | async-done | bytes 57376 | tf_op jit(solution)/shard_map/all_to_all | solution.py:961
  462.9 3.5 all-to-all-start.5
  468.1 6.5 %all-to-all-done.5 = f32[8,32,384]{2,1,0:T(8,128)S(1)} async-done(((f32[8,32,384]{2,1,0:T(8,128)}), f32[8,32,384]{2,1,0:T(8,128)S(1)}, u32[]{:S(2)}, u32[]{:S(2)}) %all-to-all-start.5) | async-done | bytes 393248 | tf_op jit(solution)/shard_map/all_to_all | solution.py:436
  (208 shorter events, 52.8 us)
Async XLA Ops:
  7.2 163.2 %all-gather.3.cloned.1.call-start = ((), (), s32[]{:S(2)}) async-start(), calls=%async_computation.6 | async-start | bytes 19464192 | tf_op jit(solution)/shard_map/all_gather | solution.py:331
  10.2 6.6 %copy-start.37 = (bf16[32]{0:T(256)(128)(2,1)S(1)}, bf16[32]{0:T(256)(128)(2,1)}, u32[]{:S(2)}) copy-start(bf16[32]{0:T(256)(128)(2,1)} %param.20) | copy-start | bytes 196
  10.2 6.6 %copy-start.38 = (bf16[32]{0:T(256)(128)(2,1)S(1)}, bf16[32]{0:T(256)(128)(2,1)}, u32[]{:S(2)}) copy-start(bf16[32]{0:T(256)(128)(2,1)} %param.21) | copy-start | bytes 196
  10.2 6.6 %copy-start.39 = (bf16[32]{0:T(256)(128)(2,1)S(1)}, bf16[32]{0:T(256)(128)(2,1)}, u32[]{:S(2)}) copy-start(bf16[32]{0:T(256)(128)(2,1)} %param.25) | copy-start | bytes 196
  10.2 6.6 %copy-start.40 = (bf16[32]{0:T(256)(128)(2,1)S(1)}, bf16[32]{0:T(256)(128)(2,1)}, u32[]{:S(2)}) copy-start(bf16[32]{0:T(256)(128)(2,1)} %param.26) | copy-start | bytes 196
  10.2 6.6 %copy-start.41 = (bf16[32]{0:T(256)(128)(2,1)S(1)}, bf16[32]{0:T(256)(128)(2,1)}, u32[]{:S(2)}) copy-start(bf16[32]{0:T(256)(128)(2,1)} %param.27) | copy-start | bytes 196
  10.3 6.6 %copy-start.42 = (bf16[32]{0:T(256)(128)(2,1)S(1)}, bf16[32]{0:T(256)(128)(2,1)}, u32[]{:S(2)}) copy-start(bf16[32]{0:T(256)(128)(2,1)} %param.28) | copy-start | bytes 196
  10.3 6.6 %copy-start.43 = (bf16[32]{0:T(256)(128)(2,1)S(1)}, bf16[32]{0:T(256)(128)(2,1)}, u32[]{:S(2)}) copy-start(bf16[32]{0:T(256)(128)(2,1)} %param.32) | copy-start | bytes 196
  11.2 12.3 %collective-permute-start = (bf16[384,512]{1,0:T(8,128)(2,1)}, bf16[384,512]{1,0:T(8,128)(2,1)S(1)}, u32[]{:S(2)}, u32[]{:S(2)}) collective-permute-start(bf16[384,512]{1,0:T(8,128)(2,1)} %get-tuple-element.195), channel_id=1, source_target_pairs={{0,4},{1,5},{2,6},{3,7},{4,0},{5,1},{6,2},{7,3},{8,12},{9,13},{10,... | collective-permute-start | bytes 1179656 | tf_op jit(solution)/shard_map/ppermute | solution.py:375
  14.1 11.3 %collective-permute-start.1 = (bf16[384,512]{1,0:T(8,128)(2,1)S(1)}, bf16[384,512]{1,0:T(8,128)(2,1)S(1)}, u32[]{:S(2)}, u32[]{:S(2)}) collective-permute-start(bf16[384,512]{1,0:T(8,128)(2,1)S(1)} %get-tuple-element.194), channel_id=1, source_target_pairs={{0,2},{1,3},{2,0},{3,1},{4,6},{5,7},{6,4},{7,5},{8,10},{9,11},{10,... | collective-permute-start | bytes 1179656 | tf_op jit(solution)/shard_map/ppermute | solution.py:375
  26.5 48.1 %all-to-all-start = ((bf16[32,32,512]{2,1,0:T(8,128)(2,1)}), bf16[32,32,512]{2,1,0:T(8,128)(2,1)S(1)}, u32[]{:S(2)}, u32[]{:S(2)}) async-start(bf16[32,32,512]{2,1,0:T(8,128)(2,1)} %bitcast.14), calls=%async_computation | async-start | bytes 2097152 | tf_op jit(solution)/shard_map/all_to_all | solution.py:480
  32.5 252.3 %all-gather.5.cloned.1.call-start = ((), (), s32[]{:S(2)}) async-start(), calls=%async_computation.7 | async-start | bytes 6488064 | tf_op jit(solution)/shard_map/all_gather | solution.py:331
  32.6 39.2 %collective-permute-start.3 = (bf16[2,384,512]{2,1,0:T(8,128)(2,1)S(1)}, bf16[2,384,512]{2,1,0:T(8,128)(2,1)S(1)}, u32[]{:S(2)}, u32[]{:S(2)}) collective-permute-start(bf16[2,384,512]{2,1,0:T(8,128)(2,1)S(1)} %get-tuple-element.191), channel_id=1, source_target_pairs={{0,4},{1,5},{2,6},{3,7},{4,0},{5,1},{6,2},{7,3},{8,12},{9,13},{10,... | collective-permute-start | bytes 2359304 | tf_op jit(solution)/shard_map/ppermute | solution.py:375
  34.6 38.7 %collective-permute-start.2 = (bf16[2,384,512]{2,1,0:T(8,128)(2,1)S(1)}, bf16[2,384,512]{2,1,0:T(8,128)(2,1)S(1)}, u32[]{:S(2)}, u32[]{:S(2)}) collective-permute-start(bf16[2,384,512]{2,1,0:T(8,128)(2,1)S(1)} %get-tuple-element.197), channel_id=1, source_target_pairs={{0,2},{1,3},{2,0},{3,1},{4,6},{5,7},{6,4},{7,5},{8,10},{9,11},{10,... | collective-permute-start | bytes 2359304 | tf_op jit(solution)/shard_map/ppermute | solution.py:375
  74.6 6.0 %collective-permute-start.4 = (bf16[2,2,384,512]{3,2,1,0:T(8,128)(2,1)}, bf16[2,2,384,512]{3,2,1,0:T(8,128)(2,1)}, u32[]{:S(2)}, u32[]{:S(2)}) collective-permute-start(bf16[2,2,384,512]{3,2,1,0:T(8,128)(2,1)} %pad_maximum_fusion.near_a), channel_id=1, source_target_pairs={{0,1},{1,0},{2,3},{3,2},{4,5},{5,4},{6,7},{7,6},{8,9},{9,8},{10,11... | collective-permute-start | bytes 4718600 | tf_op jit(solution)/shard_map/ppermute | solution.py:375
  74.6 6.0 %collective-permute-start.5 = (bf16[2,2,384,512]{3,2,1,0:T(8,128)(2,1)S(1)}, bf16[2,2,384,512]{3,2,1,0:T(8,128)(2,1)}, u32[]{:S(2)}, u32[]{:S(2)}) collective-permute-start(bf16[2,2,384,512]{3,2,1,0:T(8,128)(2,1)S(1)} %pad_maximum_fusion.1.near_b), channel_id=1, source_target_pairs={{0,1},{1,0},{2,3},{3,2},{4,5},{5,4},{6,7},{7,6},{8,9},{9,8},{10,11... | collective-permute-start | bytes 4718600 | tf_op jit(solution)/shard_map/ppermute | solution.py:375
  95.1 44.8 %collective-permute-start.6 = (bf16[1536,256]{1,0:T(8,128)(2,1)}, bf16[1536,256]{1,0:T(8,128)(2,1)S(1)}, u32[]{:S(2)}, u32[]{:S(2)}) collective-permute-start(bf16[1536,256]{1,0:T(8,128)(2,1)} %get-tuple-element.182), channel_id=1, source_target_pairs={{0,8},{1,9},{2,10},{3,11},{4,12},{5,13},{6,14},{7,15},{8,16},{9,17... | collective-permute-start | bytes 2359304 | tf_op jit(solution)/shard_map/ppermute | solution.py:367
  98.2 56.8 %collective-permute-start.7 = (bf16[1536,256]{1,0:T(8,128)(2,1)}, bf16[1536,256]{1,0:T(8,128)(2,1)}, u32[]{:S(2)}, u32[]{:S(2)}) collective-permute-start(bf16[1536,256]{1,0:T(8,128)(2,1)} %get-tuple-element.181), channel_id=1, source_target_pairs={{8,0},{9,1},{10,2},{11,3},{12,4},{13,5},{14,6},{15,7},{16,8},{17,9... | collective-permute-start | bytes 2359304 | tf_op jit(solution)/shard_map/ppermute | solution.py:367
  102.3 52.7 %copy-start.20 = (bf16[3072,128]{1,0:T(8,128)(2,1)S(1)}, bf16[3072,128]{1,0:T(8,128)(2,1)}, u32[]{:S(2)}) copy-start(bf16[3072,128]{1,0:T(8,128)(2,1)} %copy-done.18) | copy-start | bytes 2359300
  139.9 25.5 %copy-start.16 = (bf16[1536,256]{1,0:T(8,128)(2,1)}, bf16[1536,256]{1,0:T(8,128)(2,1)S(1)}, u32[]{:S(2)}) copy-start(bf16[1536,256]{1,0:T(8,128)(2,1)S(1)} %collective-permute-done.6.left_ref) | copy-start | bytes 2359300
  165.3 17.0 %all-to-all-start.1 = ((bf16[8,384,1,128]{3,1,2,0:T(8,128)(2,1)}), bf16[8,384,1,128]{3,1,2,0:T(8,128)(2,1)}, u32[]{:S(2)}, u32[]{:S(2)}) async-start(bf16[8,384,1,128]{3,1,2,0:T(8,128)(2,1)} %bitcast.34), calls=%async_computation.1 | async-start | bytes 1572864 | tf_op jit(solution)/shard_map/all_to_all | solution.py:361
  216.1 17.1 %collective-permute-start.8 = (bf16[16,32,4096]{2,1,0:T(8,128)(2,1)}, bf16[16,32,4096]{2,1,0:T(8,128)(2,1)}, u32[]{:S(2)}, u32[]{:S(2)}) collective-permute-start(bf16[16,32,4096]{2,1,0:T(8,128)(2,1)} %get-tuple-element.113), channel_id=1, source_target_pairs={{0,1},{1,0},{2,3},{3,2},{4,5},{5,4},{6,7},{7,6},{8,9},{9,8},{10,11... | collective-permute-start | bytes 12582920 | tf_op jit(solution)/shard_map/ppermute | solution.py:375
  216.1 17.1 %collective-permute-start.10 = (bf16[16,32,4096]{2,1,0:T(8,128)(2,1)}, bf16[16,32,4096]{2,1,0:T(8,128)(2,1)}, u32[]{:S(2)}, u32[]{:S(2)}) collective-permute-start(bf16[16,32,4096]{2,1,0:T(8,128)(2,1)} %get-tuple-element.117), channel_id=1, source_target_pairs={{0,1},{1,0},{2,3},{3,2},{4,5},{5,4},{6,7},{7,6},{8,9},{9,8},{10,11... | collective-permute-start | bytes 12582920 | tf_op jit(solution)/shard_map/ppermute | solution.py:375
  228.4 4.8 collective-permute-start.9
  228.5 17.0 %all-to-all-start.2 = ((bf16[8,384,128]{2,1,0:T(8,128)(2,1)}), bf16[8,384,128]{2,1,0:T(8,128)(2,1)}, u32[]{:S(2)}, u32[]{:S(2)}) async-start(bf16[8,384,128]{2,1,0:T(8,128)(2,1)} %copy-done.12), calls=%async_computation.2 | async-start | bytes 1572864 | tf_op jit(solution)/shard_map/all_to_all | solution.py:436
  245.5 52.7 %collective-permute-start.11 = (bf16[4,2,32,4608]{3,2,1,0:T(8,128)(2,1)}, bf16[4,2,32,4608]{3,2,1,0:T(8,128)(2,1)}, u32[]{:S(2)}, u32[]{:S(2)}) collective-permute-start(bf16[4,2,32,4608]{3,2,1,0:T(8,128)(2,1)} %copy-done.15), channel_id=1, source_target_pairs={{0,2},{1,3},{2,0},{3,1},{4,6},{5,7},{6,4},{7,5},{8,10},{9,11},{10,... | collective-permute-start | bytes 7077896 | tf_op jit(solution)/shard_map/ppermute | solution.py:375
  246.2 53.2 %collective-permute-start.12 = (bf16[4,2,32,4608]{3,2,1,0:T(8,128)(2,1)}, bf16[4,2,32,4608]{3,2,1,0:T(8,128)(2,1)}, u32[]{:S(2)}, u32[]{:S(2)}) collective-permute-start(bf16[4,2,32,4608]{3,2,1,0:T(8,128)(2,1)} %copy-done.14), channel_id=1, source_target_pairs={{0,4},{1,5},{2,6},{3,7},{4,0},{5,1},{6,2},{7,3},{8,12},{9,13},{10,... | collective-permute-start | bytes 7077896 | tf_op jit(solution)/shard_map/ppermute | solution.py:375
  309.2 45.8 %collective-permute-start.15 = (bf16[4,32,4608]{2,1,0:T(8,128)(2,1)}, bf16[4,32,4608]{2,1,0:T(8,128)(2,1)S(1)}, u32[]{:S(2)}, u32[]{:S(2)}) collective-permute-start(bf16[4,32,4608]{2,1,0:T(8,128)(2,1)} %get-tuple-element.137), channel_id=1, source_target_pairs={{0,4},{1,5},{2,6},{3,7},{4,0},{5,1},{6,2},{7,3},{8,12},{9,13},{10,... | collective-permute-start | bytes 3538952 | tf_op jit(solution)/shard_map/ppermute | solution.py:375
  310.7 44.3 %collective-permute-start.16 = (bf16[4,32,4608]{2,1,0:T(8,128)(2,1)}, bf16[4,32,4608]{2,1,0:T(8,128)(2,1)}, u32[]{:S(2)}, u32[]{:S(2)}) collective-permute-start(bf16[4,32,4608]{2,1,0:T(8,128)(2,1)} %get-tuple-element.138), channel_id=1, source_target_pairs={{0,2},{1,3},{2,0},{3,1},{4,6},{5,7},{6,4},{7,5},{8,10},{9,11},{10,... | collective-permute-start | bytes 3538952 | tf_op jit(solution)/shard_map/ppermute | solution.py:375
  311.3 43.8 %collective-permute-start.13 = (bf16[1536,256]{1,0:T(8,128)(2,1)}, bf16[1536,256]{1,0:T(8,128)(2,1)S(1)}, u32[]{:S(2)}, u32[]{:S(2)}) collective-permute-start(bf16[1536,256]{1,0:T(8,128)(2,1)} %get-tuple-element.134), channel_id=1, source_target_pairs={{0,8},{1,9},{2,10},{3,11},{4,12},{5,13},{6,14},{7,15},{8,16},{9,17... | collective-permute-start | bytes 2359304 | tf_op jit(solution)/shard_map/ppermute | solution.py:367
  320.5 34.5 %collective-permute-start.14 = (bf16[1536,256]{1,0:T(8,128)(2,1)}, bf16[1536,256]{1,0:T(8,128)(2,1)}, u32[]{:S(2)}, u32[]{:S(2)}) collective-permute-start(bf16[1536,256]{1,0:T(8,128)(2,1)} %get-tuple-element.135), channel_id=1, source_target_pairs={{8,0},{9,1},{10,2},{11,3},{12,4},{13,5},{14,6},{15,7},{16,8},{17,9... | collective-permute-start | bytes 2359304 | tf_op jit(solution)/shard_map/ppermute | solution.py:367
  324.4 31.7 %copy-start.11 = (bf16[4,32,4608]{2,1,0:T(8,128)(2,1)S(1)}, bf16[4,32,4608]{2,1,0:T(8,128)(2,1)}, u32[]{:S(2)}) copy-start(bf16[4,32,4608]{2,1,0:T(8,128)(2,1)} %copy-done.10) | copy-start | bytes 3538948
  364.4 7.6 %copy-start.31 = (bf16[32,9216]{1,0:T(8,128)(2,1)S(1)}, bf16[32,9216]{1,0:T(8,128)(2,1)}, u32[]{:S(2)}) copy-start(bf16[32,9216]{1,0:T(8,128)(2,1)} %get-tuple-element.152) | copy-start | bytes 1769476
  364.4 34.0 %all-to-all-start.3 = ((bf16[8,384,384]{2,1,0:T(8,128)(2,1)}), bf16[8,384,384]{2,1,0:T(8,128)(2,1)}, u32[]{:S(2)}, u32[]{:S(2)}) async-start(bf16[8,384,384]{2,1,0:T(8,128)(2,1)} %bitcast.184), calls=%async_computation.3 | async-start | bytes 4718592 | tf_op jit(solution)/shard_map/all_to_all | solution.py:436
  371.2 35.1 %collective-permute-start.17 = (bf16[32,9216]{1,0:T(8,128)(2,1)}, bf16[32,9216]{1,0:T(8,128)(2,1)}, u32[]{:S(2)}, u32[]{:S(2)}) collective-permute-start(bf16[32,9216]{1,0:T(8,128)(2,1)} %get-tuple-element.151), channel_id=1, source_target_pairs={{0,8},{1,9},{2,10},{3,11},{4,12},{5,13},{6,14},{7,15},{8,16},{9,17... | collective-permute-start | bytes 1769480 | tf_op jit(solution)/shard_map/ppermute | solution.py:539
  372.0 42.4 %collective-permute-start.18 = (bf16[32,9216]{1,0:T(8,128)(2,1)S(1)}, bf16[32,9216]{1,0:T(8,128)(2,1)}, u32[]{:S(2)}, u32[]{:S(2)}) collective-permute-start(bf16[32,9216]{1,0:T(8,128)(2,1)S(1)} %copy-done.31), channel_id=1, source_target_pairs={{0,16},{1,17},{2,18},{3,19},{4,20},{5,21},{6,22},{7,23},{8,24},{9,... | collective-permute-start | bytes 1769480 | tf_op jit(solution)/shard_map/ppermute | solution.py:539
  372.0 42.4 %collective-permute-start.19 = (bf16[32,9216]{1,0:T(8,128)(2,1)S(1)}, bf16[32,9216]{1,0:T(8,128)(2,1)}, u32[]{:S(2)}, u32[]{:S(2)}) collective-permute-start(bf16[32,9216]{1,0:T(8,128)(2,1)S(1)} %get-tuple-element.153), channel_id=1, source_target_pairs={{0,24},{1,25},{2,26},{3,27},{4,28},{5,29},{6,30},{7,31},{8,0},{9,1... | collective-permute-start | bytes 1769480 | tf_op jit(solution)/shard_map/ppermute | solution.py:539
  398.4 16.0 %copy-start.25 = (bf16[4,32,4608]{2,1,0:T(8,128)(2,1)S(1)}, bf16[4,32,4608]{2,1,0:T(8,128)(2,1)}, u32[]{:S(2)}) copy-start(bf16[4,32,4608]{2,1,0:T(8,128)(2,1)} %copy-done.24) | copy-start | bytes 3538948
  417.5 17.6 %copy-start.3 = (f32[384,1024]{1,0:T(8,128)S(1)}, f32[384,1024]{1,0:T(8,128)}, u32[]{:S(2)}) copy-start(f32[384,1024]{1,0:T(8,128)} %get-tuple-element.156.dy1) | copy-start | bytes 4718596
  420.2 24.5 %collective-permute-start.20 = (bf16[8,32,384]{2,1,0:T(8,128)(2,1)S(1)}, bf16[8,32,384]{2,1,0:T(8,128)(2,1)S(1)}, u32[]{:S(2)}, u32[]{:S(2)}) collective-permute-start(bf16[8,32,384]{2,1,0:T(8,128)(2,1)S(1)} %get-tuple-element.189), channel_id=1, source_target_pairs={{0,8},{1,9},{2,10},{3,11},{4,12},{5,13},{6,14},{7,15},{8,16},{9,17... | collective-permute-start | bytes 589832 | tf_op jit(solution)/shard_map/ppermute | solution.py:539
  432.7 13.1 %collective-permute-start.21 = (bf16[8,32,384]{2,1,0:T(8,128)(2,1)S(1)}, bf16[8,32,384]{2,1,0:T(8,128)(2,1)}, u32[]{:S(2)}, u32[]{:S(2)}) collective-permute-start(bf16[8,32,384]{2,1,0:T(8,128)(2,1)S(1)} %get-tuple-element.188), channel_id=1, source_target_pairs={{0,16},{1,17},{2,18},{3,19},{4,20},{5,21},{6,22},{7,23},{8,24},{9,... | collective-permute-start | bytes 589832 | tf_op jit(solution)/shard_map/ppermute | solution.py:539
  432.8 12.9 %collective-permute-start.22 = (bf16[8,32,384]{2,1,0:T(8,128)(2,1)S(1)}, bf16[8,32,384]{2,1,0:T(8,128)(2,1)}, u32[]{:S(2)}, u32[]{:S(2)}) collective-permute-start(bf16[8,32,384]{2,1,0:T(8,128)(2,1)S(1)} %get-tuple-element.187), channel_id=1, source_target_pairs={{0,24},{1,25},{2,26},{3,27},{4,28},{5,29},{6,30},{7,31},{8,0},{9,1... | collective-permute-start | bytes 589832 | tf_op jit(solution)/shard_map/ppermute | solution.py:539
  435.1 8.8 %copy-start.32 = (f32[32,512]{1,0:T(8,128)S(1)}, f32[32,512]{1,0:T(8,128)}, u32[]{:S(2)}) copy-start(f32[32,512]{1,0:T(8,128)} %get-tuple-element.186) | copy-start | bytes 196612
  435.1 10.7 %copy-start.34 = (f32[32,32]{1,0:T(8,128)S(1)}, f32[32,32]{1,0:T(8,128)}, u32[]{:S(2)}) copy-start(f32[32,32]{1,0:T(8,128)} %reshape_squeeze.25) | copy-start | bytes 12292
  435.1 10.7 %copy-start.35 = (f32[32,32]{1,0:T(8,128)S(1)}, f32[32,32]{1,0:T(8,128)}, u32[]{:S(2)}) copy-start(f32[32,32]{1,0:T(8,128)} %reshape_squeeze.26) | copy-start | bytes 12292
  435.1 10.7 %copy-start.36 = (f32[32,32]{1,0:T(8,128)S(1)}, f32[32,32]{1,0:T(8,128)}, u32[]{:S(2)}) copy-start(f32[32,32]{1,0:T(8,128)} %reshape_squeeze.27) | copy-start | bytes 12292
  446.6 16.2 %all-to-all-start.4 = ((f32[32,1,448]{2,1,0:T(1,128)}), f32[32,1,448]{2,1,0:T(1,128)S(1)}, u32[]{:S(2)}, u32[]{:S(2)}) async-start(f32[32,1,448]{2,1,0:T(1,128)} %all_to_all.25), calls=%async_computation.4 | async-start | bytes 131072 | tf_op jit(solution)/shard_map/all_to_all | solution.py:961
  462.9 11.7 %all-to-all-start.5 = ((f32[8,32,384]{2,1,0:T(8,128)}), f32[8,32,384]{2,1,0:T(8,128)S(1)}, u32[]{:S(2)}, u32[]{:S(2)}) async-start(f32[8,32,384]{2,1,0:T(8,128)} %fusion.12), calls=%async_computation.5 | async-start | bytes 786432 | tf_op jit(solution)/shard_map/all_to_all | solution.py:436
  (31 other events, 79.1 us)
Sparse Core Ops, SparseCore 0:
  10.9 158.8 all-gather.2
  173.3 68.8 all-gather.4
